TPU v7x, 32 devices: a whole 2x2x4 slice. The times are simulated.
32 devices in a mesh: section: 2 (over y), dp: 4 (over z), expert: 4 (over x, core).
Axes of the slice: x: 2, y: 2, z: 4, core: 2. Of those that a mesh axis runs over, the one named last changes fastest.
Arguments:
- inputs: bfloat16 [2, 2, 4, 1024, 512], P('section', None, 'dp', 'expert'), may hold values from -6 to 6
- cotangents: bfloat16 [2, 2, 4, 1024, 512], P('section', None, 'dp', 'expert'), may hold values from -6 to 6
- pair_ids: int32 [2, 2, 4, 1024], P(None, None, 'dp'), may hold values from 0 to 15, never falling along the last dimension, each value on 1 to 512 neighbouring positions
- self_routes: int32 [2, 2, 4, 1024, 2], P('section', None, 'dp'), may hold values from 0 to 3, all different within a row; in each aligned block of 1024 rows (0 to 1023, 1024 to 2047, ..., all dimensions but the last counted through in order) at most 640 rows name the same one
- cross_routes: int32 [2, 4, 1024, 2], P(None, 'dp'), may hold values from 0 to 3, all different within a row; in each aligned block of 1024 rows (0 to 1023, 1024 to 2047, ..., all dimensions but the last counted through in order) at most 640 rows name the same one
- norm_gain: float32 [2, 2, 512], P('section'), may hold values from 0.5 to 1.5
- norm_bias: float32 [2, 2, 512], P('section'), may hold values from -2 to 2
- w_kv: bfloat16 [2, 512, 128], P('section'), may hold values from -0.25 to 0.25
- w_router: bfloat16 [2, 512, 4], P('section'), may hold values from -0.1875 to 0.1875
- w_query: bfloat16 [2, 4, 512, 64], P('section', 'expert'), may hold values from -0.25 to 0.25
- w_out: bfloat16 [2, 4, 64, 512], P('section', 'expert'), may hold values from -3 to 3
- w_in: bfloat16 [2, 512, 2048], P('section', None, 'expert'), may hold values from -0.25 to 0.25
- w_back: bfloat16 [2, 2048, 512], P('section', 'expert'), may hold values from -0.125 to 0.125
- cross_gain: float32 [512], replicated, may hold values from 0.5 to 1.5
- cross_bias: float32 [512], replicated, may hold values from -2 to 2
- cross_kv: bfloat16 [512, 128], replicated, may hold values from -0.25 to 0.25
- cross_router: bfloat16 [512, 4], replicated, may hold values from -0.1875 to 0.1875
- cross_query: bfloat16 [4, 512, 64], P('expert'), may hold values from -0.25 to 0.25
- cross_out: bfloat16 [4, 64, 512], P('expert'), may hold values from -3 to 3
Outputs:
- layer_outputs: bfloat16 [2, 2, 4, 1024, 512], P('section', None, 'dp', 'expert')
- input_grads: float32 [2, 2, 4, 1024, 512], P('section', None, 'dp', 'expert')
- grad_norm_gain: float32 [2, 2, 512], P('section', None, ('dp', 'expert'))
- grad_norm_bias: float32 [2, 2, 512], P('section', None, ('dp', 'expert'))
- grad_w_kv: float32 [2, 512, 128], P('section', ('dp', 'expert'))
- grad_w_router: float32 [2, 512, 4], P('section', ('dp', 'expert'))
- grad_w_query: float32 [2, 4, 512, 64], P('section', 'expert', 'dp')
- grad_w_out: float32 [2, 4, 64, 512], P('section', 'expert', None, 'dp')
- grad_w_in: float32 [2, 512, 2048], P('section', 'dp', 'expert')
- grad_w_back: float32 [2, 2048, 512], P('section', 'expert', 'dp')
- grad_cross_gain: float32 [512], P(('dp', 'expert'))
- grad_cross_bias: float32 [512], P(('dp', 'expert'))
- grad_cross_kv: float32 [512, 128], P(('dp', 'expert'))
- grad_cross_router: float32 [512, 4], P(('dp', 'expert'))
- grad_cross_query: float32 [4, 512, 64], P('expert', 'dp')
- grad_cross_out: float32 [4, 64, 512], P('expert', None, 'dp')
Inputs may be any that keep to these rules, and one draw needn't show every extreme that they name: `pair_ids`: in each packed row the ids run from 0 to 15 in order, each as one run of positions, every id present; source and target rows with the same indices hold the same pairs. `self_routes`: each token names 2 different experts; in each packed row no expert is named by more than 640 tokens. `cross_routes`: each token names 2 different experts; in each packed row no expert is named by more than 640 tokens.
All inputs are finite; a program needn't handle non-finite values.
Results may differ from a plain program's by a relative error of at most 0.025.
Values may be sent and summed in bfloat16 or wider, within the bound.
A program may use at most 192 MiB of HBM per device.

v0:
```python
import jax
import jax.numpy as jnp
from jax import lax
from jax.sharding import PartitionSpec as P


def passed_along(x, axis, by):
    size = lax.axis_size(axis)
    pairs = [(i, i + by) for i in range(size) if 0 <= i + by < size]
    return lax.ppermute(x, axis, pairs)


def norm_rows(stream, gain_vec, shift_vec):
    middle = jnp.mean(stream, -1, keepdims=True)
    centred = stream - middle
    spread = jnp.mean(centred * centred, -1, keepdims=True)
    return centred * lax.rsqrt(spread + 1e-05) * gain_vec + shift_vec


def gelu_tanh(stream):
    return jax.nn.gelu(stream, approximate=True)


def local_rows(full, row_span):
    return lax.dynamic_slice_in_dim(full, lax.axis_index("expert") * row_span, row_span, 1)


def route_gates(normed, w_router, routes):
    logits = jnp.einsum("rld,de->rle", normed, w_router, preferred_element_type=jnp.float32)
    picked = (
        routes[..., None] == lax.broadcasted_iota(jnp.int32, routes.shape + (w_router.shape[1],), 3)
    ).astype(jnp.float32)
    chosen = jnp.sum(picked * logits[:, :, None, :], -1)
    return (picked, jax.nn.softmax(chosen, -1))


def route_backward(normed, w_router, routes, grad_grid):
    picked, gate_vals = route_gates(normed, w_router, routes)
    grad_gates = jnp.sum(picked * grad_grid[:, :, None, :], -1)
    grad_chosen = gate_vals * (grad_gates - jnp.sum(gate_vals * grad_gates, -1, keepdims=True))
    grad_logits = jnp.sum(picked * grad_chosen[..., None], 2).astype(jnp.bfloat16)
    grad_router = jnp.einsum("rld,rle->de", normed, grad_logits, preferred_element_type=jnp.float32)
    grad_normed = jnp.einsum(
        "rle,de->rld", grad_logits, w_router, preferred_element_type=jnp.float32
    )
    return (grad_normed, grad_router)


def pair_mask(query_pairs, query_pos, key_pairs, causal):
    same_pair = query_pairs[:, :, None] == key_pairs[:, None, :]
    key_pos = lax.broadcasted_iota(jnp.int32, same_pair.shape, 2)
    return same_pair & (jnp.logical_not(causal) | (key_pos <= query_pos[:, :, None]))


def finish_heads(grad_normed, grad_kv, grad_grid, normed, source, routes_local, w_kv, w_router):
    grad_kv_low = grad_kv.astype(jnp.bfloat16)
    grad_kv_weight = jnp.einsum(
        "rld,rlk->dk", source, grad_kv_low, preferred_element_type=jnp.float32
    )
    grad_source = jnp.einsum("rlk,dk->rld", grad_kv_low, w_kv, preferred_element_type=jnp.float32)
    grad_routed, grad_router = route_backward(normed, w_router, routes_local, grad_grid)
    return (grad_normed + grad_routed, grad_source, grad_kv_weight, grad_router)


def pair_order(routes_local, experts):
    row_count, row_span, top_count = routes_local.shape
    flat_total = row_count * row_span * top_count
    route_flat = routes_local.reshape(flat_total)
    pair_index = lax.broadcasted_iota(jnp.int32, (flat_total,), 0)
    order = jnp.argsort(route_flat * flat_total + pair_index)
    group_sizes = jnp.sum(
        (route_flat[:, None] == lax.broadcasted_iota(jnp.int32, (flat_total, experts), 1)).astype(
            jnp.int32
        ),
        0,
    )
    token_sorted = order // top_count
    return (order, group_sizes, token_sorted)


def unsort_rows(sorted_rows, order):
    return jnp.zeros_like(sorted_rows).at[order].set(sorted_rows)


def grouped_outer(left_rows, right_rows, group_sizes):
    numbers = lax.RaggedDotDimensionNumbers(
        dot_dimension_numbers=(((0,), (0,)), ((), ())),
        lhs_ragged_dimensions=[0],
        rhs_group_dimensions=[],
    )
    return lax.ragged_dot_general(
        left_rows, right_rows, group_sizes, numbers, preferred_element_type=jnp.float32
    )


def token_forward(normed, source, routes_local, own_local, key_pairs, causal, weights):
    w_kv, w_router, query_all, out_all = weights
    kv_local = jnp.einsum("rld,dk->rlk", source, w_kv, preferred_element_type=jnp.float32).astype(
        jnp.bfloat16
    )
    kv_all = lax.all_gather(kv_local, "expert", axis=1, tiled=True)
    experts, model_dim, head_dim = query_all.shape
    score_scale = head_dim ** (-0.5)
    key_rows = kv_all[..., :head_dim]
    value_rows = kv_all[..., head_dim:]
    row_count, row_span, top_count = routes_local.shape
    flat_count = row_span * top_count
    flat_total = row_count * flat_count
    picked, gate_vals = route_gates(normed, w_router, routes_local)
    order, group_sizes, token_sorted = pair_order(routes_local, experts)
    gathered = normed.reshape(row_count * row_span, model_dim)[token_sorted]
    queries_sorted = lax.ragged_dot(
        gathered, query_all, group_sizes, preferred_element_type=jnp.float32
    ).astype(jnp.bfloat16)
    queries = unsort_rows(queries_sorted, order).reshape(row_count, flat_count, head_dim)
    positions = lax.axis_index("expert") * row_span + lax.broadcasted_iota(
        jnp.int32, (row_count, row_span, top_count), 1
    )
    query_pairs = jnp.broadcast_to(own_local[:, :, None], (row_count, row_span, top_count)).reshape(
        row_count, flat_count
    )
    raw_scores = (
        jnp.einsum("rch,rlh->rcl", queries, key_rows, preferred_element_type=jnp.float32)
        * score_scale
    )
    allowed = pair_mask(query_pairs, positions.reshape(row_count, flat_count), key_pairs, causal)
    attn_probs = jax.nn.softmax(jnp.where(allowed, raw_scores, -1e30), -1)
    probs_low = attn_probs.astype(jnp.bfloat16)
    head_out = jnp.einsum(
        "rcl,rlh->rch", probs_low, value_rows, preferred_element_type=jnp.float32
    ).astype(jnp.bfloat16)
    head_sorted = head_out.reshape(flat_total, head_dim)[order]
    result_sorted = lax.ragged_dot(
        head_sorted, out_all, group_sizes, preferred_element_type=jnp.float32
    )
    result = unsort_rows(result_sorted, order).reshape(row_count, row_span, top_count, model_dim)
    output = jnp.sum(result * gate_vals[..., None], 2)
    picked_flat = picked.reshape(row_count, flat_count, experts)
    return (
        output,
        (
            key_rows,
            value_rows,
            picked_flat,
            gate_vals,
            queries,
            attn_probs,
            probs_low,
            head_sorted,
            result,
            order,
            group_sizes,
            token_sorted,
            gathered,
        ),
    )


def token_backward(grad_local, normed, source, routes_local, weights, cache):
    w_kv, w_router, query_all, out_all = weights
    (
        key_rows,
        value_rows,
        picked_flat,
        gate_vals,
        queries,
        attn_probs,
        probs_low,
        head_sorted,
        result,
        order,
        group_sizes,
        token_sorted,
        gathered,
    ) = cache
    experts, model_dim, head_dim = query_all.shape
    score_scale = head_dim ** (-0.5)
    row_count, row_span, top_count = routes_local.shape
    flat_count = row_span * top_count
    flat_total = row_count * flat_count
    upstream = jnp.broadcast_to(
        grad_local[:, :, None, :], (row_count, row_span, top_count, model_dim)
    )
    grad_result = (
        (upstream * gate_vals[..., None]).reshape(flat_total, model_dim).astype(jnp.bfloat16)
    )
    grad_gates = jnp.sum(upstream * result, -1)
    result_grad_sorted = grad_result[order]
    grad_out_all = grouped_outer(head_sorted, result_grad_sorted, group_sizes)
    head_grad_sorted = lax.ragged_dot(
        result_grad_sorted,
        out_all.transpose(0, 2, 1),
        group_sizes,
        preferred_element_type=jnp.float32,
    ).astype(jnp.bfloat16)
    grad_head = unsort_rows(head_grad_sorted, order).reshape(row_count, flat_count, head_dim)
    grad_probs = jnp.einsum(
        "rch,rlh->rcl", grad_head, value_rows, preferred_element_type=jnp.float32
    )
    grad_values = jnp.einsum(
        "rcl,rch->rlh", probs_low, grad_head, preferred_element_type=jnp.float32
    )
    grad_scores = (
        attn_probs * (grad_probs - jnp.sum(grad_probs * attn_probs, -1, keepdims=True))
    ).astype(jnp.bfloat16)
    grad_queries = (
        jnp.einsum("rcl,rlh->rch", grad_scores, key_rows, preferred_element_type=jnp.float32)
        * score_scale
    ).astype(jnp.bfloat16)
    grad_keys = (
        jnp.einsum("rcl,rch->rlh", grad_scores, queries, preferred_element_type=jnp.float32)
        * score_scale
    )
    query_grad_sorted = grad_queries.reshape(flat_total, head_dim)[order]
    grad_query_all = grouped_outer(gathered, query_grad_sorted, group_sizes)
    grad_gathered = lax.ragged_dot(
        query_grad_sorted,
        query_all.transpose(0, 2, 1),
        group_sizes,
        preferred_element_type=jnp.float32,
    )
    grad_normed = (
        jnp.zeros((row_count * row_span, model_dim), jnp.float32)
        .at[token_sorted]
        .add(grad_gathered)
        .reshape(row_count, row_span, model_dim)
    )
    grad_kv = lax.psum_scatter(
        jnp.concatenate([grad_keys, grad_values], -1).astype(jnp.bfloat16),
        "expert",
        scatter_dimension=1,
        tiled=True,
    ).astype(jnp.float32)
    grad_grid = jnp.sum(
        picked_flat.reshape(row_count, row_span, top_count, experts) * grad_gates[..., None], 2
    )
    grad_normed, grad_source, grad_kv_weight, grad_router = finish_heads(
        grad_normed, grad_kv, grad_grid, normed, source, routes_local, w_kv, w_router
    )
    return (grad_normed, grad_source, (grad_kv_weight, grad_router, grad_query_all, grad_out_all))


def heads_pass(normed, source, routes, own_pairs, key_pairs, causal, weights):
    row_span = normed.shape[1]
    return token_forward(
        normed,
        source,
        local_rows(routes, row_span),
        local_rows(own_pairs, row_span),
        key_pairs,
        causal,
        weights,
    )


def heads_back(grad_local, normed, source, routes, weights, cache):
    routes_local = local_rows(routes, normed.shape[1])
    return token_backward(grad_local, normed, source, routes_local, weights, cache)


def query_blocks(full, dp_size, ex_size):
    experts, model_dim, head_dim = full.shape
    per_device = experts // ex_size
    shaped = full.reshape(ex_size, per_device, dp_size, model_dim // dp_size, head_dim)
    return shaped.transpose(2, 0, 1, 3, 4).reshape(
        dp_size * ex_size, per_device, model_dim // dp_size, head_dim
    )


def out_blocks(full, dp_size, ex_size):
    experts, head_dim, model_dim = full.shape
    per_device = experts // ex_size
    shaped = full.reshape(ex_size, per_device, head_dim, dp_size, model_dim // dp_size)
    return shaped.transpose(3, 0, 1, 2, 4).reshape(
        dp_size * ex_size, per_device, head_dim, model_dim // dp_size
    )


def body(
    inputs,
    cotangents,
    pair_ids,
    self_routes,
    cross_routes,
    norm_gain,
    norm_bias,
    w_kv,
    w_router,
    w_query,
    w_out,
    w_in,
    w_back,
    cross_gain,
    cross_bias,
    cross_kv,
    cross_router,
    cross_query,
    cross_out,
):
    micro_count = inputs.shape[1]
    section_id = lax.axis_index("section")
    causal = section_id == 1
    w_in_full, w_back_full, query_all, out_all, cross_query_all, cross_out_all = (
        lax.all_gather(w_in[0], "expert", axis=1, tiled=True),
        lax.all_gather(w_back[0], "expert", axis=0, tiled=True),
        lax.all_gather(w_query[0], "expert", axis=0, tiled=True),
        lax.all_gather(w_out[0], "expert", axis=0, tiled=True),
        lax.all_gather(cross_query, "expert", axis=0, tiled=True),
        lax.all_gather(cross_out, "expert", axis=0, tiled=True),
    )
    self_heads = (w_kv[0], w_router[0], query_all, out_all)
    cross_heads = (cross_kv, cross_router, cross_query_all, cross_out_all)
    norm_gains = (norm_gain[0, 0], cross_gain, norm_gain[0, 1])
    shifts = (norm_bias[0, 0], cross_bias, norm_bias[0, 1])
    own_all = lax.dynamic_index_in_dim(pair_ids, section_id, 0, False)
    source_all = pair_ids[0]

    def micro_piece(micro_slot):
        routes = lax.dynamic_index_in_dim(self_routes[0], micro_slot, 0, False)
        routes_cross = lax.dynamic_index_in_dim(cross_routes, micro_slot, 0, False)
        own_pairs = lax.dynamic_index_in_dim(own_all, micro_slot, 0, False)
        source_pairs = lax.dynamic_index_in_dim(source_all, micro_slot, 0, False)
        return (routes, routes_cross, own_pairs, source_pairs)

    def layer_forward(stream, memory, routes, routes_cross, own_pairs, source_pairs):
        normed0 = norm_rows(stream, norm_gains[0], shifts[0]).astype(jnp.bfloat16)
        attend, cache0 = heads_pass(
            normed0, normed0, routes, own_pairs, own_pairs, causal, self_heads
        )
        after_self = stream + attend
        normed1 = norm_rows(after_self, norm_gains[1], shifts[1]).astype(jnp.bfloat16)
        cross_part, cache1 = heads_pass(
            normed1, memory, routes_cross, own_pairs, source_pairs, False, cross_heads
        )
        after_cross = after_self + cross_part
        normed2 = norm_rows(after_cross, norm_gains[2], shifts[2]).astype(jnp.bfloat16)
        hidden = jnp.einsum("rld,df->rlf", normed2, w_in_full, preferred_element_type=jnp.float32)
        active = gelu_tanh(hidden).astype(jnp.bfloat16)
        result = after_cross + jnp.einsum(
            "rlf,fd->rld", active, w_back_full, preferred_element_type=jnp.float32
        )
        saved_acts = (
            stream,
            after_self,
            after_cross,
            normed0,
            normed1,
            normed2,
            cache0,
            cache1,
            hidden,
            active,
        )
        return (result, saved_acts)

    outputs = jnp.zeros(inputs.shape[1:], jnp.bfloat16)
    memories = jnp.zeros(inputs.shape[1:], jnp.bfloat16)
    previous = jnp.zeros(inputs.shape[2:], jnp.bfloat16)
    for tick_num in range(micro_count + 1):
        memory = passed_along(previous, "section", 1)
        micro_idx = tick_num - section_id
        in_range = (micro_idx >= 0) & (micro_idx < micro_count)
        micro_slot = jnp.clip(micro_idx, 0, micro_count - 1)
        routes, routes_cross, own_pairs, source_pairs = micro_piece(micro_slot)
        stream = lax.dynamic_index_in_dim(inputs[0], micro_slot, 0, False).astype(jnp.float32)
        result, unused_acts = layer_forward(
            stream, memory, routes, routes_cross, own_pairs, source_pairs
        )
        lowered = result.astype(jnp.bfloat16)
        outputs = outputs.at[micro_slot].set(jnp.where(in_range, lowered, outputs[micro_slot]))
        memories = memories.at[micro_slot].set(jnp.where(in_range, memory, memories[micro_slot]))
        previous = lowered
    input_grads = jnp.zeros(inputs.shape[1:], jnp.float32)
    sending = jnp.zeros(inputs.shape[2:], jnp.bfloat16)
    totals = None
    for tick_num in range(micro_count + 1):
        incoming = passed_along(sending, "section", -1)
        micro_idx = micro_count - tick_num - section_id
        in_range = (micro_idx >= 0) & (micro_idx < micro_count)
        micro_slot = jnp.clip(micro_idx, 0, micro_count - 1)
        routes, routes_cross, own_pairs, source_pairs = micro_piece(micro_slot)
        stream = lax.dynamic_index_in_dim(inputs[0], micro_slot, 0, False).astype(jnp.float32)
        grad_out = lax.dynamic_index_in_dim(cotangents[0], micro_slot, 0, False).astype(
            jnp.float32
        ) + incoming.astype(jnp.float32)
        memory = memories[micro_slot]
        unused_result, saved_acts = layer_forward(
            stream, memory, routes, routes_cross, own_pairs, source_pairs
        )
        (
            layer_stream,
            layer_after_self,
            layer_after_cross,
            layer_normed0,
            layer_normed1,
            layer_normed2,
            layer_cache0,
            layer_cache1,
            layer_hidden,
            layer_active,
        ) = saved_acts
        grad_low = grad_out.astype(jnp.bfloat16)
        grad_back = jnp.einsum(
            "rlf,rld->fd", layer_active, grad_low, preferred_element_type=jnp.float32
        )
        grad_active = jnp.einsum(
            "rld,fd->rlf", grad_low, w_back_full, preferred_element_type=jnp.float32
        )
        grad_hidden = jax.vjp(gelu_tanh, layer_hidden)[1](grad_active)[0].astype(jnp.bfloat16)
        grad_in = jnp.einsum(
            "rld,rlf->df", layer_normed2, grad_hidden, preferred_element_type=jnp.float32
        )
        grad_normed2 = jnp.einsum(
            "rlf,df->rld", grad_hidden, w_in_full, preferred_element_type=jnp.float32
        )
        grad_x2, gain_two, shift_two = jax.vjp(
            norm_rows, layer_after_cross, norm_gains[2], shifts[2]
        )[1](grad_normed2)
        grad_after_cross = grad_out + grad_x2
        grad_normed1, grad_memory, cross_grads = heads_back(
            grad_after_cross, layer_normed1, memory, routes_cross, cross_heads, layer_cache1
        )
        grad_x1, gain_one, shift_one = jax.vjp(
            norm_rows, layer_after_self, norm_gains[1], shifts[1]
        )[1](grad_normed1)
        grad_after_self = grad_after_cross + grad_x1
        grad_normed0, grad_source0, self_grads = heads_back(
            grad_after_self, layer_normed0, layer_normed0, routes, self_heads, layer_cache0
        )
        grad_x0, gain_zero, shift_zero = jax.vjp(norm_rows, layer_stream, norm_gains[0], shifts[0])[
            1
        ](grad_normed0 + grad_source0)
        grad_stream = grad_after_self + grad_x0
        gain_rows = jnp.stack([gain_zero, gain_one, gain_two])
        shift_rows = jnp.stack([shift_zero, shift_one, shift_two])
        grad_stream, grad_memory, weight_grads = (
            grad_stream,
            grad_memory,
            (gain_rows, shift_rows, grad_in, grad_back) + self_grads + cross_grads,
        )
        factor = in_range.astype(jnp.float32)
        weight_grads = jax.tree.map(lambda grad_val: grad_val * factor, weight_grads)
        if totals is None:
            totals = weight_grads
        else:
            totals = jax.tree.map(
                lambda first_val, second_val: first_val + second_val, totals, weight_grads
            )
        input_grads = input_grads.at[micro_slot].set(
            jnp.where(in_range, grad_stream, input_grads[micro_slot])
        )
        sending = (grad_memory * factor).astype(jnp.bfloat16)
    (
        gain_sum,
        shift_sum,
        in_sum,
        back_sum,
        kv_sum,
        router_sum,
        query_sum,
        out_sum,
        ckv_sum,
        crouter_sum,
        cquery_sum,
        cout_sum,
    ) = totals
    dp_size = lax.axis_size("dp")
    ex_size = lax.axis_size("expert")
    model_dim, hidden_dim = in_sum.shape
    in_blocks = (
        in_sum.reshape(dp_size, model_dim // dp_size, ex_size, hidden_dim // ex_size)
        .transpose(0, 2, 1, 3)
        .reshape(dp_size * ex_size, model_dim // dp_size, hidden_dim // ex_size)
    )
    back_blocks = (
        back_sum.reshape(ex_size, hidden_dim // ex_size, dp_size, model_dim // dp_size)
        .transpose(2, 0, 1, 3)
        .reshape(dp_size * ex_size, hidden_dim // ex_size, model_dim // dp_size)
    )
    (
        gain_part,
        shift_part,
        kv_part,
        router_part,
        ckv_part,
        crouter_part,
        in_part,
        back_part,
        query_part,
        out_part,
        cquery_part,
        cout_part,
    ) = (
        lax.psum_scatter(gain_sum, ("dp", "expert"), scatter_dimension=1, tiled=True),
        lax.psum_scatter(shift_sum, ("dp", "expert"), scatter_dimension=1, tiled=True),
        lax.psum_scatter(kv_sum, ("dp", "expert"), scatter_dimension=0, tiled=True),
        lax.psum_scatter(router_sum, ("dp", "expert"), scatter_dimension=0, tiled=True),
        lax.psum_scatter(ckv_sum, ("dp", "expert"), scatter_dimension=0, tiled=True),
        lax.psum_scatter(crouter_sum, ("dp", "expert"), scatter_dimension=0, tiled=True),
        lax.psum_scatter(in_blocks, ("dp", "expert"), scatter_dimension=0, tiled=True),
        lax.psum_scatter(back_blocks, ("dp", "expert"), scatter_dimension=0, tiled=True),
        lax.psum_scatter(
            query_blocks(query_sum, dp_size, ex_size),
            ("dp", "expert"),
            scatter_dimension=0,
            tiled=True,
        ),
        lax.psum_scatter(
            out_blocks(out_sum, dp_size, ex_size), ("dp", "expert"), scatter_dimension=0, tiled=True
        ),
        lax.psum_scatter(
            query_blocks(cquery_sum, dp_size, ex_size),
            ("dp", "expert"),
            scatter_dimension=0,
            tiled=True,
        ),
        lax.psum_scatter(
            out_blocks(cout_sum, dp_size, ex_size),
            ("dp", "expert"),
            scatter_dimension=0,
            tiled=True,
        ),
    )
    query_part = query_part[0]
    out_part = out_part[0]
    cquery_part = cquery_part[0]
    cout_part = cout_part[0]
    (
        cross_gain_part,
        cross_shift_part,
        cross_kv_part,
        cross_router_part,
        cross_query_part,
        cross_out_part,
    ) = lax.psum(
        (gain_part[1], shift_part[1], ckv_part, crouter_part, cquery_part, cout_part), "section"
    )
    norm_gain_part = jnp.stack([gain_part[0], gain_part[2]])[None]
    norm_shift_part = jnp.stack([shift_part[0], shift_part[2]])[None]
    return (
        outputs[None],
        input_grads[None],
        norm_gain_part,
        norm_shift_part,
        kv_part[None],
        router_part[None],
        query_part[None],
        out_part[None],
        in_part[0][None],
        back_part[0][None],
        cross_gain_part,
        cross_shift_part,
        cross_kv_part,
        cross_router_part,
        cross_query_part,
        cross_out_part,
    )


def solution(mesh):
    placed = (
        P("section", None, "dp", "expert", None),
        P("section", None, "dp", "expert", None),
        P(None, None, "dp", None),
        P("section", None, "dp", None, None),
        P(None, "dp", None, None),
        P("section", None, None),
        P("section", None, None),
        P("section", None, None),
        P("section", None, None),
        P("section", "expert", None, None),
        P("section", "expert", None, None),
        P("section", None, "expert"),
        P("section", "expert", None),
        P(),
        P(),
        P(),
        P(),
        P("expert", None, None),
        P("expert", None, None),
    )
    return jax.shard_map(
        body,
        mesh=mesh,
        in_specs=placed,
        out_specs=(
            P("section", None, "dp", "expert", None),
            P("section", None, "dp", "expert", None),
            P("section", None, ("dp", "expert")),
            P("section", None, ("dp", "expert")),
            P("section", ("dp", "expert"), None),
            P("section", ("dp", "expert"), None),
            P("section", "expert", "dp", None),
            P("section", "expert", None, "dp"),
            P("section", "dp", "expert"),
            P("section", "expert", "dp"),
            P(("dp", "expert")),
            P(("dp", "expert")),
            P(("dp", "expert"), None),
            P(("dp", "expert"), None),
            P("expert", "dp", None),
            P("expert", None, "dp"),
        ),
        check_vma=False,
    )
```

profile of v0, /device:TPU:0, one launch (start us, length us, event | category | flops | bytes accessed | tf_op | source)
XLA Modules:
  0.0 1622.6 jit_solution(503953258766283894)
XLA Ops:
  40.5 5.9 all-gather.6
  49.5 6.3 ragged-dot-none.34
  62.4 6.9 all-gather.2
  71.2 6.1 ragged-dot-none.33
  94.9 5.9 all-gather.1
  103.7 6.0 ragged-dot-none.38
  154.9 6.1 all_gather.51
  162.3 6.1 all_gather.53
  194.1 6.3 ragged-dot-none.36
  202.5 6.1 ragged-dot-none.32
  213.9 6.0 all-gather.3
  223.8 6.2 ragged-dot-none.35
  246.9 6.3 collective-permute-start.1
  270.1 6.4 ragged-dot-none.31
  320.2 6.0 ragged-dot-none.21
  336.7 5.9 all-gather.12
  348.5 6.2 ragged-dot-none.16
  378.0 6.3 ragged-dot-none.30
  393.2 6.0 ragged-dot-none.29
  411.1 5.9 all-gather.9
  417.0 6.1 ragged-dot-none.28
  430.3 6.0 ragged-dot-none.27
  443.9 6.1 all-gather.10
  456.9 6.0 ragged-dot-none.26
  493.4 6.1 ragged-dot-none.25
  516.2 17.0 %reduce-scatter.29.cloned.1.call-done = bf16[1,256,128]{1,2,0:T(8,128)(2,1)} async-done(((bf16[1,1024,128]{1,2,0:T(8,128)(2,1)}), bf16[1,256,128]{1,2,0:T(8,128)(2,1)}) %reduce-scatter.29.cloned.1.call-update) | async-done | bytes 65552 | tf_op jit(solution)/shard_map/reduce_scatter | solution.py:228
  543.2 6.0 ragged-dot-none.24
  553.6 6.3 ragged-dot-none.2
  578.0 6.1 ragged-dot-none.20
  599.1 15.8 reduce-scatter.33.cloned.1.call-done
  620.5 6.0 ragged-dot-none.19
  631.2 5.9 ragged-dot-none.1
  654.4 6.2 ragged-dot-none.15
  672.3 6.1 ragged-dot-none.14
  697.1 6.2 ragged-dot-none.18
  718.1 6.0 ragged-dot-none.13
  739.2 6.1 ragged-dot-none.23
  789.0 6.1 ragged-dot-none.17
  795.1 5.8 ragged-dot-none.12
  800.9 6.2 ragged-dot-none.22
  808.5 5.9 ragged-dot-none
  847.1 6.3 ragged-dot-none.5
  853.3 6.3 ragged-dot-none.4
  859.7 6.2 ragged-dot-none.3
  880.3 5.9 ragged-dot-none.8
  886.3 6.1 ragged-dot-none.6
  892.3 6.0 ragged-dot-none.7
  907.2 6.3 ragged-dot-none.11
  913.5 6.3 ragged-dot-none.9
  919.9 6.3 ragged-dot-none.10
  941.7 21.5 %reduce-scatter.57.cloned.1.call-done = f32[32,3]{1,0:T(8,128)} async-done(((f32[512,3]{1,0:T(8,128)}), f32[32,3]{1,0:T(8,128)}) %reduce-scatter.57.cloned.1.call-update) | async-done | bytes 400
  964.7 57.0 %reduce-scatter.55.cloned.1.call-done = f32[32,3]{1,0:T(8,128)} async-done(((f32[512,3]{1,0:T(8,128)}), f32[32,3]{1,0:T(8,128)}) %reduce-scatter.55.cloned.1.call-update) | async-done | bytes 400
  1023.1 56.7 %reduce-scatter.53.cloned.1.call-done = f32[1,1,64,128]{3,2,1,0:T(8,128)} async-done(((f32[16,1,64,128]{3,2,1,0:T(8,128)}), f32[1,1,64,128]{3,2,1,0:T(8,128)}) %reduce-scatter.53.cloned.1.call-update) | async-done | bytes 32784 | tf_op jit(solution)/shard_map/reduce_scatter | solution.py:517
  1079.9 58.8 %reduce-scatter.51.cloned.1.call-done = f32[1,1,128,64]{2,3,1,0:T(8,128)} async-done(((f32[16,1,128,64]{2,3,1,0:T(8,128)}), f32[1,1,128,64]{2,3,1,0:T(8,128)}) %reduce-scatter.51.cloned.1.call-update) | async-done | bytes 32784 | tf_op jit(solution)/shard_map/reduce_scatter | solution.py:511
  1138.7 57.7 %reduce-scatter.49.cloned.1.call-done = f32[32,128]{1,0:T(8,128)} async-done(((f32[512,128]{1,0:T(8,128)}), f32[32,128]{1,0:T(8,128)}) %reduce-scatter.49.cloned.1.call-update) | async-done | bytes 16400 | tf_op jit(solution)/shard_map/reduce_scatter | solution.py:498
  1196.5 7.7 multiply_add_fusion
  1221.9 6.0 reshape.5456
  1240.9 13.2 reduce-scatter.59.cloned.1.call-done
  1260.7 52.3 %reduce-scatter.41.cloned.1.call-done = f32[1,1,64,128]{3,2,1,0:T(8,128)} async-done(((f32[16,1,64,128]{3,2,1,0:T(8,128)}), f32[1,1,64,128]{3,2,1,0:T(8,128)}) %reduce-scatter.41.cloned.1.call-update) | async-done | bytes 32784 | tf_op jit(solution)/shard_map/reduce_scatter | solution.py:508
  1313.0 59.2 %reduce-scatter.39.cloned.1.call-done = f32[1,1,128,64]{2,3,1,0:T(8,128)} async-done(((f32[16,1,128,64]{2,3,1,0:T(8,128)}), f32[1,1,128,64]{2,3,1,0:T(8,128)}) %reduce-scatter.39.cloned.1.call-update) | async-done | bytes 32784 | tf_op jit(solution)/shard_map/reduce_scatter | solution.py:502
  1372.2 58.3 %reduce-scatter.37.cloned.1.call-done = f32[32,128]{1,0:T(8,128)} async-done(((f32[512,128]{1,0:T(8,128)}), f32[32,128]{1,0:T(8,128)}) %reduce-scatter.37.cloned.1.call-update) | async-done | bytes 16400 | tf_op jit(solution)/shard_map/reduce_scatter | solution.py:496
  1430.5 23.3 %all-reduce.3.cloned.1.call-done = (f32[32]{0:T(128)}, f32[32]{0:T(128)}, f32[32,128]{1,0:T(8,128)}, f32[32,4]{0,1:T(4,128)}, f32[1,128,64]{1,2,0:T(8,128)}, /*index=5*/f32[1,64,128]{2,1,0:T(8,128)}) async-done(((f32[32]{0:T(128)}, f32[32]{0:T(128)}, f32[32,128]{1,0:T(8,128)}, f32[32,4]{0,1:T(4,128)}, f32[1,128,64]{1,2,0:T(8,128)}, /*index=5*/f32[1,64,128]{2,1,0:T(8,128)}), (f32[32]{0:T(128)}, f32[32]{0:T(128)}, ...) | async-done | bytes 82704 | tf_op jit(solution)/shard_map/psum | solution.py:535
  1453.8 77.6 %reduce-scatter.45.cloned.1.call-done = f32[1,512,128]{2,1,0:T(8,128)} async-done(((f32[16,512,128]{2,1,0:T(8,128)}), f32[1,512,128]{2,1,0:T(8,128)}) %reduce-scatter.45.cloned.1.call-update) | async-done | bytes 262160 | tf_op jit(solution)/shard_map/reduce_scatter | solution.py:501
  1531.4 76.3 %reduce-scatter.43.cloned.1.call-done = f32[1,128,512]{2,1,0:T(8,128)} async-done(((f32[16,128,512]{2,1,0:T(8,128)}), f32[1,128,512]{2,1,0:T(8,128)}) %reduce-scatter.43.cloned.1.call-update) | async-done | bytes 262160 | tf_op jit(solution)/shard_map/reduce_scatter | solution.py:500
  (1366 shorter events, 650.3 us)
Async XLA Ops:
  7.2 33.1 %copy-start = (bf16[1,512,128]{2,1,0:T(8,128)(2,1)S(1)}, bf16[1,512,128]{2,1,0:T(8,128)(2,1)}, u32[]{:S(2)}) copy-start(bf16[1,512,128]{2,1,0:T(8,128)(2,1)} %param.44) | copy-start | bytes 393220
  7.2 26.2 %copy-start.192 = (bf16[1,1,512,64]{2,3,1,0:T(8,128)(2,1)S(1)}, bf16[1,1,512,64]{2,3,1,0:T(8,128)(2,1)}, u32[]{:S(2)}) copy-start(bf16[1,1,512,64]{2,3,1,0:T(8,128)(2,1)} %param.46) | copy-start | bytes 196612
  7.3 233.2 %all-gather.16.cloned.1.call-start = ((), (), s32[]{:S(2)}) async-start(), calls=%async_computation.32 | async-start | bytes 2621440 | tf_op jit(solution)/shard_map/all_gather | solution.py:304
  8.0 232.5 %all-gather.18.cloned.1.call-start = ((), (), s32[]{:S(2)}) async-start(), calls=%async_computation.33 | async-start | bytes 2621440 | tf_op jit(solution)/shard_map/all_gather | solution.py:305
  8.8 204.0 %collective-permute-start = (bf16[1,256,512]{2,1,0:T(8,128)(2,1)}, bf16[1,256,512]{2,1,0:T(8,128)(2,1)}, u32[]{:S(2)}, u32[]{:S(2)}) collective-permute-start(bf16[1,256,512]{2,1,0:T(8,128)(2,1)} %broadcast.2756), channel_id=1, source_target_pairs={{0,16},{1,17},{2,18},{3,19},{4,20},{5,21},{6,22},{7,23},{8,24},{9,... | collective-permute-start | bytes 786440 | tf_op jit(solution)/shard_map/ppermute | solution.py:10
  14.3 463.3 %collective-permute-start.3 = (bf16[1,256,512]{2,1,0:T(8,128)(2,1)}, bf16[1,256,512]{2,1,0:T(8,128)(2,1)}, u32[]{:S(2)}, u32[]{:S(2)}) collective-permute-start(bf16[1,256,512]{2,1,0:T(8,128)(2,1)} %broadcast.2756), channel_id=1, source_target_pairs={{16,0},{17,1},{18,2},{19,3},{20,4},{21,5},{22,6},{23,7},{24,8},{25... | collective-permute-start | bytes 786440 | tf_op jit(solution)/shard_map/ppermute | solution.py:10
  15.6 517.5 %reduce-scatter.29.cloned.1.call-start = ((), (), s32[]{:S(2)}) async-start(), calls=%async_computation.19 | async-start | bytes 327680 | tf_op jit(solution)/shard_map/reduce_scatter | solution.py:228
  17.9 66.8 %copy-start.154 = (f32[1,1,512]{2,1,0:T(1,128)}, f32[1,1,512]{2,1,0:T(1,128)S(1)}, u32[]{:S(2)}) copy-start(f32[1,1,512]{2,1,0:T(1,128)S(1)} %get-tuple-element.480) | copy-start | bytes 6148
  18.5 31.0 %copy-start.4 = (bf16[256,512]{1,0:T(8,128)(2,1)}, bf16[256,512]{1,0:T(8,128)(2,1)S(1)}, u32[]{:S(2)}) copy-start(bf16[256,512]{1,0:T(8,128)(2,1)S(1)} %fusion.226) | copy-start | bytes 786436
  18.7 62.9 %copy-start.96 = (bf16[256,512]{1,0:T(8,128)(2,1)}, bf16[256,512]{1,0:T(8,128)(2,1)S(1)}, u32[]{:S(2)}) copy-start(bf16[256,512]{1,0:T(8,128)(2,1)S(1)} %fusion.310) | copy-start | bytes 786436
  20.9 28.7 %copy-start.162 = (s32[1,1,1,256,2]{3,4,2,1,0:T(2,128)}, s32[1,1,1,256,2]{3,4,2,1,0:T(2,128)S(1)}, u32[]{:S(2)}) copy-start(s32[1,1,1,256,2]{3,4,2,1,0:T(2,128)S(1)} %get-tuple-element.469) | copy-start | bytes 6148
  20.9 60.9 %copy-start.168 = (s32[1,1,1,256,2]{3,4,2,1,0:T(2,128)}, s32[1,1,1,256,2]{3,4,2,1,0:T(2,128)S(1)}, u32[]{:S(2)}) copy-start(s32[1,1,1,256,2]{3,4,2,1,0:T(2,128)S(1)} %get-tuple-element.471) | copy-start | bytes 6148
  20.9 68.5 %copy-start.166 = (s32[1,1,1,256,2]{3,4,2,1,0:T(2,128)}, s32[1,1,1,256,2]{3,4,2,1,0:T(2,128)S(1)}, u32[]{:S(2)}) copy-start(s32[1,1,1,256,2]{3,4,2,1,0:T(2,128)S(1)} %get-tuple-element.470) | copy-start | bytes 6148
  29.6 47.7 %copy-start.354 = (s32[512]{0:T(512)}, s32[512]{0:T(512)S(1)}, u32[]{:S(2)}) copy-start(s32[512]{0:T(512)S(1)} %get-tuple-element.548) | copy-start | bytes 6148
  31.1 54.5 %copy-start.170 = (s32[1,1,256,2]{2,3,1,0:T(2,128)}, s32[1,1,256,2]{2,3,1,0:T(2,128)S(1)}, u32[]{:S(2)}) copy-start(s32[1,1,256,2]{2,3,1,0:T(2,128)S(1)} %get-tuple-element.461) | copy-start | bytes 6148
  31.1 56.7 %copy-start.174 = (s32[1,1,256,2]{2,3,1,0:T(2,128)}, s32[1,1,256,2]{2,3,1,0:T(2,128)S(1)}, u32[]{:S(2)}) copy-start(s32[1,1,256,2]{2,3,1,0:T(2,128)S(1)} %get-tuple-element.460) | copy-start | bytes 6148
  46.9 22.5 %copy-start.237 = (s32[1024]{0:T(1024)}, s32[1024]{0:T(1024)S(1)}, u32[]{:S(2)}) copy-start(s32[1024]{0:T(1024)S(1)} %pad_clamp_fusion.6) | copy-start | bytes 12292
  89.7 39.2 %copy-start.123 = (f32[256,2]{1,0:T(8,128)}, f32[256,2]{1,0:T(8,128)S(1)}, u32[]{:S(2)}) copy-start(f32[256,2]{1,0:T(8,128)S(1)} %copy.204) | copy-start | bytes 6148
  93.5 30.4 %copy-start.352 = (s32[512]{0:T(512)}, s32[512]{0:T(512)S(1)}, u32[]{:S(2)}) copy-start(s32[512]{0:T(512)S(1)} %get-tuple-element.500) | copy-start | bytes 6148
  131.6 46.6 %copy-start.80 = (bf16[4,1,64,512]{3,2,1,0:T(8,128)(2,1)S(1)}, bf16[4,1,64,512]{3,2,1,0:T(8,128)(2,1)}, u32[]{:S(2)}) copy-start(bf16[4,1,64,512]{3,2,1,0:T(8,128)(2,1)} %all-gather.2) | copy-start | bytes 786436
  131.6 21.9 %copy-start.224 = (f32[256]{0:T(256)}, f32[256]{0:T(256)S(1)}, u32[]{:S(2)}) copy-start(f32[256]{0:T(256)S(1)} %broadcast_multiply_fusion.10) | copy-start | bytes 3076
  132.4 21.1 %copy-start.290 = (f32[256]{0:T(256)}, f32[256]{0:T(256)S(1)}, u32[]{:S(2)}) copy-start(f32[256]{0:T(256)S(1)} %fusion.490) | copy-start | bytes 3076
  132.7 53.2 %copy-start.2 = (bf16[256,512]{1,0:T(8,128)(2,1)}, bf16[256,512]{1,0:T(8,128)(2,1)S(1)}, u32[]{:S(2)}) copy-start(bf16[256,512]{1,0:T(8,128)(2,1)S(1)} %get-tuple-element.476) | copy-start | bytes 786436
  132.9 28.7 %copy-start.183 = (f32[256,2]{0,1:T(2,128)}, f32[256,2]{0,1:T(2,128)S(1)}, u32[]{:S(2)}) copy-start(f32[256,2]{0,1:T(2,128)S(1)} %select_reduce_fusion.20) | copy-start | bytes 6148
  132.9 28.7 %copy-start.252 = (f32[256]{0:T(256)}, f32[256]{0:T(256)S(1)}, u32[]{:S(2)}) copy-start(f32[256]{0:T(256)S(1)} %reduce_max.142) | copy-start | bytes 3076
  133.0 28.6 %copy-start.303 = (f32[256]{0:T(256)}, f32[256]{0:T(256)S(1)}, u32[]{:S(2)}) copy-start(f32[256]{0:T(256)S(1)} %fusion.469) | copy-start | bytes 3076
  133.9 27.7 %copy-start.181 = (f32[256,2]{0,1:T(2,128)}, f32[256,2]{0,1:T(2,128)S(1)}, u32[]{:S(2)}) copy-start(f32[256,2]{0,1:T(2,128)S(1)} %select_reduce_fusion.22) | copy-start | bytes 6148
  133.9 27.7 %copy-start.250 = (f32[256]{0:T(256)}, f32[256]{0:T(256)S(1)}, u32[]{:S(2)}) copy-start(f32[256]{0:T(256)S(1)} %reduce_max.135) | copy-start | bytes 3076
  133.9 27.7 %copy-start.301 = (f32[256]{0:T(256)}, f32[256]{0:T(256)S(1)}, u32[]{:S(2)}) copy-start(f32[256]{0:T(256)S(1)} %fusion.465) | copy-start | bytes 3076
  138.4 23.2 %copy-start.285 = (s32[512]{0:T(512)}, s32[512]{0:T(512)S(1)}, u32[]{:S(2)}) copy-start(s32[512]{0:T(512)S(1)} %get-tuple-element.497) | copy-start | bytes 6148
  161.0 24.9 %copy-start.79 = (bf16[4,512,64]{1,2,0:T(8,128)(2,1)}, bf16[4,512,64]{1,2,0:T(8,128)(2,1)S(1)}, u32[]{:S(2)}) copy-start(bf16[4,512,64]{1,2,0:T(8,128)(2,1)S(1)} %all_gather.51) | copy-start | bytes 786436
  168.3 23.3 %copy-start.36 = (bf16[4,64,512]{2,1,0:T(8,128)(2,1)}, bf16[4,64,512]{2,1,0:T(8,128)(2,1)S(1)}, u32[]{:S(2)}) copy-start(bf16[4,64,512]{2,1,0:T(8,128)(2,1)S(1)} %all_gather.53) | copy-start | bytes 786436
  194.1 25.9 %copy-start.381 = (s32[512]{0:T(512)S(1)}, s32[512]{0:T(512)}, u32[]{:S(2)}) copy-start(s32[512]{0:T(512)} %copy-done.380) | copy-start | bytes 6148
  246.9 11.8 collective-permute-start.1
  292.7 10.0 collective-permute-start.2
  336.7 28.2 %copy-start.156 = (f32[256]{0:T(256)}, f32[256]{0:T(256)S(1)}, u32[]{:S(2)}) copy-start(f32[256]{0:T(256)S(1)} %broadcast_multiply_fusion.1) | copy-start | bytes 3076
  369.5 34.4 %copy-start.121 = (f32[256,2]{1,0:T(8,128)}, f32[256,2]{1,0:T(8,128)S(1)}, u32[]{:S(2)}) copy-start(f32[256,2]{1,0:T(8,128)S(1)} %copy.222) | copy-start | bytes 6148
  406.7 68.1 %copy-start.37 = (f32[256,512]{1,0:T(8,128)}, f32[256,512]{1,0:T(8,128)S(1)}, u32[]{:S(2)}) copy-start(f32[256,512]{1,0:T(8,128)S(1)} %get-tuple-element.427) | copy-start | bytes 1572868
  425.7 24.3 %copy-start.145 = (bf16[512,64]{1,0:T(8,128)(2,1)}, bf16[512,64]{1,0:T(8,128)(2,1)S(1)}, u32[]{:S(2)}) copy-start(bf16[512,64]{1,0:T(8,128)(2,1)S(1)} %scatter_custom_fusion.10) | copy-start | bytes 196612
  509.0 105.9 %reduce-scatter.33.cloned.1.call-start = ((), (), s32[]{:S(2)}) async-start(), calls=%async_computation.21 | async-start | bytes 327680 | tf_op jit(solution)/shard_map/reduce_scatter | solution.py:228
  535.0 26.4 %collective-permute-start.4 = (bf16[1,256,512]{2,1,0:T(8,128)(2,1)}, bf16[1,256,512]{2,1,0:T(8,128)(2,1)}, u32[]{:S(2)}, u32[]{:S(2)}) collective-permute-start(bf16[1,256,512]{2,1,0:T(8,128)(2,1)} %fusion.127), channel_id=1, source_target_pairs={{16,0},{17,1},{18,2},{19,3},{20,4},{21,5},{22,6},{23,7},{24,8},{25... | collective-permute-start | bytes 786440 | tf_op jit(solution)/shard_map/ppermute | solution.py:10
  591.9 23.1 %copy-start.74 = (bf16[512,128]{1,0:T(8,128)(2,1)S(1)}, bf16[512,128]{1,0:T(8,128)(2,1)}, u32[]{:S(2)}) copy-start(bf16[512,128]{1,0:T(8,128)(2,1)} %param.52) | copy-start | bytes 393220
  592.9 221.5 %reduce-scatter.31.cloned.1.call-start = ((), (), s32[]{:S(2)}) async-start(), calls=%async_computation.20 | async-start | bytes 327680 | tf_op jit(solution)/shard_map/reduce_scatter | solution.py:228
  599.1 27.4 %copy-start.288 = (s32[512]{0:T(512)S(1)}, s32[512]{0:T(512)}, u32[]{:S(2)}) copy-start(s32[512]{0:T(512)} %copy-done.287) | copy-start | bytes 6148
  616.7 21.1 %collective-permute-start.5 = (bf16[1,256,512]{2,1,0:T(8,128)(2,1)}, bf16[1,256,512]{2,1,0:T(8,128)(2,1)}, u32[]{:S(2)}, u32[]{:S(2)}) collective-permute-start(bf16[1,256,512]{2,1,0:T(8,128)(2,1)} %fusion.126), channel_id=1, source_target_pairs={{16,0},{17,1},{18,2},{19,3},{20,4},{21,5},{22,6},{23,7},{24,8},{25... | collective-permute-start | bytes 786440 | tf_op jit(solution)/shard_map/ppermute | solution.py:10
  754.8 64.7 %reduce-scatter.35.cloned.1.call-start = ((), (), s32[]{:S(2)}) async-start(), calls=%async_computation.22 | async-start | bytes 327680 | tf_op jit(solution)/shard_map/reduce_scatter | solution.py:228
  773.7 51.5 %reduce-scatter.27.cloned.1.call-start = ((), (), s32[]{:S(2)}) async-start(), calls=%async_computation.18 | async-start | bytes 327680 | tf_op jit(solution)/shard_map/reduce_scatter | solution.py:228
  778.9 96.8 %reduce-scatter.47.cloned.1.call-start = ((), (), s32[]{:S(2)}) async-start(), calls=%async_computation.28 | async-start | bytes 327680 | tf_op jit(solution)/shard_map/reduce_scatter | solution.py:228
  779.7 27.4 %copy-start.281 = (bf16[256,4]{0,1:T(4,128)(2,1)}, bf16[256,4]{0,1:T(4,128)(2,1)S(1)}, u32[]{:S(2)}) copy-start(bf16[256,4]{0,1:T(4,128)(2,1)S(1)} %select_reduce_fusion) | copy-start | bytes 6148
  781.9 154.3 %reduce-scatter.61.cloned.1.call-start = ((), (), s32[]{:S(2)}) async-start(), calls=%async_computation.37 | async-start | bytes 278528
  782.0 25.4 %copy-start.282 = (bf16[256,4]{0,1:T(4,128)(2,1)}, bf16[256,4]{0,1:T(4,128)(2,1)S(1)}, u32[]{:S(2)}) copy-start(bf16[256,4]{0,1:T(4,128)(2,1)S(1)} %select_reduce_fusion.12) | copy-start | bytes 6148
  808.5 154.7 %reduce-scatter.57.cloned.1.call-start = ((), (), s32[]{:S(2)}) async-start(), calls=%async_computation.35 | async-start | bytes 278528
  835.7 186.0 %reduce-scatter.55.cloned.1.call-start = ((), (), s32[]{:S(2)}) async-start(), calls=%async_computation.34 | async-start | bytes 278528
  838.7 241.2 %reduce-scatter.53.cloned.1.call-start = ((), (), s32[]{:S(2)}) async-start(), calls=%async_computation.31 | async-start | bytes 557056 | tf_op jit(solution)/shard_map/reduce_scatter | solution.py:517
  842.9 295.8 %reduce-scatter.51.cloned.1.call-start = ((), (), s32[]{:S(2)}) async-start(), calls=%async_computation.30 | async-start | bytes 557056 | tf_op jit(solution)/shard_map/reduce_scatter | solution.py:511
  871.0 325.4 %reduce-scatter.49.cloned.1.call-start = ((), (), s32[]{:S(2)}) async-start(), calls=%async_computation.29 | async-start | bytes 278528 | tf_op jit(solution)/shard_map/reduce_scatter | solution.py:498
  877.7 376.5 %reduce-scatter.59.cloned.1.call-start = ((), (), s32[]{:S(2)}) async-start(), calls=%async_computation.36 | async-start | bytes 278528
  880.3 432.7 %reduce-scatter.41.cloned.1.call-start = ((), (), s32[]{:S(2)}) async-start(), calls=%async_computation.25 | async-start | bytes 557056 | tf_op jit(solution)/shard_map/reduce_scatter | solution.py:508
  902.6 469.5 %reduce-scatter.39.cloned.1.call-start = ((), (), s32[]{:S(2)}) async-start(), calls=%async_computation.24 | async-start | bytes 557056 | tf_op jit(solution)/shard_map/reduce_scatter | solution.py:502
  931.6 498.9 %reduce-scatter.37.cloned.1.call-start = ((), (), s32[]{:S(2)}) async-start(), calls=%async_computation.23 | async-start | bytes 278528 | tf_op jit(solution)/shard_map/reduce_scatter | solution.py:496
  941.7 512.1 %all-reduce.3.cloned.1.call-start = ((), (), s32[]{:S(2)}) async-start(), calls=%async_computation.38 | async-start | bytes 169984 | tf_op jit(solution)/shard_map/psum | solution.py:535
  1196.5 334.9 %reduce-scatter.45.cloned.1.call-start = ((), (), s32[]{:S(2)}) async-start(), calls=%async_computation.27 | async-start | bytes 4456448 | tf_op jit(solution)/shard_map/reduce_scatter | solution.py:501
  1214.1 393.6 %reduce-scatter.43.cloned.1.call-start = ((), (), s32[]{:S(2)}) async-start(), calls=%async_computation.26 | async-start | bytes 4456448 | tf_op jit(solution)/shard_map/reduce_scatter | solution.py:500
  1259.2 356.1 %copy-start.130 = (f32[1,2,1,256,512]{4,3,1,2,0:T(8,128)}, f32[1,2,1,256,512]{4,3,1,2,0:T(8,128)S(1)}, u32[]{:S(2)}) copy-start(f32[1,2,1,256,512]{4,3,1,2,0:T(8,128)S(1)} %bitcast_dynamic-update-slice_fusion) | copy-start | bytes 3145732
  (353 other events, 1707.0 us)
Sparse Core Ops, SparseCore 0:
  9.6 25.2 all-gather.15
  36.5 22.5 all-gather.17
  509.1 23.9 reduce-scatter.28
  593.1 21.8 reduce-scatter.32
  754.9 21.9 reduce-scatter.30
  779.9 20.0 reduce-scatter.34
  803.1 20.0 reduce-scatter.26
  825.7 20.0 reduce-scatter.46
  849.4 55.5 reduce-scatter.60
  908.9 54.2 reduce-scatter.56
  967.3 54.3 reduce-scatter.54
  1025.1 54.7 reduce-scatter.52
  1083.9 54.8 reduce-scatter.50
  1142.1 54.3 reduce-scatter.48
  1199.8 54.2 reduce-scatter.58
  1258.1 54.7 reduce-scatter.40
  1317.4 54.7 reduce-scatter.38
  1376.1 54.3 reduce-scatter.36
  1433.7 20.1 all-reduce.2
  1458.1 73.2 reduce-scatter.44
  1536.3 71.3 reduce-scatter.42
where the time goes:
time: 1640 us; the launch traced here: 1620 us
  waiting for transfers between devices  649 us (40%)
  Pallas kernels  255 us (16%)
  local copies, waits for them, and re-layouts  253 us (15%)
  other arithmetic  204 us (12%)
  matrix products  143 us (9%)
  blocking collectives  77.7 us (5%)
  starting transfers between devices  21.4 us (1%)
  between operations  20 us (1%)
    another operation x39, Pallas kernels  239 us
    unnamed x25, waiting for transfers between devices  92.7 us
    reduce_scatter x1, waiting for transfers between devices, body(): lax.psum_scatter(back_blocks, ('dp', 'expert'), scatter_dimension=0, tile...  77.6 us
    reduce_scatter x1, waiting for transfers between devices, body(): lax.psum_scatter(in_blocks, ('dp', 'expert'), scatter_dimension=0, tiled=...  76.3 us
    reduce_scatter x1, waiting for transfers between devices, body(): lax.psum_scatter(query_blocks(query_sum, dp_size, ex_size), ('dp', 'exper...  59.2 us
    reduce_scatter x1, waiting for transfers between devices, body(): lax.psum_scatter(query_blocks(cquery_sum, dp_size, ex_size), ('dp', 'expe...  58.8 us
    reduce_scatter x1, waiting for transfers between devices, body(): lax.psum_scatter(kv_sum, ('dp', 'expert'), scatter_dimension=0, tiled=True)  58.3 us
    reduce_scatter x1, waiting for transfers between devices, body(): lax.psum_scatter(ckv_sum, ('dp', 'expert'), scatter_dimension=0, tiled=True)  57.7 us
  transfers between devices with their start and end apart: 27, of which 16 were waited for; matrix products, arithmetic and copies ran while one was open for 27% of the time, Pallas kernels for 13%

commit v1 on v0

v1 whole, which is shorter than its diff:
```python
from types import SimpleNamespace

import jax
import jax.numpy as jnp
from jax import lax
from jax.experimental import pallas as pl
from jax.experimental.pallas import tpu as pltpu
from jax.sharding import PartitionSpec as P

F32 = jnp.float32
BF16 = jnp.bfloat16
MESH = pl.DeviceIdType.MESH
RT = 16


def nn(a, b):
    return lax.dot_general(a, b, (((1,), (0,)), ((), ())), preferred_element_type=F32)


def nt(a, b):
    return lax.dot_general(a, b, (((1,), (1,)), ((), ())), preferred_element_type=F32)


def tn(a, b):
    return lax.dot_general(a, b, (((0,), (0,)), ((), ())), preferred_element_type=F32)


def gelu_parts(h):
    c = 0.7978845608028654
    h2 = h * h
    t = jnp.tanh(c * h * (1.0 + 0.044715 * h2))
    half = 0.5 * (1.0 + t)
    slope = half + 0.5 * h * (1.0 - t * t) * (c * (1.0 + 3 * 0.044715 * h2))
    return h * half, slope


def norm_stats(x):
    centred = x - jnp.mean(x, -1, keepdims=True)
    r = lax.rsqrt(jnp.mean(centred * centred, -1, keepdims=True) + 1e-05)
    return centred * r, r


def norm_back(x, gain, grad):
    xhat, r = norm_stats(x)
    gg = grad * gain
    m1 = jnp.mean(gg, -1, keepdims=True)
    m2 = jnp.mean(gg * xhat, -1, keepdims=True)
    return (
        r * (gg - m1 - xhat * m2),
        jnp.sum(grad * xhat, 0, keepdims=True),
        jnp.sum(grad, 0, keepdims=True),
    )


def make_plan(dims):
    (NI, L, D, SEQ, T, NE, HD, HB, E, DP) = dims
    npd = NE // E
    QB = npd * HD
    NQ = NE * HD
    X = E // 2
    DB = D // DP
    ins = [
        "x", "cot", "pairs", "routes_s", "routes_c", "ng", "nb", "wkv", "wr", "wq", "wo", "win",
        "wback", "cg", "cb", "ckv", "cr", "cq", "co",
    ]
    outs = [
        ("o_layer", (NI, L, D), BF16),
        ("o_ig", (NI, L, D), F32),
        ("o_in", (DB, HB), F32),
        ("o_back", (DB, HB), F32),
        ("o_qos", (DB, 2 * QB), F32),
        ("o_qoc", (DB, 2 * QB), F32),
        ("o_kv", (2, DB, 2 * HD), F32),
        ("o_small", (24, D), F32),
    ]
    bufs = [
        ("win_all", (E, D, HB), BF16),
        ("wback_all", (E, HB, D), BF16),
        ("wqr", (2, NQ + RT, D), BF16),
        ("wo_all", (2, NQ, D), BF16),
        ("x1", (NI, L, D), F32),
        ("x2", (NI, L, D), F32),
        ("n", (NI, 3, L, D), BF16),
        ("dz", (NI, L, D), BF16),
        ("acc", (L, D), F32),
        ("h", (NI, E, L, HB), F32),
        ("dh", (max(NI * E * L, E * D), HB), BF16),
        ("kv_s", (NI, SEQ, 2 * HD), BF16),
        ("kv_c", (NI, SEQ, 2 * HD), BF16),
        ("kvt", (2, NI, 2 * HD, SEQ), BF16),
        ("bias", (SEQ, L), F32),
        ("qt", (2, NI, T, HD, L), BF16),
        ("gate", (2, NI, T, 8, L), F32),
        ("p", (2, NI, T, SEQ, L), BF16),
        ("heads", (2, NI, T, HD, L), F32),
        ("ht", (2, NI, NQ, L), BF16),
        ("dq", (T, HD, L), BF16),
        ("dkv_acc", (SEQ, 2 * HD), F32),
        ("dkv_send", (NI, SEQ, 2 * HD), BF16),
        ("dkv_recv", (NI, E, L, 2 * HD), BF16),
        ("dckv_send", (NI, SEQ, 2 * HD), BF16),
        ("dckv_recv", (NI, E, L, 2 * HD), BF16),
        ("ckv_own", (NI, L, 2 * HD), BF16),
        ("g_big", (E, 2, D, HB), F32),
        ("g_qr", (2, NQ + RT, D), F32),
        ("g_o", (2, NQ, D), F32),
        ("g_kv", (2, D, 2 * HD), F32),
        ("small", (24, D), F32),
        ("a_big_r", (2, X * D, HB), BF16),
        ("a_qo", (X, 4 * QB, D), BF16),
        ("a_qo_r", (X, 4 * QB, D), BF16),
        ("b_big", (X - 1, 2, D, HB), BF16),
        ("b_big_r", (X - 1, 2, D, HB), BF16),
        ("b_qo", (X - 1, 4 * QB, D), BF16),
        ("b_qo_r", (X - 1, 4 * QB, D), BF16),
        ("c_big", (DP, 2, DB, HB), BF16),
        ("c_big_r", (DP, 2, DB, HB), BF16),
        ("c_qo", (DP, DB, 4 * QB), F32),
        ("c_qo_r", (DP, DB, 4 * QB), F32),
        ("own_qo", (D, 4 * QB), F32),
        ("kv_r", (DP, 2, DB, 2 * HD), F32),
        ("kv_sum", (2, DB, 2 * HD), F32),
        ("kv_x", (E, 2, DB, 2 * HD), F32),
        ("sm_x", (E, 24, D), F32),
        ("sm_sum", (24, D), F32),
        ("sm_d", (DP, 24, D), F32),
        ("sec_qo", (DB, 2 * QB), F32),
        ("sec_qo_r", (DB, 2 * QB), F32),
        ("sec_kv_r", (DB, 2 * HD), F32),
        ("sec_sm_r", (24, D), F32),
    ]
    sems = [
        ("q_s", (4, E)), ("q_r", (4, E)),
        ("sib_s", (2,)), ("sib_r", (2,)),
        ("wx_s", (2, X)), ("wx_r", (2, X)),
        ("wf_s", (2, X)), ("wf_r", (2, X)),
        ("kv_ss", (NI, E)), ("kv_rs", (NI, E)),
        ("ckv_s", (NI, E)), ("ckv_r", (NI, E)),
        ("dckv_s", (NI, E)), ("dckv_r", (NI, E)),
        ("dkv_s", (NI, E)), ("dkv_r", (NI, E)),
        ("a_s", (3,)), ("a_r", (3,)),
        ("b_s", (3, X - 1)), ("b_r", (3, X - 1)),
        ("c_s", (2, DP)), ("c_r", (2, DP)),
        ("kd_s", (DP,)), ("kd_r", (DP,)),
        ("ke_s", (E,)), ("ke_r", (E,)),
        ("se_s", (E,)), ("se_r", (E,)),
        ("sd_s", (DP,)), ("sd_r", (DP,)),
        ("sec_s", (3,)), ("sec_r", (3,)),
    ]
    return ins, outs, bufs, sems


def make_kernel(dims):
    (NI, L, D, SEQ, T, NE, HD, HB, E, DP) = dims
    npd = NE // E
    QB = npd * HD
    NQ = NE * HD
    X = E // 2
    DB = D // DP
    scale = HD ** -0.5
    ins, outs, bufs, sems = make_plan(dims)
    names = ins + [o[0] for o in outs] + [b[0] for b in bufs] + [s[0] for s in sems]

    def kernel(*refs):
        r = SimpleNamespace(**dict(zip(names, refs)))
        sec = lax.axis_index("section")
        dpi = lax.axis_index("dp")
        me = lax.axis_index("expert")
        core = lax.rem(me, 2)
        xi = me // 2
        sib = xi * 2 + (1 - core)
        dec = sec == 1
        enc = sec == 0
        other = 1 - sec
        row0 = pl.multiple_of(me * L, L)

        def to_expert(j):
            return (sec, dpi, j)

        def to_dp(j):
            return (sec, j, me)

        def to_section(j):
            return (other, dpi, j)

        def rcopy(src, dst, ssem, rsem, dev):
            return pltpu.make_async_remote_copy(
                src_ref=src, dst_ref=dst, send_sem=ssem, recv_sem=rsem, device_id=dev,
                device_id_type=MESH,
            )

        def qblock(a, j):
            return r.wqr.at[a, pl.ds(pl.multiple_of(j * QB, QB), QB)]

        def oblock(a, j):
            return r.wo_all.at[a, pl.ds(pl.multiple_of(j * QB, QB), QB)]

        def q_copy(kind, block, to, frm):
            ref = qblock(kind // 2, block) if kind % 2 == 0 else oblock(kind // 2, block)
            return rcopy(ref, ref, r.q_s.at[kind, to], r.q_r.at[kind, frm], to_expert(to))

        def w_ref(kind, c):
            return (r.win_all if kind == 0 else r.wback_all).at[c]

        def sib_copy(kind, c):
            ref = w_ref(kind, c)
            return rcopy(ref, ref, r.sib_s.at[kind], r.sib_r.at[kind], to_expert(sib))

        def wx_copy(kind, c, to_x, frm_x):
            ref = w_ref(kind, c)
            return rcopy(
                ref, ref, r.wx_s.at[kind, to_x], r.wx_r.at[kind, frm_x], to_expert(to_x * 2 + core)
            )

        def wf_copy(kind, c, x):
            ref = w_ref(kind, c)
            return rcopy(ref, ref, r.wf_s.at[kind, x], r.wf_r.at[kind, x], to_expert(sib))

        def rows_of(ref, i, j):
            return ref.at[i, pl.ds(pl.multiple_of(j * L, L), L)]

        def kv_copy(i, block, to, frm):
            ref = rows_of(r.kv_s, i, block)
            return rcopy(ref, ref, r.kv_ss.at[i, to], r.kv_rs.at[i, frm], to_expert(to))

        def ckv_copy(i, block, to, frm):
            return rcopy(
                r.ckv_own.at[i], rows_of(r.kv_c, i, block), r.ckv_s.at[i, to], r.ckv_r.at[i, frm],
                to_section(to),
            )

        def dckv_copy(i, to, frm):
            return rcopy(
                rows_of(r.dckv_send, i, to), r.dckv_recv.at[i, frm], r.dckv_s.at[i, to],
                r.dckv_r.at[i, frm], to_section(to),
            )

        def dkv_copy(i, to, frm):
            return rcopy(
                rows_of(r.dkv_send, i, to), r.dkv_recv.at[i, frm], r.dkv_s.at[i, to],
                r.dkv_r.at[i, frm], to_expert(to),
            )

        def a_copy(kind):
            if kind < 2:
                src, dst = r.dh.at[pl.ds(kind * X * D, X * D)], r.a_big_r.at[kind]
            else:
                src, dst = r.a_qo, r.a_qo_r
            return rcopy(src, dst, r.a_s.at[kind], r.a_r.at[kind], to_expert(sib))

        def b_copy(kind, o):
            if kind < 2:
                src, dst = r.b_big.at[o, kind], r.b_big_r.at[o, kind]
            else:
                src, dst = r.b_qo.at[o], r.b_qo_r.at[o]
            to = lax.rem(xi + o + 1, X) * 2 + core
            return rcopy(src, dst, r.b_s.at[kind, o], r.b_r.at[kind, o], to_expert(to))

        def c_copy(kind, to, frm):
            src, dst = (r.c_big, r.c_big_r) if kind == 0 else (r.c_qo, r.c_qo_r)
            return rcopy(src.at[to], dst.at[frm], r.c_s.at[kind, to], r.c_r.at[kind, frm], to_dp(to))

        def kd_copy(to, frm):
            return rcopy(
                r.g_kv.at[:, pl.ds(pl.multiple_of(to * DB, DB), DB)], r.kv_r.at[frm], r.kd_s.at[to],
                r.kd_r.at[frm], to_dp(to),
            )

        def ke_copy(to, frm):
            return rcopy(r.kv_sum, r.kv_x.at[frm], r.ke_s.at[to], r.ke_r.at[frm], to_expert(to))

        def se_copy(to, frm):
            return rcopy(r.small, r.sm_x.at[frm], r.se_s.at[to], r.se_r.at[frm], to_expert(to))

        def sd_copy(to, frm):
            return rcopy(r.sm_sum, r.sm_d.at[frm], r.sd_s.at[to], r.sd_r.at[frm], to_dp(to))

        def sec_copy(kind):
            src, dst = (
                (r.sec_qo, r.sec_qo_r), (r.o_kv.at[1], r.sec_kv_r), (r.o_small, r.sec_sm_r)
            )[kind]
            return rcopy(src, dst, r.sec_s.at[kind], r.sec_r.at[kind], to_section(me))

        def peers():
            return [lax.rem(me + o, E) for o in range(1, E)]

        def xpeers():
            return [lax.rem(xi + o, X) for o in range(1, X)]

        def dpeers():
            return [lax.rem(dpi + o, DP) for o in range(1, DP)]

        barrier = pltpu.get_barrier_semaphore()
        for j in peers():
            pl.semaphore_signal(barrier, inc=1, device_id=to_expert(j), device_id_type=MESH)
        for j in dpeers():
            pl.semaphore_signal(barrier, inc=1, device_id=to_dp(j), device_id_type=MESH)
        for j in range(E):
            pl.semaphore_signal(barrier, inc=1, device_id=to_section(j), device_id_type=MESH)

        for a, (q_ref, o_ref, wr_ref) in enumerate(
            ((r.wq, r.wo, r.wr), (r.cq, r.co, r.cr))
        ):
            for j in range(npd):
                at = pl.multiple_of(me * QB + j * HD, HD)
                r.wqr[a, pl.ds(at, HD)] = q_ref[j].astype(F32).T.astype(BF16)
                r.wo_all[a, pl.ds(at, HD)] = o_ref[j]
            r.wqr[a, pl.ds(NQ, RT)] = wr_ref[...]
        r.win_all[me] = r.win[...]
        r.wback_all[me] = r.wback[...]

        pl.semaphore_wait(barrier, (E - 1) + (DP - 1) + E)

        for kind in (0, 1):
            for j in peers():
                q_copy(kind, me, j, me).start()

        def norm_rows(x, gain, shift):
            return norm_stats(x)[0] * gain + shift

        def gain_of(which):
            if which == 1:
                return r.cg[...], r.cb[...]
            return r.ng[which // 2 : which // 2 + 1], r.nb[which // 2 : which // 2 + 1]

        def first_norm(i, _):
            g, b = gain_of(0)
            n = norm_rows(r.x[i].astype(F32), g, b).astype(BF16)
            r.n[i, 0] = n
            r.kv_s[i, pl.ds(row0, L)] = nn(n, r.wkv[...]).astype(BF16)
            for j in peers():
                kv_copy(i, me, j, me).start()
            return 0

        lax.fori_loop(0, NI, first_norm, 0)

        for kind in (0, 1):
            sib_copy(kind, me).start()
            for x in xpeers():
                wx_copy(kind, me, x, xi).start()

        @pl.when(dec)
        def _():
            for kind in (2, 3):
                for j in peers():
                    q_copy(kind, me, j, me).start()

        zeros_h = jnp.zeros((HD, L), BF16)

        def set_bias(i, a):
            own = r.pairs[sec, i, :, pl.ds(row0, L)].astype(F32)
            if a == 0:
                keys = r.pairs[sec, i].astype(F32)
            else:
                keys = r.pairs[0, i].astype(F32)
            kc = jnp.broadcast_to(keys, (128, SEQ)).T
            if L > 128:
                kc = jnp.concatenate([kc] * (L // 128), 1)
            same = kc == own
            if a == 0:
                qpos = row0 + lax.broadcasted_iota(jnp.int32, (1, L), 1)
                limit = jnp.where(dec, qpos, SEQ)
                same = same & (lax.broadcasted_iota(jnp.int32, (SEQ, L), 0) <= limit)
            r.bias[...] = jnp.where(same, 0.0, -1e30)

        def route_rows(i, a):
            ref = r.routes_s if a == 0 else r.routes_c
            return [ref[i, k, :, pl.ds(row0, L)] for k in range(T)]

        def pick(rows, route, size):
            total = jnp.zeros((size, L), F32)
            for e in range(NE):
                total = jnp.where(route == e, rows[e * size : (e + 1) * size], total)
            return total

        def project_queries(i, a):
            n = r.n[i, a]
            ql = nt(r.wqr[a], n)
            routes = route_rows(i, a)
            chosen = []
            for k in range(T):
                r.qt[a, i, k] = (pick(ql[:NQ], routes[k], HD).astype(BF16).astype(F32) * scale).astype(BF16)
                chosen.append(pick(ql[NQ : NQ + NE], routes[k], 1))
            top = chosen[0]
            for k in range(1, T):
                top = jnp.maximum(top, chosen[k])
            ex = [jnp.exp(c - top) for c in chosen]
            total = ex[0]
            for k in range(1, T):
                total = total + ex[k]
            for k in range(T):
                r.gate[a, i, k] = jnp.broadcast_to(ex[k] / total, (8, L))

        def attend(i, a, kv_ref, base):
            kv = kv_ref[i]
            r.kvt[a, i] = kv.astype(F32).T.astype(BF16)

            def one(k, _):
                q = jnp.concatenate([r.qt[a, i, k], zeros_h], 0)
                s = nn(kv, q) + r.bias[...]
                m = jnp.max(s, 0, keepdims=True)
                ex = jnp.exp(s - m)
                p = (ex * (1.0 / jnp.sum(ex, 0, keepdims=True))).astype(BF16)
                r.p[a, i, k] = p
                r.heads[a, i, k] = nn(r.kvt[a, i, HD:], p)
                return 0

            lax.fori_loop(0, T, one, 0)
            routes = route_rows(i, a)
            gated = [
                r.heads[a, i, k].astype(BF16).astype(F32) * r.gate[a, i, k, 0:1] for k in range(T)
            ]
            for e in range(NE):
                block = jnp.zeros((HD, L), F32)
                for k in range(T):
                    block = jnp.where(routes[k] == e, gated[k], block)
                r.ht[a, i, e * HD : (e + 1) * HD] = block.astype(BF16)
            return base + tn(r.ht[a, i], r.wo_all[a])

        def attend_back(i, a, kv_ref, dx, send_ref):
            dxb = dx.astype(BF16)
            routes = route_rows(i, a)
            r.g_o[a] += nn(r.ht[a, i], dxb)
            gt = nt(r.wo_all[a], dxb)
            dgates = []
            for k in range(T):
                g = pick(gt, routes[k], HD)
                dgates.append(
                    jnp.sum(r.heads[a, i, k].astype(BF16).astype(F32) * g, 0, keepdims=True)
                )
                r.dq[k] = (g * r.gate[a, i, k, 0:1]).astype(BF16)
            gates = [r.gate[a, i, k, 0:1] for k in range(T)]
            mid = gates[0] * dgates[0]
            for k in range(1, T):
                mid = mid + gates[k] * dgates[k]
            dchosen = [gates[k] * (dgates[k] - mid) for k in range(T)]
            kv = kv_ref[i]
            r.dkv_acc[...] = jnp.zeros_like(r.dkv_acc)

            def one(k, _):
                dheads = r.dq[k]
                p = r.p[a, i, k]
                dv = jnp.concatenate([zeros_h, dheads], 0)
                dp = nn(kv, dv)
                pf = p.astype(F32)
                delta = jnp.sum(dp * pf, 0, keepdims=True)
                ds = (pf * (dp - delta)).astype(BF16)
                qk = jnp.concatenate([r.qt[a, i, k], zeros_h], 0)
                r.dkv_acc[...] += nt(ds, qk) + nt(p, dv)
                r.dq[k] = (nn(r.kvt[a, i, :HD], ds) * scale).astype(BF16)
                return 0

            lax.fori_loop(0, T, one, 0)
            send_ref[i] = r.dkv_acc[...].astype(BF16)
            blocks = []
            for e in range(NE):
                block = jnp.zeros((HD, L), F32)
                for k in range(T):
                    block = jnp.where(routes[k] == e, r.dq[k].astype(F32), block)
                blocks.append(block)
            logit_rows = jnp.zeros((RT, L), F32)
            rows = lax.broadcasted_iota(jnp.int32, (RT, L), 0)
            for k in range(T):
                logit_rows = jnp.where(rows == routes[k], dchosen[k], logit_rows)
            dql = jnp.concatenate(blocks + [logit_rows], 0).astype(BF16)
            r.g_qr[a] += nn(dql, r.n[i, a])
            return tn(dql, r.wqr[a])

        def chunk_at(s):
            x = lax.rem(xi + s // 2, X)
            return x * 2 + jnp.where(lax.rem(s, 2) == 0, core, 1 - core)

        def weights_in(s):
            for kind in (0, 1):
                c = chunk_at(s)

                @pl.when(s == 1)
                def _():
                    sib_copy(kind, c).wait_recv()

                for o in range(1, X):
                    x = lax.rem(xi + o, X)

                    @pl.when(s == 2 * o)
                    def _():
                        wx_copy(kind, c, x, x).wait_recv()
                        wf_copy(kind, c, x).start()

                    @pl.when(s == 2 * o + 1)
                    def _():
                        wf_copy(kind, c, x).wait_recv()

        def dh_rows(i, c):
            return pl.ds(pl.multiple_of((i * E + c) * L, L), L)

        def ffn_hidden(i, wait, finish):
            n = r.n[i, 2]
            if finish:
                r.acc[...] = jnp.zeros_like(r.acc)

            def one(s, _):
                if wait:
                    weights_in(s)
                c = chunk_at(s)
                h = nn(n, r.win_all[c])
                r.h[i, c] = h
                if finish:
                    r.acc[...] += nn(gelu_parts(h)[0].astype(BF16), r.wback_all[c])
                return 0

            lax.fori_loop(0, E, one, 0)

        def ffn_back(i):
            dz = r.dz[i]
            r.acc[...] = jnp.zeros_like(r.acc)

            def one(c, _):
                da = nt(dz, r.wback_all[c])
                dh = (da * gelu_parts(r.h[i, c])[1]).astype(BF16)
                r.dh[dh_rows(i, c)] = dh
                r.acc[...] += nt(dh, r.win_all[c])
                return 0

            lax.fori_loop(0, E, one, 0)
            return r.acc[...]

        def ffn_weights(i):
            nt_ = r.n[i, 2].astype(F32).T.astype(BF16)
            dzt = r.dz[i].astype(F32).T.astype(BF16)
            r.acc[...] = jnp.zeros_like(r.acc)

            def one(c, _):
                act = gelu_parts(r.h[i, c])[0].astype(BF16)
                r.g_big[c, 0] += nn(nt_, r.dh[dh_rows(i, c)])
                r.g_big[c, 1] += nn(dzt, act)

                @pl.when(dec)
                def _():
                    r.acc[...] += nn(act, r.wback_all[c])

                return 0

            lax.fori_loop(0, E, one, 0)

            @pl.when(dec)
            def _():
                r.o_layer[i] = (r.x2[i] + r.acc[...]).astype(BF16)

        def add_small(which, dgain, dshift):
            r.small[2 * which : 2 * which + 1] += dgain
            r.small[2 * which + 1 : 2 * which + 2] += dshift

        def zero(ref):
            ref[...] = jnp.zeros_like(ref)

        r.small[...] = jnp.zeros_like(r.small)
        r.g_qr[...] = jnp.zeros_like(r.g_qr)
        r.g_o[...] = jnp.zeros_like(r.g_o)
        r.g_kv[...] = jnp.zeros_like(r.g_kv)

        def zero_big(c, _):
            r.g_big[c] = jnp.zeros((2, D, HB), F32)
            return 0

        lax.fori_loop(0, E, zero_big, 0)

        for kind in (0, 1):
            for j in peers():
                q_copy(kind, j, j, j).wait_recv()

        def forward(i, _):
            project_queries(i, 0)
            set_bias(i, 0)
            for j in peers():
                kv_copy(i, j, j, j).wait_recv()
            x1 = attend(i, 0, r.kv_s, r.x[i].astype(F32))
            r.x1[i] = x1

            @pl.when(enc)
            def _():
                g, b = gain_of(2)
                r.n[i, 2] = norm_rows(r.x1[i], g, b).astype(BF16)

                @pl.when(i == 0)
                def _():
                    ffn_hidden(0, True, True)

                @pl.when(i > 0)
                def _():
                    ffn_hidden(i, False, True)

                mem = (r.x1[i] + r.acc[...]).astype(BF16)
                r.o_layer[i] = mem
                r.ckv_own[i] = nn(mem, r.ckv[...]).astype(BF16)
                for j in range(E):
                    ckv_copy(i, me, j, me).start()

            @pl.when(dec)
            def _():
                g, b = gain_of(1)
                r.n[i, 1] = norm_rows(r.x1[i], g, b).astype(BF16)
                r.dz[i] = r.cot[i]

            return 0

        lax.fori_loop(0, NI, forward, 0)

        @pl.when(dec)
        def _():
            for s in range(E):
                weights_in(jnp.int32(s))
            for kind in (2, 3):
                for j in peers():
                    q_copy(kind, j, j, j).wait_recv()

            def middle(i, _):
                project_queries(i, 1)
                set_bias(i, 1)
                for j in range(E):
                    ckv_copy(i, j, j, j).wait_recv()
                x2 = attend(i, 1, r.kv_c, r.x1[i])
                r.x2[i] = x2
                g, b = gain_of(2)
                r.n[i, 2] = norm_rows(x2, g, b).astype(BF16)
                ffn_hidden(i, False, False)
                dn = ffn_back(i)
                dx, dg, db = norm_back(r.x2[i], g, dn)
                add_small(2, dg, db)
                r.o_ig[i] = r.cot[i].astype(F32) + dx
                dn = attend_back(i, 1, r.kv_c, r.o_ig[i], r.dckv_send)
                for j in range(E):
                    dckv_copy(i, j, me).start()
                g, b = gain_of(1)
                dx, dg, db = norm_back(r.x1[i], g, dn)
                add_small(1, dg, db)
                r.o_ig[i] += dx
                return 0

            lax.fori_loop(0, NI, middle, 0)

        def send_big(kind):
            for x in range(X):
                r.dh[(kind * X + x) * D : (kind * X + x + 1) * D] = r.g_big[
                    x * 2 + (1 - core), kind
                ].astype(BF16)
            a_copy(kind).start()

        def backward(i, _):
            @pl.when(enc)
            def _():
                total = jnp.zeros((L, 2 * HD), F32)
                for j in range(E):
                    dckv_copy(i, j, j).wait_recv()
                    total = total + r.dckv_recv[i, j].astype(F32)
                dkv = total.astype(BF16)
                r.g_kv[1] += tn(r.o_layer[i], dkv)
                dmem = nt(dkv, r.ckv[...]).astype(BF16).astype(F32)
                dx = r.cot[i].astype(F32) + dmem
                r.o_ig[i] = dx
                r.dz[i] = dx.astype(BF16)
                dn = ffn_back(i)
                g, b = gain_of(2)
                dx, dg, db = norm_back(r.x1[i], g, dn)
                add_small(2, dg, db)
                r.o_ig[i] += dx

            ffn_weights(i)

            @pl.when(i == NI - 1)
            def _():
                send_big(0)
                send_big(1)

            dn = attend_back(i, 0, r.kv_s, r.o_ig[i], r.dkv_send)
            r.acc[...] = dn
            for j in peers():
                dkv_copy(i, j, me).start()
            total = r.dkv_send[i, pl.ds(row0, L)].astype(F32)
            for j in peers():
                dkv_copy(i, j, j).wait_recv()
                total = total + r.dkv_recv[i, j].astype(F32)
            dkv = total.astype(BF16)
            r.g_kv[0] += tn(r.n[i, 0], dkv)
            dn = r.acc[...] + nt(dkv, r.wkv[...])
            g, b = gain_of(0)
            dx, dg, db = norm_back(r.x[i].astype(F32), g, dn)
            add_small(0, dg, db)
            r.o_ig[i] += dx
            return 0

        lax.fori_loop(0, NI, backward, 0)

        for a in range(2):
            r.small[6 + a * NE : 6 + (a + 1) * NE] = r.g_qr[a, NQ : NQ + NE]
        for j in peers():
            se_copy(j, me).start()
        for j in dpeers():
            kd_copy(j, dpi).start()

        def qo_rows(c):
            at = pl.ds(pl.multiple_of(c * QB, QB), QB)
            return jnp.concatenate([r.g_qr[0, at], r.g_o[0, at], r.g_qr[1, at], r.g_o[1, at]], 0)

        for x in range(X):
            r.a_qo[x] = qo_rows(x * 2 + (1 - core)).astype(BF16)
        a_copy(2).start()

        for kind in range(2):
            a_copy(kind).wait_recv()
            for o, x in enumerate(xpeers()):
                r.b_big[o, kind] = (
                    r.g_big[x * 2 + core, kind] + r.a_big_r[kind, pl.ds(pl.multiple_of(x * D, D), D)].astype(F32)
                ).astype(BF16)
                b_copy(kind, o).start()
            r.g_big[me, kind] += r.a_big_r[kind, pl.ds(pl.multiple_of(xi * D, D), D)].astype(F32)
        a_copy(2).wait_recv()
        for o, x in enumerate(xpeers()):
            r.b_qo[o] = (qo_rows(x * 2 + core) + r.a_qo_r[x].astype(F32)).astype(BF16)
            b_copy(2, o).start()
        own_qo = qo_rows(me) + r.a_qo_r[xi].astype(F32)

        total = r.g_kv[:, pl.ds(pl.multiple_of(dpi * DB, DB), DB)]
        for j in dpeers():
            kd_copy(j, j).wait_recv()
            total = total + r.kv_r[j]
        r.kv_sum[...] = total
        for j in peers():
            ke_copy(j, me).start()
        total = r.small[...]
        for j in peers():
            se_copy(j, j).wait_recv()
            total = total + r.sm_x[j]
        r.sm_sum[...] = total
        for j in dpeers():
            sd_copy(j, dpi).start()

        for kind in range(2):
            total = r.g_big[me, kind]
            for o in range(X - 1):
                b_copy(kind, o).wait_recv()
                total = total + r.b_big_r[o, kind].astype(F32)
            r.g_big[me, kind] = total
            for d in range(DP):
                r.c_big[d, kind] = total[d * DB : (d + 1) * DB].astype(BF16)
        for j in dpeers():
            c_copy(0, j, dpi).start()
        for o in range(X - 1):
            b_copy(2, o).wait_recv()
            own_qo = own_qo + r.b_qo_r[o].astype(F32)
        r.own_qo[...] = own_qo.T
        for d in range(DP):
            r.c_qo[d] = r.own_qo[d * DB : (d + 1) * DB]
        for j in dpeers():
            c_copy(1, j, dpi).start()

        total = r.kv_sum[...]
        for j in peers():
            ke_copy(j, j).wait_recv()
            total = total + r.kv_x[j]
        r.o_kv[...] = total
        total = r.sm_sum[...]
        for j in dpeers():
            sd_copy(j, j).wait_recv()
            total = total + r.sm_d[j]
        r.o_small[...] = total
        sec_copy(1).start()
        sec_copy(2).start()

        mine = pl.ds(pl.multiple_of(dpi * DB, DB), DB)
        for j in dpeers():
            c_copy(0, j, j).wait_recv()
        for kind, out in ((0, r.o_in), (1, r.o_back)):
            total = r.g_big[me, kind, mine]
            for j in dpeers():
                total = total + r.c_big_r[j, kind].astype(F32)
            out[...] = total
        total = r.own_qo[mine]
        for j in dpeers():
            c_copy(1, j, j).wait_recv()
            total = total + r.c_qo_r[j]
        r.o_qos[...] = total[:, : 2 * QB]
        r.sec_qo[...] = total[:, 2 * QB :]
        sec_copy(0).start()
        for kind in range(3):
            sec_copy(kind).wait_send()
            sec_copy(kind).wait_recv()
        r.o_qoc[...] = r.sec_qo[...] + r.sec_qo_r[...]
        r.o_kv[1] += r.sec_kv_r[...]
        r.o_small[2:4] += r.sec_sm_r[2:4]
        r.o_small[6 + NE : 6 + 2 * NE] += r.sec_sm_r[6 + NE : 6 + 2 * NE]

        for kind in (0, 1):
            for j in peers():
                q_copy(kind, me, j, me).wait_send()
            sib_copy(kind, me).wait_send()
            for x in xpeers():
                wx_copy(kind, me, x, xi).wait_send()
                wf_copy(kind, x * 2 + core, x).wait_send()

        @pl.when(dec)
        def _():
            for kind in (2, 3):
                for j in peers():
                    q_copy(kind, me, j, me).wait_send()

        def sent(i, _):
            for j in peers():
                kv_copy(i, me, j, me).wait_send()
                dkv_copy(i, j, me).wait_send()

            @pl.when(enc)
            def _():
                for j in range(E):
                    ckv_copy(i, me, j, me).wait_send()

            @pl.when(dec)
            def _():
                for j in range(E):
                    dckv_copy(i, j, me).wait_send()

            return 0

        lax.fori_loop(0, NI, sent, 0)
        for kind in range(3):
            a_copy(kind).wait_send()
            for o in range(X - 1):
                b_copy(kind, o).wait_send()
        for j in dpeers():
            kd_copy(j, dpi).wait_send()
            sd_copy(j, dpi).wait_send()
            for kind in range(2):
                c_copy(kind, j, dpi).wait_send()
        for j in peers():
            ke_copy(j, me).wait_send()
            se_copy(j, me).wait_send()

    return kernel


def body(
    inputs, cotangents, pair_ids, self_routes, cross_routes, norm_gain, norm_bias, w_kv, w_router,
    w_query, w_out, w_in, w_back, cross_gain, cross_bias, cross_kv, cross_router, cross_query,
    cross_out,
):
    E = lax.axis_size("expert")
    DP = lax.axis_size("dp")
    _, MB, R, L, D = inputs.shape
    NI = MB * R
    SEQ = pair_ids.shape[-1]
    T = self_routes.shape[-1]
    NE = w_router.shape[-1]
    HD = w_query.shape[-1]
    HB = w_in.shape[-1]
    npd = NE // E
    QB = npd * HD
    dims = (NI, L, D, SEQ, T, NE, HD, HB, E, DP)
    ins, outs, bufs, sems = make_plan(dims)

    def router_rows(w):
        return jnp.pad(w.T, ((0, RT - NE), (0, 0)))

    operands = [
        inputs.reshape(NI, L, D),
        cotangents.reshape(NI, L, D),
        pair_ids.reshape(2, NI, 1, SEQ),
        jnp.swapaxes(self_routes.reshape(NI, SEQ, T), 1, 2)[:, :, None],
        jnp.swapaxes(cross_routes.reshape(NI, SEQ, T), 1, 2)[:, :, None],
        norm_gain[0],
        norm_bias[0],
        w_kv[0],
        router_rows(w_router[0]),
        w_query[0],
        w_out[0],
        w_in[0],
        w_back[0],
        cross_gain[None],
        cross_bias[None],
        cross_kv,
        router_rows(cross_router),
        cross_query,
        cross_out,
    ]
    vmem = pl.BlockSpec(memory_space=pltpu.VMEM)
    res = pl.pallas_call(
        make_kernel(dims),
        out_shape=[jax.ShapeDtypeStruct(s, t) for _, s, t in outs],
        in_specs=[vmem] * len(operands),
        out_specs=[vmem] * len(outs),
        scratch_shapes=[pltpu.VMEM(s, t) for _, s, t in bufs]
        + [pltpu.SemaphoreType.DMA(s) for _, s in sems],
        compiler_params=pltpu.CompilerParams(
            collective_id=0, has_side_effects=True, vmem_limit_bytes=62 * 1024 * 1024
        ),
        name="layers",
    )(*operands)
    o_layer, o_ig, o_in, o_back, o_qos, o_qoc, o_kv, o_small = res
    me = lax.axis_index("expert")
    dpi = lax.axis_index("dp")
    DB = D // DP
    EB = DB // E
    kv = lax.dynamic_slice_in_dim(o_kv, me * EB, EB, 1)
    small = lax.dynamic_slice_in_dim(o_small, (dpi * E + me) * EB, EB, 1)
    qos = o_qos.reshape(DB, 2, npd, HD)
    qoc = o_qoc.reshape(DB, 2, npd, HD)
    return (
        o_layer.reshape(inputs.shape),
        o_ig.reshape(inputs.shape),
        jnp.stack([small[0], small[4]])[None],
        jnp.stack([small[1], small[5]])[None],
        kv[0][None],
        small[6 : 6 + NE].T[None],
        qos[:, 0].transpose(1, 0, 2)[None],
        qos[:, 1].transpose(1, 2, 0)[None],
        o_in[None],
        o_back.T[None],
        small[2],
        small[3],
        kv[1],
        small[6 + NE : 6 + 2 * NE].T,
        qoc[:, 0].transpose(1, 0, 2),
        qoc[:, 1].transpose(1, 2, 0),
    )


def solution(mesh):
    placed = (
        P("section", None, "dp", "expert", None),
        P("section", None, "dp", "expert", None),
        P(None, None, "dp", None),
        P("section", None, "dp", None, None),
        P(None, "dp", None, None),
        P("section", None, None),
        P("section", None, None),
        P("section", None, None),
        P("section", None, None),
        P("section", "expert", None, None),
        P("section", "expert", None, None),
        P("section", None, "expert"),
        P("section", "expert", None),
        P(),
        P(),
        P(),
        P(),
        P("expert", None, None),
        P("expert", None, None),
    )
    return jax.shard_map(
        body,
        mesh=mesh,
        in_specs=placed,
        out_specs=(
            P("section", None, "dp", "expert", None),
            P("section", None, "dp", "expert", None),
            P("section", None, ("dp", "expert")),
            P("section", None, ("dp", "expert")),
            P("section", ("dp", "expert"), None),
            P("section", ("dp", "expert"), None),
            P("section", "expert", "dp", None),
            P("section", "expert", None, "dp"),
            P("section", "dp", "expert"),
            P("section", "expert", "dp"),
            P(("dp", "expert")),
            P(("dp", "expert")),
            P(("dp", "expert"), None),
            P(("dp", "expert"), None),
            P("expert", "dp", None),
            P("expert", None, "dp"),
        ),
        check_vma=False,
    )
```

time: 1640 us -> 179 us (0.11)
  waiting for transfers between devices: 649 us -> 0 us
  local copies, waits for them, and re-layouts: 253 us -> 14.3 us
  other arithmetic: 204 us -> 0.57 us
  matrix products: 143 us -> 0 us
  Pallas kernels: 255 us -> 161 us
  blocking collectives: 77.7 us -> 0 us
  starting transfers between devices: 21.4 us -> 0 us
  between operations: 20 us -> 0.73 us
    reduce_scatter x14 -> x0, waiting for transfers between devices: 530 us -> none  [the longest x1 77.6 us: body(): lax.psum_scatter(back_blocks, ('dp', 'expert'), scatter_dimension=0, tile...]
    another operation x39 -> x0, Pallas kernels: 239 us -> none
    pallas_call x0 -> x1, Pallas kernels: none -> 161 us  [body(): pl.pallas_call(make_kernel(dims), out_shape=[jax.ShapeDtypeStruct(s, t) f...]
    dot_general x98 -> x0, matrix products: 143 us -> none  [the longest x3 16.8 us: body(): jnp.einsum('rlf,rld->fd', layer_active, grad_low, preferred_element_type=...]
    unnamed x25 -> x0, waiting for transfers between devices: 92.7 us -> none
    all_gather x13 -> x0, blocking collectives: 77.7 us -> none  [the longest x9 52.9 us: token_forward(): kv_all = lax.all_gather(kv_local, 'expert', axis=1, tiled=True)]
    gather x27 -> x0, local copies, waits for them, and re-layouts: 61.9 us -> none  [the longest x9 17.4 us: token_forward(): head_sorted = head_out.reshape(flat_total, head_dim)[order]]
    reduce_sum x81 -> x0, other arithmetic: 56.1 us -> none  [the longest x8 21.2 us: token_forward(): output = jnp.sum(result * gate_vals[..., None], 2)]
  transfers between devices with their start and end apart: 27 -> 0, of which waited for: 16 -> 0; matrix products, arithmetic and copies ran while one was open for 27% -> 0% of each run, Pallas kernels for 13% -> 0%
where the time goes in v1:
time: 179 us; the launch traced here: 177 us
  Pallas kernels  161 us (90%)
  local copies, waits for them, and re-layouts  14.3 us (8%)
    pallas_call x1, Pallas kernels, body(): pl.pallas_call(make_kernel(dims), out_shape=[jax.ShapeDtypeStruct(s, t) f...  161 us
    unnamed x28, local copies, waits for them, and re-layouts  6.17 us

profile of v1, /device:TPU:0, one launch (start us, length us, event | category | flops | bytes accessed | tf_op | source)
XLA Modules:
  0.0 176.7 jit_solution(18184579618823068038)
XLA Ops:
  0.7 0.0 copy-start.4
  0.7 1.6 copy.44
  2.3 0.0 copy-done.4
  2.3 0.0 copy-start.7
  2.3 0.8 copy.45.refs_17_
  3.1 0.0 copy-done.7
  3.1 0.0 copy-start.8
  3.1 0.6 broadcast_in_dim.30.refs_3_
  3.7 0.1 copy-done.8
  3.8 0.0 copy-start.9
  3.8 0.6 broadcast_in_dim.31.refs_4_
  4.4 0.1 copy-done.9
  4.5 0.0 copy-start.10
  4.5 0.6 pad.7.refs_8_
  5.1 0.1 copy-done.10
  5.2 0.6 pad.8.refs_16_
  5.8 161.0 %layers.1 = (bf16[2,256,512]{2,1,0:T(8,128)(2,1)}, f32[2,256,512]{2,1,0:T(8,128)}, f32[128,512]{1,0:T(8,128)}, f32[128,512]{1,0:T(8,128)}, f32[128,128]{1,0:T(8,...) custom-call(bf16[2,256,512]{2,1,0:T(8,128)(2,1)} %bitcast.66, bf16[2,256,512]{2,1,0:T(8,128)(2,1)} %bitcast.67, ...), custom_call_target="tpu_custom_call" | custom-call | tf_op jit(solution)/shard_map/layers/pallas_call | solution.py:884
  166.8 0.0 copy-start.6
  166.8 1.5 dynamic-slice_bitcast_fusion.3
  168.3 0.6 maximum_bitcast_fusion
  168.9 1.4 dynamic-slice_bitcast_fusion.1
  170.3 1.3 dynamic-slice_bitcast_fusion
  171.7 0.0 copy-start.5
  171.7 0.0 copy-start.3
  171.7 0.0 copy-start.1
  171.7 0.0 copy-done.6
  171.7 0.0 copy-start
  171.7 0.1 copy.46
  171.8 0.6 slice_bitcast_fusion.2
  172.4 0.1 copy-done.5
  172.5 0.1 copy.47
  172.6 0.6 slice_bitcast_fusion
  173.2 0.0 copy-done.3
  173.3 0.8 copy.50
  174.1 0.0 copy-done.1
  174.1 0.8 copy.54
  174.9 0.0 copy-done
  174.9 0.0 copy-start.2
  174.9 1.0 copy.55
  175.9 0.1 copy-done.2
  176.0 0.7 copy.56
Async XLA Ops:
  0.7 1.6 copy-start.4
  2.3 0.8 copy-start.7
  3.1 0.7 copy-start.8
  3.8 0.7 copy-start.9
  4.5 0.7 copy-start.10
  166.8 4.9 %copy-start.6 = (f32[128,128]{1,0:T(8,128)S(1)}, f32[128,128]{1,0:T(8,128)}, u32[]{:S(2)}) copy-start(f32[128,128]{1,0:T(8,128)} %get-tuple-element.28) | copy-start | bytes 196612
  171.7 0.8 copy-start.5
  171.7 1.6 copy-start.3
  171.7 2.4 %copy-start.1 = (bf16[2,256,512]{2,1,0:T(8,128)(2,1)S(1)}, bf16[2,256,512]{2,1,0:T(8,128)(2,1)}, u32[]{:S(2)}) copy-start(bf16[2,256,512]{2,1,0:T(8,128)(2,1)} %get-tuple-element.24) | copy-start | bytes 1572868
  171.7 3.2 %copy-start = (f32[2,256,512]{2,1,0:T(8,128)S(1)}, f32[2,256,512]{2,1,0:T(8,128)}, u32[]{:S(2)}) copy-start(f32[2,256,512]{2,1,0:T(8,128)} %get-tuple-element.25) | copy-start | bytes 3145732
  174.9 1.1 copy-start.2

commit v2 on v1

v2 whole, which is shorter than its diff:
```python
from types import SimpleNamespace

import jax
import jax.numpy as jnp
from jax import lax
from jax.experimental import pallas as pl
from jax.experimental.pallas import tpu as pltpu
from jax.sharding import PartitionSpec as P

F32 = jnp.float32
BF16 = jnp.bfloat16
MESH = pl.DeviceIdType.MESH
RT = 16
SR = 32
NP = 4


def nn(a, b):
    return lax.dot_general(a, b, (((1,), (0,)), ((), ())), preferred_element_type=F32)


def nt(a, b):
    return lax.dot_general(a, b, (((1,), (1,)), ((), ())), preferred_element_type=F32)


def tn(a, b):
    return lax.dot_general(a, b, (((0,), (0,)), ((), ())), preferred_element_type=F32)


def gelu_parts(h):
    c = 0.7978845608028654
    h2 = h * h
    t = jnp.tanh(c * h * (1.0 + 0.044715 * h2))
    half = 0.5 * (1.0 + t)
    slope = half + 0.5 * h * (1.0 - t * t) * (c * (1.0 + 3 * 0.044715 * h2))
    return h * half, slope


def norm_stats(x):
    centred = x - jnp.mean(x, -1, keepdims=True)
    r = lax.rsqrt(jnp.mean(centred * centred, -1, keepdims=True) + 1e-05)
    return centred * r, r


def norm_back(x, gain, grad):
    xhat, r = norm_stats(x)
    gg = grad * gain
    m1 = jnp.mean(gg, -1, keepdims=True)
    m2 = jnp.mean(gg * xhat, -1, keepdims=True)
    return (
        r * (gg - m1 - xhat * m2),
        jnp.sum(grad * xhat, 0, keepdims=True),
        jnp.sum(grad, 0, keepdims=True),
    )


def make_plan(dims):
    (NI, L, D, SEQ, T, NE, HD, HB, E, DP) = dims
    npd = NE // E
    QB = npd * HD
    NQ = NE * HD
    X = E // 2
    DB = D // DP
    ins = [
        "x", "cot", "pairs", "routes_s", "routes_c", "ng", "nb", "wkv", "wr", "wq", "wo", "win",
        "wback", "cg", "cb", "ckv", "cr", "cq", "co",
    ]
    outs = [
        ("o_layer", (NI, L, D), BF16),
        ("o_ig", (NI, L, D), F32),
        ("o_in", (DB, HB), F32),
        ("o_back", (DB, HB), F32),
        ("o_qo", (2, DB, 2 * QB), F32),
        ("o_kv", (2, DB, 2 * HD), F32),
        ("o_small", (SR, D), F32),
    ]
    bufs = [
        ("win_all", (E, D, HB), BF16),
        ("wback_all", (E, HB, D), BF16),
        ("wqr", (2, NQ + RT, D), BF16),
        ("wo_all", (2, NQ, D), BF16),
        ("wr_pad", (RT, D), F32),
        ("x1", (NI, L, D), F32),
        ("x2", (NI, L, D), F32),
        ("n", (NI, 3, L, D), BF16),
        ("dz", (NI, L, D), BF16),
        ("acc", (L, D), F32),
        ("act", (NI, E, L, HB), BF16),
        ("dh", (NI, E, L, HB), BF16),
        ("kv_s", (NI, SEQ, 2 * HD), BF16),
        ("kv_c", (NI, SEQ, 2 * HD), BF16),
        ("kvt", (2, NI, 2 * HD, SEQ), BF16),
        ("bias", (SEQ, L), F32),
        ("qt", (2, NI, T, HD, L), BF16),
        ("gate", (2, NI, T, 8, L), F32),
        ("p", (2, NI, T, SEQ, L), BF16),
        ("heads", (2, NI, T, HD, L), F32),
        ("ht", (2, NI, NQ, L), BF16),
        ("dq", (T, HD, L), BF16),
        ("dkv_acc", (SEQ, 2 * HD), F32),
        ("dkv_send", (NI, SEQ, 2 * HD), BF16),
        ("dkv_recv", (NI, E, L, 2 * HD), BF16),
        ("dckv_send", (NI, SEQ, 2 * HD), BF16),
        ("dckv_recv", (NI, E, L, 2 * HD), BF16),
        ("ckv_own", (NI, L, 2 * HD), BF16),
        ("g_big", (E, 2, D, HB), F32),
        ("g_qr", (2, NQ + RT, D), F32),
        ("g_o", (2, NQ, D), F32),
        ("g_kv", (2, D, 2 * HD), F32),
        ("small", (SR, D), F32),
        ("a_big", (2, X, D, HB), BF16),
        ("a_big_r", (2, X, D, HB), BF16),
        ("a_qo", (2, X, 2 * QB, D), BF16),
        ("a_qo_r", (2, X, 2 * QB, D), BF16),
        ("b_big", (X - 1, 2, D, HB), BF16),
        ("b_big_r", (X - 1, 2, D, HB), BF16),
        ("b_qo", (2, X - 1, 2 * QB, D), BF16),
        ("b_qo_r", (2, X - 1, 2 * QB, D), BF16),
        ("c_big", (DP - 1, 2, DB, HB), BF16),
        ("c_big_r", (DP - 1, 2, DB, HB), BF16),
        ("own_qo", (D, 2 * QB), F32),
        ("c_qo", (2, DP - 1, DB, 2 * QB), BF16),
        ("c_qo_r", (2, DP - 1, DB, 2 * QB), BF16),
        ("kv_ar", (D, 2 * HD), F32),
        ("kv_sum", (D, 2 * HD), F32),
        ("kv_b", (D, 2 * HD), BF16),
        ("kv_br", (X - 1, D, 2 * HD), BF16),
        ("kv_c2", (DP - 1, DB, 2 * HD), BF16),
        ("kv_cr", (DP - 1, DB, 2 * HD), BF16),
        ("kv_fin", (DB, 2 * HD), F32),
        ("kv_sib", (DB, 2 * HD), F32),
        ("kv_sec", (DB, 2 * HD), F32),
        ("sm_ar", (SR, D), F32),
        ("sm_b", (SR, D), BF16),
        ("sm_br", (X - 1, SR, D), BF16),
        ("sm_c", (SR, D), BF16),
        ("sm_cr", (DP - 1, SR, D), BF16),
        ("sm_fin", (SR, D), F32),
        ("sm_sec", (SR, D), F32),
        ("qo_fin", (DB, 2 * QB), F32),
        ("qo_sec", (DB, 2 * QB), F32),
    ]
    sems = [
        ("q_s", (2, 2, E)), ("q_r", (2, 2, E)),
        ("sib_s", (2,)), ("sib_r", (2,)),
        ("wx_s", (2, X, NP // 2)), ("wx_r", (2, X, NP // 2)),
        ("wz_s", (2, X, NP // 2)), ("wz_r", (2, X, NP // 2)),
        ("wf_s", (2, X, NP)), ("wf_r", (2, X, NP)),
        ("kv_ss", (NI, E)), ("kv_rs", (NI, E)),
        ("ckv_s", (NI, E)), ("ckv_r", (NI, E)),
        ("dckv_s", (NI, E)), ("dckv_r", (NI, E)),
        ("dkv_s", (NI, E)), ("dkv_r", (NI, E)),
        ("a_s", (2, X)), ("a_r", (2, X)),
        ("b_s", (X - 1, 2, DP)), ("b_r", (X - 1, 2, DP)),
        ("c_s", (2, DP - 1)), ("c_r", (2, DP - 1)),
        ("aq_s", (2,)), ("aq_r", (2,)),
        ("bq_s", (2, X - 1)), ("bq_r", (2, X - 1)),
        ("cq_s", (2, DP - 1)), ("cq_r", (2, DP - 1)),
        ("ka_s", (1,)), ("ka_r", (1,)),
        ("kb_s", (X - 1,)), ("kb_r", (X - 1,)),
        ("kc_s", (DP - 1,)), ("kc_r", (DP - 1,)),
        ("kf_s", (3,)), ("kf_r", (2,)),
        ("sa_s", (1,)), ("sa_r", (1,)),
        ("sb_s", (X - 1,)), ("sb_r", (X - 1,)),
        ("sc_s", (DP - 1,)), ("sc_r", (DP - 1,)),
        ("sec_s", (2,)), ("sec_r", (2,)),
    ]
    return ins, outs, bufs, sems


def make_kernel(dims):
    (NI, L, D, SEQ, T, NE, HD, HB, E, DP) = dims
    npd = NE // E
    QB = npd * HD
    NQ = NE * HD
    X = E // 2
    DB = D // DP
    scale = HD ** -0.5
    ins, outs, bufs, sems = make_plan(dims)
    names = ins + [o[0] for o in outs] + [b[0] for b in bufs] + [s[0] for s in sems]

    def kernel(*refs):
        r = SimpleNamespace(**dict(zip(names, refs)))
        sec = lax.axis_index("section")
        dpi = lax.axis_index("dp")
        me = lax.axis_index("expert")
        core = lax.rem(me, 2)
        xi = me // 2
        sib = xi * 2 + (1 - core)
        dec = sec == 1
        enc = sec == 0
        other = 1 - sec
        half = lax.rem(dpi, 2)
        mate = dpi + 1 - 2 * half
        row0 = pl.multiple_of(me * L, L)

        def to_expert(j):
            return (sec, dpi, j)

        def to_dp(j):
            return (sec, j, me)

        def to_section(j):
            return (other, dpi, j)

        def rcopy(src, dst, ssem, rsem, dev):
            return pltpu.make_async_remote_copy(
                src_ref=src, dst_ref=dst, send_sem=ssem, recv_sem=rsem, device_id=dev,
                device_id_type=MESH,
            )

        def chip(x):
            return x * 2 + core

        def q_copy(a, kind, block, to, slot):
            ref = r.wqr if kind == 0 else r.wo_all
            ref = ref.at[a, pl.ds(pl.multiple_of(block * QB, QB), QB)]
            return rcopy(ref, ref, r.q_s.at[a, kind, slot], r.q_r.at[a, kind, block], to_expert(to))

        def w_ref(kind, c):
            return (r.win_all if kind == 0 else r.wback_all).at[c]

        def w_piece(kind, c, p):
            rows = (D if kind == 0 else HB) // NP
            return w_ref(kind, c).at[pl.ds(pl.multiple_of(p * rows, rows), rows)]

        def sib_copy(kind, c):
            ref = w_ref(kind, c)
            return rcopy(ref, ref, r.sib_s.at[kind], r.sib_r.at[kind], to_expert(sib))

        def wx_copy(kind, c, q, to_x, frm_x):
            ref = w_piece(kind, c, 2 * q + half)
            return rcopy(
                ref, ref, r.wx_s.at[kind, to_x, q], r.wx_r.at[kind, frm_x, q],
                to_expert(chip(to_x)),
            )

        def wz_copy(kind, x, q, parity):
            ref = w_piece(kind, chip(x), 2 * q + parity)
            return rcopy(ref, ref, r.wz_s.at[kind, x, q], r.wz_r.at[kind, x, q], to_dp(mate))

        def wf_copy(kind, c, x, p):
            ref = w_piece(kind, c, p)
            return rcopy(ref, ref, r.wf_s.at[kind, x, p], r.wf_r.at[kind, x, p], to_expert(sib))

        def rows_of(ref, i, j):
            return ref.at[i, pl.ds(pl.multiple_of(j * L, L), L)]

        def kv_copy(i, block, to, slot):
            ref = rows_of(r.kv_s, i, block)
            return rcopy(ref, ref, r.kv_ss.at[i, slot], r.kv_rs.at[i, block], to_expert(to))

        def ckv_copy(i, block, to, frm):
            return rcopy(
                r.ckv_own.at[i], rows_of(r.kv_c, i, block), r.ckv_s.at[i, to], r.ckv_r.at[i, frm],
                to_section(to),
            )

        def dckv_copy(i, to, frm):
            return rcopy(
                rows_of(r.dckv_send, i, to), r.dckv_recv.at[i, frm], r.dckv_s.at[i, to],
                r.dckv_r.at[i, frm], to_section(to),
            )

        def dkv_copy(i, to, frm):
            return rcopy(
                rows_of(r.dkv_send, i, to), r.dkv_recv.at[i, frm], r.dkv_s.at[i, to],
                r.dkv_r.at[i, frm], to_expert(to),
            )

        def over_x(src, dst, ssem, rsem, o):
            return rcopy(src, dst, ssem, rsem, to_expert(chip(lax.rem(xi + o + 1, X))))

        def over_dp(src, dst, ssem, rsem, o):
            return rcopy(src, dst, ssem, rsem, to_dp(lax.rem(dpi + o + 1, DP)))

        def over_sib(src, dst, ssem, rsem):
            return rcopy(src, dst, ssem, rsem, to_expert(sib))

        def a_copy(kind, x):
            return over_sib(
                r.a_big.at[kind, x], r.a_big_r.at[kind, x], r.a_s.at[kind, x], r.a_r.at[kind, x]
            )

        def block_rows(d):
            return pl.ds(pl.multiple_of(d * DB, DB), DB)

        def b_copy(kind, o, d):
            return over_x(
                r.b_big.at[o, kind, block_rows(d)], r.b_big_r.at[o, kind, block_rows(d)],
                r.b_s.at[o, kind, d], r.b_r.at[o, kind, d], o,
            )

        def c_copy(kind, o):
            return over_dp(
                r.c_big.at[o, kind], r.c_big_r.at[o, kind], r.c_s.at[kind, o], r.c_r.at[kind, o], o
            )

        def aq_copy(a):
            return over_sib(r.a_qo.at[a], r.a_qo_r.at[a], r.aq_s.at[a], r.aq_r.at[a])

        def bq_copy(a, o):
            return over_x(
                r.b_qo.at[a, o], r.b_qo_r.at[a, o], r.bq_s.at[a, o], r.bq_r.at[a, o], o
            )

        def cq_copy(a, o):
            return over_dp(
                r.c_qo.at[a, o], r.c_qo_r.at[a, o], r.cq_s.at[a, o], r.cq_r.at[a, o], o
            )

        def ka_copy():
            return over_sib(r.g_kv.at[1 - core], r.kv_ar, r.ka_s.at[0], r.ka_r.at[0])

        def kb_copy(o):
            return over_x(r.kv_b, r.kv_br.at[o], r.kb_s.at[o], r.kb_r.at[o], o)

        def kc_copy(o):
            return over_dp(r.kv_c2.at[o], r.kv_cr.at[o], r.kc_s.at[o], r.kc_r.at[o], o)

        def kf_copy():
            return over_sib(r.kv_fin, r.kv_sib, r.kf_s.at[0], r.kf_r.at[0])

        def ks_copy(to_core):
            return rcopy(
                r.kv_fin, r.kv_sec, r.kf_s.at[1 + to_core], r.kf_r.at[1],
                to_section(xi * 2 + to_core),
            )

        def sa_copy():
            return over_sib(r.small, r.sm_ar, r.sa_s.at[0], r.sa_r.at[0])

        def sb_copy(o):
            return over_x(r.sm_b, r.sm_br.at[o], r.sb_s.at[o], r.sb_r.at[o], o)

        def sc_copy(o):
            return over_dp(r.sm_c, r.sm_cr.at[o], r.sc_s.at[o], r.sc_r.at[o], o)

        def sec_copy(kind):
            src, dst = ((r.qo_fin, r.qo_sec), (r.sm_fin, r.sm_sec))[kind]
            return rcopy(src, dst, r.sec_s.at[kind], r.sec_r.at[kind], to_section(me))

        def peers():
            return [lax.rem(me + o, E) for o in range(1, E)]

        def xpeers():
            return [lax.rem(xi + o, X) for o in range(1, X)]

        def dpeers():
            return [lax.rem(dpi + o, DP) for o in range(1, DP)]

        barrier = pltpu.get_barrier_semaphore()
        for j in peers():
            pl.semaphore_signal(barrier, inc=1, device_id=to_expert(j), device_id_type=MESH)
        for j in dpeers():
            pl.semaphore_signal(barrier, inc=1, device_id=to_dp(j), device_id_type=MESH)
        for j in range(E):
            pl.semaphore_signal(barrier, inc=1, device_id=to_section(j), device_id_type=MESH)

        for a, (q_ref, o_ref, wr_ref) in enumerate(((r.wq, r.wo, r.wr), (r.cq, r.co, r.cr))):
            for j in range(npd):
                at = pl.multiple_of(me * QB + j * HD, HD)
                r.wqr[a, pl.ds(at, HD)] = q_ref[j]
                r.wo_all[a, pl.ds(at, HD)] = o_ref[j]
            r.wr_pad[...] = jnp.zeros_like(r.wr_pad)
            r.wr_pad[:NE] = wr_ref[...].astype(F32)
            r.wqr[a, pl.ds(NQ, RT)] = r.wr_pad[...].astype(BF16)

        pl.semaphore_wait(barrier, (E - 1) + (DP - 1) + E)

        def gather_send(copy):
            copy(me, sib, sib).start()
            for x in xpeers():
                copy(me, chip(x), chip(x)).start()

        def gather_relay(copy):
            for x in xpeers():
                copy(chip(x), sib, x * 2 + 1 - core).wait_recv()
                copy(chip(x), sib, x * 2 + 1 - core).start()

        def gather_take(copy):
            copy(sib, sib, sib).wait_recv()
            for x in xpeers():
                c = x * 2 + 1 - core
                copy(c, sib, c).wait_recv()

        def gather_sent(copy):
            copy(me, sib, sib).wait_send()
            for x in xpeers():
                copy(me, chip(x), chip(x)).wait_send()
                copy(chip(x), sib, x * 2 + 1 - core).wait_send()

        def q_of(a, kind):
            return lambda block, to, slot: q_copy(a, kind, block, to, slot)

        def kv_of(i):
            return lambda block, to, slot: kv_copy(i, block, to, slot)

        for kind in (0, 1):
            gather_send(q_of(0, kind))

        def norm_rows(x, gain, shift):
            return norm_stats(x)[0] * gain + shift

        def gain_of(which):
            if which == 1:
                return r.cg[...], r.cb[...]
            return r.ng[which // 2 : which // 2 + 1], r.nb[which // 2 : which // 2 + 1]

        def first_norm(i, _):
            g, b = gain_of(0)
            n = norm_rows(r.x[i].astype(F32), g, b).astype(BF16)
            r.n[i, 0] = n
            r.kv_s[i, pl.ds(row0, L)] = nn(n, r.wkv[...]).astype(BF16)
            gather_send(kv_of(i))
            return 0

        lax.fori_loop(0, NI, first_norm, 0)

        r.win_all[me] = r.win[...]
        r.wback_all[me] = r.wback[...]
        for kind in (0, 1):
            sib_copy(kind, me).start()
        for kind in (0, 1):
            for q in range(NP // 2):
                for x in xpeers():
                    wx_copy(kind, me, q, x, xi).start()

        @pl.when(dec)
        def _():
            for kind in (0, 1):
                gather_send(q_of(1, kind))

        def weights_over_x(kind, q):
            for x in xpeers():
                wx_copy(kind, chip(x), q, x, x).wait_recv()
                wz_copy(kind, x, q, half).start()
                wf_copy(kind, chip(x), x, 2 * q + half).start()

        def weights_over_z(kind, q):
            for x in xpeers():
                wz_copy(kind, x, q, 1 - half).wait_recv()
                wf_copy(kind, chip(x), x, 2 * q + 1 - half).start()

        def weights_over_sib(kind):
            for x in xpeers():
                for p in range(NP):
                    wf_copy(kind, x * 2 + 1 - core, x, p).wait_recv()

        def weights_sent():
            for kind in (0, 1):
                sib_copy(kind, me).wait_send()
                for x in xpeers():
                    for q in range(NP // 2):
                        wx_copy(kind, me, q, x, xi).wait_send()
                        wz_copy(kind, x, q, half).wait_send()
                    for p in range(NP):
                        wf_copy(kind, chip(x), x, p).wait_send()

        zeros_h = jnp.zeros((HD, L), BF16)

        def set_bias(i, a):
            own = r.pairs[sec, i, :, pl.ds(row0, L)].astype(F32)
            if a == 0:
                keys = r.pairs[sec, i].astype(F32)
            else:
                keys = r.pairs[0, i].astype(F32)
            kc = jnp.broadcast_to(keys, (128, SEQ)).T
            if L > 128:
                kc = jnp.concatenate([kc] * (L // 128), 1)
            same = kc == own
            if a == 0:
                qpos = row0 + lax.broadcasted_iota(jnp.int32, (1, L), 1)
                limit = jnp.where(dec, qpos, SEQ)
                same = same & (lax.broadcasted_iota(jnp.int32, (SEQ, L), 0) <= limit)
            r.bias[...] = jnp.where(same, 0.0, -1e30)

        def route_rows(i, a):
            ref = r.routes_s if a == 0 else r.routes_c
            return [ref[i, k : k + 1, pl.ds(row0, L)] for k in range(T)]

        def pick(rows, route, size):
            total = jnp.zeros((size, L), F32)
            for e in range(NE):
                total = jnp.where(route == e, rows[e * size : (e + 1) * size], total)
            return total

        def project_queries(i, a):
            n = r.n[i, a]
            ql = nt(r.wqr[a], n)
            routes = route_rows(i, a)
            chosen = []
            for k in range(T):
                r.qt[a, i, k] = (pick(ql[:NQ], routes[k], HD).astype(BF16).astype(F32) * scale).astype(BF16)
                chosen.append(pick(ql[NQ : NQ + NE], routes[k], 1))
            top = chosen[0]
            for k in range(1, T):
                top = jnp.maximum(top, chosen[k])
            ex = [jnp.exp(c - top) for c in chosen]
            total = ex[0]
            for k in range(1, T):
                total = total + ex[k]
            for k in range(T):
                r.gate[a, i, k] = jnp.broadcast_to(ex[k] / total, (8, L))

        def attend(i, a, kv_ref, base):
            kv = kv_ref[i]
            r.kvt[a, i] = kv.astype(F32).T.astype(BF16)

            def one(k, _):
                q = jnp.concatenate([r.qt[a, i, k], zeros_h], 0)
                s = nn(kv, q) + r.bias[...]
                m = jnp.max(s, 0, keepdims=True)
                ex = jnp.exp(s - m)
                p = (ex * (1.0 / jnp.sum(ex, 0, keepdims=True))).astype(BF16)
                r.p[a, i, k] = p
                r.heads[a, i, k] = nn(r.kvt[a, i, HD:], p)
                return 0

            lax.fori_loop(0, T, one, 0)
            routes = route_rows(i, a)
            gated = [
                r.heads[a, i, k].astype(BF16).astype(F32) * r.gate[a, i, k, 0:1] for k in range(T)
            ]
            for e in range(NE):
                block = jnp.zeros((HD, L), F32)
                for k in range(T):
                    block = jnp.where(routes[k] == e, gated[k], block)
                r.ht[a, i, e * HD : (e + 1) * HD] = block.astype(BF16)
            return base + tn(r.ht[a, i], r.wo_all[a])

        def attend_back(i, a, kv_ref, dx, send_ref):
            dxb = dx.astype(BF16)
            routes = route_rows(i, a)
            r.g_o[a] += nn(r.ht[a, i], dxb)
            gt = nt(r.wo_all[a], dxb)
            dgates = []
            for k in range(T):
                g = pick(gt, routes[k], HD)
                dgates.append(
                    jnp.sum(r.heads[a, i, k].astype(BF16).astype(F32) * g, 0, keepdims=True)
                )
                r.dq[k] = (g * r.gate[a, i, k, 0:1]).astype(BF16)
            gates = [r.gate[a, i, k, 0:1] for k in range(T)]
            mid = gates[0] * dgates[0]
            for k in range(1, T):
                mid = mid + gates[k] * dgates[k]
            dchosen = [gates[k] * (dgates[k] - mid) for k in range(T)]
            kv = kv_ref[i]
            r.dkv_acc[...] = jnp.zeros_like(r.dkv_acc)

            def one(k, _):
                dheads = r.dq[k]
                p = r.p[a, i, k]
                dv = jnp.concatenate([zeros_h, dheads], 0)
                dp = nn(kv, dv)
                pf = p.astype(F32)
                delta = jnp.sum(dp * pf, 0, keepdims=True)
                ds = (pf * (dp - delta)).astype(BF16)
                qk = jnp.concatenate([r.qt[a, i, k], zeros_h], 0)
                r.dkv_acc[...] += nt(ds, qk) + nt(p, dv)
                r.dq[k] = (nn(r.kvt[a, i, :HD], ds) * scale).astype(BF16)
                return 0

            lax.fori_loop(0, T, one, 0)
            send_ref[i] = r.dkv_acc[...].astype(BF16)
            blocks = []
            for e in range(NE):
                block = jnp.zeros((HD, L), F32)
                for k in range(T):
                    block = jnp.where(routes[k] == e, r.dq[k].astype(F32), block)
                blocks.append(block)
            logit_rows = jnp.zeros((RT, L), F32)
            rows = lax.broadcasted_iota(jnp.int32, (RT, L), 0)
            for k in range(T):
                logit_rows = jnp.where(rows == routes[k], dchosen[k], logit_rows)
            dql = jnp.concatenate(blocks + [logit_rows], 0).astype(BF16)
            r.g_qr[a] += nn(dql, r.n[i, a])
            return tn(dql, r.wqr[a])

        def chunk_at(s):
            return lax.rem(xi + s // 2, X) * 2 + jnp.where(lax.rem(s, 2) == 0, core, 1 - core)

        def chunk_out(s):
            return lax.rem(xi + s // 2 + 1, X) * 2 + jnp.where(lax.rem(s, 2) == 0, 1 - core, core)

        def ffn_forward(i, low, high):
            n = r.n[i, 2]

            def one(s, _):
                c = chunk_at(s)
                act, slope = gelu_parts(nn(n, r.win_all[c]))
                act = act.astype(BF16)
                r.act[i, c] = act
                r.dh[i, c] = slope.astype(BF16)
                r.acc[...] += nn(act, r.wback_all[c])
                return 0

            lax.fori_loop(low, high, one, 0)

        def ffn_middle(i):
            n = r.n[i, 2]
            dz = r.cot[i]
            r.acc[...] = jnp.zeros_like(r.acc)

            def one(c, _):
                act, slope = gelu_parts(nn(n, r.win_all[c]))
                r.act[i, c] = act.astype(BF16)
                dh = (nt(dz, r.wback_all[c]) * slope).astype(BF16)
                r.dh[i, c] = dh
                r.acc[...] += nt(dh, r.win_all[c])
                return 0

            lax.fori_loop(0, E, one, 0)
            return r.acc[...]

        def hand_out(i, s, c, kind):
            @pl.when((i == NI - 1) & (lax.rem(s, 2) == 0))
            def _():
                x = c // 2
                r.a_big[kind, x] = r.g_big[c, kind].astype(BF16)
                a_copy(kind, x).start()

        def ffn_back(i):
            dz = r.dz[i]
            dzt = dz.astype(F32).T.astype(BF16)
            nt_ = r.n[i, 2].astype(F32).T.astype(BF16)
            r.acc[...] = jnp.zeros_like(r.acc)

            def back(s, _):
                c = chunk_out(s)
                r.g_big[c, 1] += nn(dzt, r.act[i, c])
                hand_out(i, s, c, 1)
                return 0

            lax.fori_loop(0, E, back, 0)

            def inward(s, _):
                c = chunk_out(s)
                dh = (nt(dz, r.wback_all[c]) * r.dh[i, c].astype(F32)).astype(BF16)
                r.acc[...] += nt(dh, r.win_all[c])
                r.g_big[c, 0] += nn(nt_, dh)
                hand_out(i, s, c, 0)
                return 0

            lax.fori_loop(0, E, inward, 0)
            return r.acc[...]

        def ffn_weights(i):
            dzt = r.cot[i].astype(F32).T.astype(BF16)
            nt_ = r.n[i, 2].astype(F32).T.astype(BF16)
            r.acc[...] = r.x2[i]

            def one(s, _):
                c = chunk_out(s)
                act = r.act[i, c]
                r.g_big[c, 1] += nn(dzt, act)
                hand_out(i, s, c, 1)
                r.g_big[c, 0] += nn(nt_, r.dh[i, c])
                hand_out(i, s, c, 0)
                r.acc[...] += nn(act, r.wback_all[c])
                return 0

            lax.fori_loop(0, E, one, 0)
            r.o_layer[i] = r.acc[...].astype(BF16)

        def add_small(which, dgain, dshift):
            r.small[2 * which : 2 * which + 1] += dgain
            r.small[2 * which + 1 : 2 * which + 2] += dshift

        r.small[...] = jnp.zeros_like(r.small)
        r.g_qr[...] = jnp.zeros_like(r.g_qr)
        r.g_o[...] = jnp.zeros_like(r.g_o)
        r.g_kv[...] = jnp.zeros_like(r.g_kv)

        def zero_big(c, _):
            r.g_big[c] = jnp.zeros((2, D, HB), F32)
            return 0

        lax.fori_loop(0, E, zero_big, 0)

        for kind in (0, 1):
            gather_relay(q_of(0, kind))
        for kind in (0, 1):
            gather_take(q_of(0, kind))

        def forward(i, _):
            project_queries(i, 0)
            set_bias(i, 0)
            gather_relay(kv_of(i))
            gather_take(kv_of(i))
            x1 = attend(i, 0, r.kv_s, r.x[i].astype(F32))
            r.x1[i] = x1

            @pl.when(enc)
            def _():
                g, b = gain_of(2)
                r.n[i, 2] = norm_rows(r.x1[i], g, b).astype(BF16)

            @pl.when(dec)
            def _():
                g, b = gain_of(1)
                r.n[i, 1] = norm_rows(r.x1[i], g, b).astype(BF16)

            return 0

        lax.fori_loop(0, NI, forward, 0)

        @pl.when(enc)
        def _():
            r.acc[...] = r.x1[0]
            for kind in (0, 1):
                sib_copy(kind, sib).wait_recv()
            ffn_forward(0, 0, 2)

        for kind in (0, 1):
            for q in range(NP // 2):
                weights_over_x(kind, q)
        for kind in (0, 1):
            for q in range(NP // 2):
                weights_over_z(kind, q)
        for kind in (0, 1):
            weights_over_sib(kind)

        @pl.when(enc)
        def _():
            def encode(i, _):
                @pl.when(i == 0)
                def _():
                    ffn_forward(0, 2, E)

                @pl.when(i > 0)
                def _():
                    r.acc[...] = r.x1[i]
                    ffn_forward(i, 0, E)

                mem = r.acc[...].astype(BF16)
                r.o_layer[i] = mem
                r.ckv_own[i] = nn(mem, r.ckv[...]).astype(BF16)
                for j in range(E):
                    ckv_copy(i, me, j, me).start()
                return 0

            lax.fori_loop(0, NI, encode, 0)

        @pl.when(dec)
        def _():
            for kind in (0, 1):
                sib_copy(kind, sib).wait_recv()
            for kind in (0, 1):
                gather_relay(q_of(1, kind))
            for kind in (0, 1):
                gather_take(q_of(1, kind))

            def middle(i, _):
                project_queries(i, 1)
                set_bias(i, 1)
                for j in range(E):
                    ckv_copy(i, j, j, j).wait_recv()
                x2 = attend(i, 1, r.kv_c, r.x1[i])
                r.x2[i] = x2
                g, b = gain_of(2)
                r.n[i, 2] = norm_rows(x2, g, b).astype(BF16)
                dn = ffn_middle(i)
                dx, dg, db = norm_back(r.x2[i], g, dn)
                add_small(2, dg, db)
                r.o_ig[i] = r.cot[i].astype(F32) + dx
                dn = attend_back(i, 1, r.kv_c, r.o_ig[i], r.dckv_send)
                for j in range(E):
                    dckv_copy(i, j, me).start()
                g, b = gain_of(1)
                dx, dg, db = norm_back(r.x1[i], g, dn)
                add_small(1, dg, db)
                r.o_ig[i] += dx
                return 0

            lax.fori_loop(0, NI, middle, 0)

            def weights(i, _):
                ffn_weights(i)
                return 0

            lax.fori_loop(0, NI, weights, 0)

        def big_sib(kind):
            for o, x in enumerate(xpeers()):
                a_copy(kind, x).wait_recv()
                r.b_big[o, kind] = (
                    r.g_big[chip(x), kind] + r.a_big_r[kind, x].astype(F32)
                ).astype(BF16)
            a_copy(kind, xi).wait_recv()
            r.g_big[me, kind] += r.a_big_r[kind, xi].astype(F32)

        def dp_at(s):
            return lax.rem(dpi + s + 1, DP)

        def big_send(kind, low, high):
            for s in range(low, high):
                for o in range(X - 1):
                    b_copy(kind, o, dp_at(s)).start()

        def big_over_x(kind, s):
            d = dp_at(s)
            total = r.g_big[me, kind, block_rows(d)]
            for o in range(X - 1):
                b_copy(kind, o, d).wait_recv()
                total = total + r.b_big_r[o, kind, block_rows(d)].astype(F32)
            if s < DP - 1:
                r.c_big[s, kind] = total.astype(BF16)
                c_copy(kind, s).start()
            else:
                r.g_big[me, kind, block_rows(d)] = total

        def big_end(kind, out):
            total = r.g_big[me, kind, block_rows(dpi)]
            for o in range(DP - 1):
                c_copy(kind, o).wait_recv()
                total = total + r.c_big_r[o, kind].astype(F32)
            out[...] = total

        def qo_rows(a, c):
            at = pl.ds(pl.multiple_of(c * QB, QB), QB)
            return jnp.concatenate([r.g_qr[a, at], r.g_o[a, at]], 0)

        def qo_send(a):
            for x in range(X):
                r.a_qo[a, x] = qo_rows(a, x * 2 + (1 - core)).astype(BF16)
            aq_copy(a).start()

        def qo_sib(a):
            aq_copy(a).wait_recv()
            for o, x in enumerate(xpeers()):
                r.b_qo[a, o] = (qo_rows(a, chip(x)) + r.a_qo_r[a, x].astype(F32)).astype(BF16)
                bq_copy(a, o).start()

        def qo_over_x(a):
            total = qo_rows(a, me) + r.a_qo_r[a, xi].astype(F32)
            for o in range(X - 1):
                bq_copy(a, o).wait_recv()
                total = total + r.b_qo_r[a, o].astype(F32)
            r.own_qo[...] = total.T
            for o in range(DP - 1):
                r.c_qo[a, o] = r.own_qo[block_rows(dp_at(o))].astype(BF16)
                cq_copy(a, o).start()
            return r.own_qo[block_rows(dpi)]

        def qo_end(a, total):
            for o in range(DP - 1):
                cq_copy(a, o).wait_recv()
                total = total + r.c_qo_r[a, o].astype(F32)
            return total

        kv_busy = enc | (core == 0)
        kv_sib_busy = enc | (core == 1)

        def kv_send():
            @pl.when(kv_sib_busy)
            def _():
                ka_copy().start()

        def kv_sib():
            @pl.when(kv_busy)
            def _():
                ka_copy().wait_recv()
                total = r.g_kv[core] + r.kv_ar[...]
                r.kv_sum[...] = total
                r.kv_b[...] = total.astype(BF16)
                for o in range(X - 1):
                    kb_copy(o).start()

        def kv_over_x():
            @pl.when(kv_busy)
            def _():
                total = r.kv_sum[...]
                for o in range(X - 1):
                    kb_copy(o).wait_recv()
                    total = total + r.kv_br[o].astype(F32)
                r.kv_sum[...] = total
                for o in range(DP - 1):
                    r.kv_c2[o] = r.kv_sum[block_rows(dp_at(o))].astype(BF16)
                    kc_copy(o).start()

        def kv_over_dp():
            @pl.when(kv_busy)
            def _():
                total = r.kv_sum[block_rows(dpi)]
                for o in range(DP - 1):
                    kc_copy(o).wait_recv()
                    total = total + r.kv_cr[o].astype(F32)
                r.kv_fin[...] = total
                kf_copy().start()

            @pl.when(enc & (core == 1))
            def _():
                ks_copy(0).start()
                ks_copy(1).start()

        def kv_end():
            @pl.when(kv_sib_busy)
            def _():
                kf_copy().wait_recv()

            @pl.when(dec)
            def _():
                ks_copy(core).wait_recv()
                r.o_kv[0] = jnp.where(core == 0, r.kv_fin[...], r.kv_sib[...])
                r.o_kv[1] = r.kv_sec[...]

            @pl.when(enc)
            def _():
                r.o_kv[0] = jnp.where(core == 0, r.kv_fin[...], r.kv_sib[...])
                r.o_kv[1] = jnp.where(core == 0, r.kv_sib[...], r.kv_fin[...])

        def small_sib():
            sa_copy().wait_recv()
            r.sm_fin[...] = r.small[...] + r.sm_ar[...]
            r.sm_b[...] = r.sm_fin[...].astype(BF16)
            for o in range(X - 1):
                sb_copy(o).start()

        def small_over_x():
            total = r.sm_fin[...]
            for o in range(X - 1):
                sb_copy(o).wait_recv()
                total = total + r.sm_br[o].astype(F32)
            r.sm_fin[...] = total
            r.sm_c[...] = total.astype(BF16)
            for o in range(DP - 1):
                sc_copy(o).start()

        def small_over_dp():
            total = r.sm_fin[...]
            for o in range(DP - 1):
                sc_copy(o).wait_recv()
                total = total + r.sm_cr[o].astype(F32)
            r.sm_fin[...] = total

        def backward(i, _):
            @pl.when(enc)
            def _():
                total = jnp.zeros((L, 2 * HD), F32)
                for j in range(E):
                    dckv_copy(i, j, j).wait_recv()
                    total = total + r.dckv_recv[i, j].astype(F32)
                dkv = total.astype(BF16)
                dmem = nt(dkv, r.ckv[...]).astype(BF16).astype(F32)
                dx = r.cot[i].astype(F32) + dmem
                r.o_ig[i] = dx
                r.dz[i] = dx.astype(BF16)
                dn = ffn_back(i)
                r.g_kv[1] += tn(r.o_layer[i], dkv)
                g, b = gain_of(2)
                dx, dg, db = norm_back(r.x1[i], g, dn)
                add_small(2, dg, db)
                r.o_ig[i] += dx

            @pl.when(i == NI - 1)
            def _():
                big_sib(1)
                big_send(1, 0, DP // 2)

            r.acc[...] = attend_back(i, 0, r.kv_s, r.o_ig[i], r.dkv_send)
            for j in peers():
                dkv_copy(i, j, me).start()

            @pl.when(i == NI - 1)
            def _():
                big_send(1, DP // 2, DP)
                qo_send(0)
                big_sib(0)
                big_send(0, 0, DP // 2)

            total = r.dkv_send[i, pl.ds(row0, L)].astype(F32)
            for j in peers():
                dkv_copy(i, j, j).wait_recv()
                total = total + r.dkv_recv[i, j].astype(F32)
            dkv = total.astype(BF16)
            r.g_kv[0] += tn(r.n[i, 0], dkv)
            dn = r.acc[...] + nt(dkv, r.wkv[...])
            g, b = gain_of(0)
            dx, dg, db = norm_back(r.x[i].astype(F32), g, dn)
            add_small(0, dg, db)
            r.o_ig[i] += dx
            return 0

        lax.fori_loop(0, NI, backward, 0)

        for a in range(2):
            r.small[6 + a * NE : 6 + (a + 1) * NE] = r.g_qr[a, NQ : NQ + NE]
        sa_copy().start()
        kv_send()

        @pl.when(dec)
        def _():
            qo_send(1)

        qo_sib(0)
        small_sib()
        kv_sib()

        @pl.when(dec)
        def _():
            qo_sib(1)

        big_send(0, DP // 2, DP)
        for s in range(DP):
            big_over_x(1, s)
        small_over_x()
        kv_over_x()
        own_qo = qo_over_x(0)
        r.o_qo[0] = own_qo

        @pl.when(dec)
        def _():
            r.qo_fin[...] = qo_over_x(1)

        for s in range(DP):
            big_over_x(0, s)
        small_over_dp()
        kv_over_dp()
        r.o_qo[0] = qo_end(0, r.o_qo[0])

        @pl.when(dec)
        def _():
            sec_copy(1).start()
            r.qo_fin[...] = qo_end(1, r.qo_fin[...])
            sec_copy(0).start()
            r.o_qo[1] = r.qo_fin[...]
            r.o_small[...] = r.sm_fin[...]

        big_end(1, r.o_back)
        big_end(0, r.o_in)
        kv_end()

        @pl.when(enc)
        def _():
            sec_copy(1).wait_recv()
            sec_copy(0).wait_recv()
            r.o_qo[1] = r.qo_sec[...]
            rows = lax.broadcasted_iota(jnp.int32, (SR, D), 0)
            theirs = ((rows >= 2) & (rows < 4)) | ((rows >= 6 + NE) & (rows < 6 + 2 * NE))
            r.o_small[...] = jnp.where(theirs, r.sm_sec[...], r.sm_fin[...])

        for kind in (0, 1):
            gather_sent(q_of(0, kind))
            for x in range(X):
                a_copy(kind, x).wait_send()
            for o in range(X - 1):
                for d in range(DP):
                    b_copy(kind, o, d).wait_send()
            for o in range(DP - 1):
                c_copy(kind, o).wait_send()
        weights_sent()
        sa_copy().wait_send()
        for o in range(X - 1):
            sb_copy(o).wait_send()
        for o in range(DP - 1):
            sc_copy(o).wait_send()

        def qo_sent(a):
            aq_copy(a).wait_send()
            for o in range(X - 1):
                bq_copy(a, o).wait_send()
            for o in range(DP - 1):
                cq_copy(a, o).wait_send()

        qo_sent(0)

        @pl.when(dec)
        def _():
            for kind in (0, 1):
                gather_sent(q_of(1, kind))
                sec_copy(kind).wait_send()
            qo_sent(1)

        @pl.when(kv_sib_busy)
        def _():
            ka_copy().wait_send()

        @pl.when(kv_busy)
        def _():
            for o in range(X - 1):
                kb_copy(o).wait_send()
            for o in range(DP - 1):
                kc_copy(o).wait_send()
            kf_copy().wait_send()

        @pl.when(enc & (core == 1))
        def _():
            ks_copy(0).wait_send()
            ks_copy(1).wait_send()

        def sent(i, _):
            gather_sent(kv_of(i))
            for j in peers():
                dkv_copy(i, j, me).wait_send()

            @pl.when(enc)
            def _():
                for j in range(E):
                    ckv_copy(i, me, j, me).wait_send()

            @pl.when(dec)
            def _():
                for j in range(E):
                    dckv_copy(i, j, me).wait_send()

            return 0

        lax.fori_loop(0, NI, sent, 0)

    return kernel


def make_finish(E, NE, EB, QB):
    def kernel(
        layer, grads, w_in, w_back, qo, kv, small, o_layer, o_grads, o_gain, o_bias, o_kv, o_router,
        o_query, o_out, o_w_in, o_w_back, o_cgain, o_cbias, o_ckv, o_crouter, o_cquery, o_cout,
    ):
        me = lax.axis_index("expert")
        o_layer[...] = layer[...]
        o_grads[...] = grads[...]
        o_w_in[...] = w_in[...]
        o_w_back[...] = w_back[...].T
        for a, (q, o) in enumerate(((o_query, o_out), (o_cquery, o_cout))):
            both = qo[a].T
            q[...] = both[:QB]
            o[...] = both[QB:]
        for a, out in enumerate((o_kv, o_ckv)):
            total = kv[a, :EB]
            for j in range(1, E):
                total = jnp.where(me == j, kv[a, j * EB : (j + 1) * EB], total)
            out[...] = total
        off = (lax.axis_index("dp") * E + me) * EB
        part = small[:, pl.ds(pl.multiple_of(off // 128 * 128, 128), 128)]
        part = pltpu.roll(part, lax.rem(128 - lax.rem(off, 128), 128), 1)[:, :EB]
        o_gain[0] = jnp.concatenate([part[0:1], part[4:5]], 0)
        o_bias[0] = jnp.concatenate([part[1:2], part[5:6]], 0)
        o_cgain[...] = part[2:3]
        o_cbias[...] = part[3:4]
        o_router[...] = part[6 : 6 + NE]
        o_crouter[...] = part[6 + NE : 6 + 2 * NE]

    return kernel


def body(
    inputs, cotangents, pair_ids, self_routes, cross_routes, norm_gain, norm_bias, w_kv, w_router,
    w_query, w_out, w_in, w_back, cross_gain, cross_bias, cross_kv, cross_router, cross_query,
    cross_out,
):
    E = lax.axis_size("expert")
    DP = lax.axis_size("dp")
    _, MB, R, L, D = inputs.shape
    NI = MB * R
    SEQ = pair_ids.shape[-1]
    T = self_routes.shape[-1]
    NE = w_router.shape[-1]
    HD = w_query.shape[-1]
    HB = w_in.shape[-1]
    npd = NE // E
    QB = npd * HD
    dims = (NI, L, D, SEQ, T, NE, HD, HB, E, DP)
    ins, outs, bufs, sems = make_plan(dims)

    operands = [
        inputs.reshape(NI, L, D),
        cotangents.reshape(NI, L, D),
        pair_ids.reshape(2, NI, 1, SEQ),
        jnp.swapaxes(self_routes.reshape(NI, SEQ, T), 1, 2),
        jnp.swapaxes(cross_routes.reshape(NI, SEQ, T), 1, 2),
        norm_gain[0],
        norm_bias[0],
        w_kv[0],
        w_router[0].T,
        jnp.swapaxes(w_query[0], 1, 2),
        w_out[0],
        w_in[0],
        w_back[0],
        cross_gain[None],
        cross_bias[None],
        cross_kv,
        cross_router.T,
        jnp.swapaxes(cross_query, 1, 2),
        cross_out,
    ]
    vmem = pl.BlockSpec(memory_space=pltpu.VMEM)
    res = pl.pallas_call(
        make_kernel(dims),
        out_shape=[jax.ShapeDtypeStruct(s, t) for _, s, t in outs],
        in_specs=[vmem] * len(operands),
        out_specs=[vmem] * len(outs),
        scratch_shapes=[pltpu.VMEM(s, t) for _, s, t in bufs]
        + [pltpu.SemaphoreType.DMA(s) for _, s in sems],
        compiler_params=pltpu.CompilerParams(
            collective_id=0, has_side_effects=True, vmem_limit_bytes=62 * 1024 * 1024
        ),
        name="layers",
    )(*operands)
    DB = D // DP
    EB = DB // E
    shapes = [
        ((NI, L, D), BF16),
        ((NI, L, D), F32),
        ((1, 2, EB), F32),
        ((1, 2, EB), F32),
        ((EB, 2 * HD), F32),
        ((NE, EB), F32),
        ((QB, DB), F32),
        ((QB, DB), F32),
        ((DB, HB), F32),
        ((HB, DB), F32),
        ((1, EB), F32),
        ((1, EB), F32),
        ((EB, 2 * HD), F32),
        ((NE, EB), F32),
        ((QB, DB), F32),
        ((QB, DB), F32),
    ]
    (
        layer, grads, gain, bias, kv, router, query, out, w_in_g, w_back_g, c_gain, c_bias, c_kv,
        c_router, c_query, c_out,
    ) = pl.pallas_call(
        make_finish(E, NE, EB, QB),
        out_shape=[jax.ShapeDtypeStruct(s, t) for s, t in shapes],
        in_specs=[vmem] * len(outs),
        out_specs=[vmem] * len(shapes),
        name="results",
    )(*res)

    def of_query(g):
        return jnp.swapaxes(g.reshape(npd, HD, DB), 1, 2)

    def of_out(g):
        return g.reshape(npd, HD, DB)

    return (
        layer.reshape(inputs.shape),
        grads.reshape(inputs.shape),
        gain,
        bias,
        kv[None],
        router.T[None],
        of_query(query)[None],
        of_out(out)[None],
        w_in_g[None],
        w_back_g[None],
        c_gain[0],
        c_bias[0],
        c_kv,
        c_router.T,
        of_query(c_query),
        of_out(c_out),
    )


def solution(mesh):
    placed = (
        P("section", None, "dp", "expert", None),
        P("section", None, "dp", "expert", None),
        P(None, None, "dp", None),
        P("section", None, "dp", None, None),
        P(None, "dp", None, None),
        P("section", None, None),
        P("section", None, None),
        P("section", None, None),
        P("section", None, None),
        P("section", "expert", None, None),
        P("section", "expert", None, None),
        P("section", None, "expert"),
        P("section", "expert", None),
        P(),
        P(),
        P(),
        P(),
        P("expert", None, None),
        P("expert", None, None),
    )
    return jax.shard_map(
        body,
        mesh=mesh,
        in_specs=placed,
        out_specs=(
            P("section", None, "dp", "expert", None),
            P("section", None, "dp", "expert", None),
            P("section", None, ("dp", "expert")),
            P("section", None, ("dp", "expert")),
            P("section", ("dp", "expert"), None),
            P("section", ("dp", "expert"), None),
            P("section", "expert", "dp", None),
            P("section", "expert", None, "dp"),
            P("section", "dp", "expert"),
            P("section", "expert", "dp"),
            P(("dp", "expert")),
            P(("dp", "expert")),
            P(("dp", "expert"), None),
            P(("dp", "expert"), None),
            P("expert", "dp", None),
            P("expert", None, "dp"),
        ),
        check_vma=False,
    )
```

time: 179 us -> 136 us (0.76); the launches traced: 177 us -> 136 us
  Pallas kernels: 161 us -> 135 us
  local copies, waits for them, and re-layouts: 14.3 us -> 0 us
    pallas_call x1, Pallas kernels: 161 us -> 132 us  [body(): pl.pallas_call(make_kernel(dims), out_shape=[jax.ShapeDtypeStruct(s, t) f...]
    unnamed x28 -> x0, local copies, waits for them, and re-layouts: 6.17 us -> none
    pallas_call x0 -> x1, Pallas kernels: none -> 3.12 us  [body(): pl.pallas_call(make_finish(E, NE, EB, QB), out_shape=[jax.ShapeDtypeStruc...]
    squeeze x2 -> x0, local copies, waits for them, and re-layouts: 2.85 us -> none  [the longest x1 1.5 us: body(): small[3]]
    transpose x2 -> x0, local copies, waits for them, and re-layouts: 2.06 us -> none  [the longest x1 1.43 us: body(): small[6 + NE:6 + 2 * NE]]
    broadcast_in_dim x3 -> x0, local copies, waits for them, and re-layouts: 1.87 us -> none  [the longest x1 0.64 us: body(): qos[:, 1].transpose(1, 2, 0)[None]]
where the time goes in v2:
time: 136 us
  Pallas kernels  135 us (99%)
    pallas_call x1, Pallas kernels, body(): pl.pallas_call(make_kernel(dims), out_shape=[jax.ShapeDtypeStruct(s, t) f...  132 us
    pallas_call x1, Pallas kernels, body(): pl.pallas_call(make_finish(E, NE, EB, QB), out_shape=[jax.ShapeDtypeStruc...  3.12 us

profile of v2, /device:TPU:0, one launch (start us, length us, event | category | flops | bytes accessed | tf_op | source)
XLA Modules:
  0.0 136.2 jit_solution(12216768454090675647)
XLA Ops:
  0.7 132.3 %layers.1 = (bf16[2,256,512]{2,1,0:T(8,128)(2,1)}, f32[2,256,512]{2,1,0:T(8,128)}, f32[128,512]{1,0:T(8,128)}, f32[128,512]{1,0:T(8,128)}, f32[2,128,128]{2,1,0:...) custom-call(bf16[2,256,512]{2,1,0:T(8,128)(2,1)} %bitcast.49, bf16[2,256,512]{2,1,0:T(8,128)(2,1)} %bitcast.50, ...), custom_call_target="tpu_custom_call" | custom-call | tf_op jit(solution)/shard_map/layers/pallas_call | solution.py:1188
  132.9 3.1 %results.1 = (bf16[2,256,512]{2,1,0:T(8,128)(2,1)}, f32[2,256,512]{2,1,0:T(8,128)}, f32[1,2,32]{2,1,0:T(2,128)}, f32[1,2,32]{2,1,0:T(2,128)}, f32[32,128]{1,0:T(...) custom-call(bf16[2,256,512]{2,1,0:T(8,128)(2,1)} %get-tuple-element., ...), custom_call_target="tpu_custom_call" | custom-call | tf_op jit(solution)/shard_map/results/pallas_call | solution.py:1223

commit v3 on v2

v3 whole, which is shorter than its diff:
```python
from types import SimpleNamespace

import jax
import jax.numpy as jnp
from jax import lax
from jax.experimental import pallas as pl
from jax.experimental.pallas import tpu as pltpu
from jax.sharding import PartitionSpec as P

F32 = jnp.float32
BF16 = jnp.bfloat16
MESH = pl.DeviceIdType.MESH
RT = 16
SR = 32
NP = 8
NS = 3
NX = NP - NS


def nn(a, b):
    return lax.dot_general(a, b, (((1,), (0,)), ((), ())), preferred_element_type=F32)


def nt(a, b):
    return lax.dot_general(a, b, (((1,), (1,)), ((), ())), preferred_element_type=F32)


def tn(a, b):
    return lax.dot_general(a, b, (((0,), (0,)), ((), ())), preferred_element_type=F32)


def gelu_parts(h):
    c = 0.7978845608028654
    h2 = h * h
    t = jnp.tanh(c * h * (1.0 + 0.044715 * h2))
    half = 0.5 * (1.0 + t)
    slope = half + 0.5 * h * (1.0 - t * t) * (c * (1.0 + 3 * 0.044715 * h2))
    return h * half, slope


def norm_stats(x):
    centred = x - jnp.mean(x, -1, keepdims=True)
    r = lax.rsqrt(jnp.mean(centred * centred, -1, keepdims=True) + 1e-05)
    return centred * r, r


def norm_back(x, gain, grad):
    xhat, r = norm_stats(x)
    gg = grad * gain
    m1 = jnp.mean(gg, -1, keepdims=True)
    m2 = jnp.mean(gg * xhat, -1, keepdims=True)
    return (
        r * (gg - m1 - xhat * m2),
        jnp.sum(grad * xhat, 0, keepdims=True),
        jnp.sum(grad, 0, keepdims=True),
    )


INS = [
    "x", "cot", "pairs", "routes_s", "routes_c", "ng", "nb", "wkv", "wr", "wq", "wo", "win",
    "wback", "cg", "cb", "ckv", "cr", "cq", "co",
]
STAY = ("wr", "cr")
PLACED = ("win", "wback")


def fetched(ins):
    return [n for n in ins if n not in STAY + PLACED]


def make_plan(dims):
    (NI, L, D, SEQ, T, NE, HD, HB, E, DP) = dims
    npd = NE // E
    QB = npd * HD
    NQ = NE * HD
    X = E // 2
    DB = D // DP
    HP = DP // 2
    ins = INS
    outs = dict(
        out_layer=((NI, L, D), BF16),
        out_ig=((NI, L, D), F32),
        o_in=((DB, HB), F32),
        o_back=((DB, HB), F32),
        o_qo=((2, DB, 2 * QB), F32),
        o_kv=((2, DB, 2 * HD), F32),
        o_small=((SR, D), F32),
    )
    bufs = dict(
        o_layer=((NI, L, D), BF16),
        o_ig=((NI, L, D), F32),
        win_all=((E, D, HB), BF16),
        wback_all=((E, HB, D), BF16),
        wqr=((2, NQ + RT, D), BF16),
        wo_all=((2, NQ, D), BF16),
        wr_pad=((RT, D), F32),
        x1=((NI, L, D), F32),
        x2=((NI, L, D), F32),
        n=((NI, 3, L, D), BF16),
        dz=((NI, L, D), BF16),
        acc=((L, D), F32),
        dn=((NI, L, D), F32),
        act=((NI, E, L, HB), BF16),
        turned=((NI, D, L), BF16),
        dh=((NI, E, L, HB), BF16),
        kv_s=((NI, SEQ, 2 * HD), BF16),
        kv_c=((NI, SEQ, 2 * HD), BF16),
        kvt=((2, NI, 2 * HD, SEQ), BF16),
        bias=((SEQ, L), F32),
        qt=((2, NI, T, HD, L), BF16),
        gate=((2, NI, T, 8, L), F32),
        p=((2, NI, T, SEQ, L), BF16),
        heads=((2, NI, T, HD, L), F32),
        ht=((2, NI, NQ, L), BF16),
        dq=((T, HD, L), BF16),
        dkv_acc=((SEQ, 2 * HD), F32),
        dkv_own=((NI, L, 2 * HD), F32),
        dkv_send=((NI, SEQ, 2 * HD), BF16),
        dkv_recv=((NI, X, L, 2 * HD), BF16),
        dksum_r=((NI, X, L, 2 * HD), BF16),
        dckv_send=((NI, SEQ, 2 * HD), BF16),
        dckv_recv=((NI, X, L, 2 * HD), BF16),
        dsum_r=((NI, X, L, 2 * HD), BF16),
        ckv_own=((NI, L, 2 * HD), BF16),
        g_big=((E, 2, D, HB), F32),
        g_qr=((2, NQ + RT, D), F32),
        g_o=((2, NQ, D), F32),
        g_kv=((2, D, 2 * HD), F32),
        small=((SR, D), F32),
        a_big=((2, X, D, HB), BF16),
        a_big_r=((2, X, D, HB), BF16),
        a_qo=((2, X, 2 * QB, D), BF16),
        a_qo_r=((2, X, 2 * QB, D), BF16),
        b_big=((X - 1, 2, D, HB), BF16),
        b_big_r=((X - 1, 2, D, HB), BF16),
        za_big=((2, HP, DB, HB), BF16),
        za_big_r=((2, HP, DB, HB), BF16),
        zb_big=((2, HP - 1, DB, HB), BF16),
        zb_big_r=((2, HP - 1, DB, HB), BF16),
        own_qo=((2, X, D, 2 * QB), F32),
        za_qo=((2, HP, X, DB, 2 * QB), BF16),
        za_qo_r=((2, HP, X, DB, 2 * QB), BF16),
        zb_qo=((2, HP - 1, X, DB, 2 * QB), BF16),
        zb_qo_r=((2, HP - 1, X, DB, 2 * QB), BF16),
        b_qo=((2, X - 1, DB, 2 * QB), BF16),
        b_qo_r=((2, X - 1, DB, 2 * QB), BF16),
        qo_own=((2, DB, 2 * QB), F32),
        kv_ar=((D, 2 * HD), F32),
        kv_sum=((D, 2 * HD), F32),
        za_kv=((HP, DB, 2 * HD), BF16),
        za_kv_r=((HP, DB, 2 * HD), BF16),
        zb_kv=((HP - 1, DB, 2 * HD), BF16),
        zb_kv_r=((HP - 1, DB, 2 * HD), BF16),
        kv_b=((DB, 2 * HD), BF16),
        kv_br=((X - 1, DB, 2 * HD), BF16),
        kv_fin=((DB, 2 * HD), F32),
        kv_sib=((DB, 2 * HD), F32),
        kv_sec=((DB, 2 * HD), F32),
        sm_ar=((SR, D), F32),
        sm_b=((SR, D), BF16),
        sm_br=((X - 1, SR, D), BF16),
        za_sm=((SR, D), BF16),
        za_sm_r=((DP - 1, SR, D), BF16),
        sm_fin=((SR, D), F32),
        sm_sec=((SR, D), F32),
        qo_fin=((DB, 2 * QB), F32),
        qo_sec=((DB, 2 * QB), F32),
    )
    sems = dict(
        q_s=(2, 2, E), q_r=(2, 2, E),
        sib_s=(2,), sib_r=(2,),
        wx_s=(2, X, NX), wx_r=(2, X, NX),
        wz_s=(2, X, NS), wz_r=(2, X, NS),
        wf_s=(2, X, NP), wf_r=(2, X, NP),
        kv_ss=(NI, E), kv_rs=(NI, E),
        ckv_s=(NI, E), ckv_r=(NI, E),
        dckv_s=(NI, X), dckv_r=(NI, X),
        dsum_ss=(NI, X), dsum_rs=(NI, X),
        dkv_s=(NI, X), dkv_r=(NI, X),
        dksum_ss=(NI, X), dksum_rs=(NI, X),
        a_s=(2, X), a_r=(2, X),
        b_s=(X - 1, 2, DP), b_r=(X - 1, 2, DP),
        zab_s=(2, HP), zab_r=(2, HP),
        zbb_s=(2, HP), zbb_r=(2, HP),
        aq_s=(2,), aq_r=(2,),
        zaq_s=(2,), zaq_r=(2,),
        zbq_s=(2, HP), zbq_r=(2, HP),
        bq_s=(2, X - 1), bq_r=(2, X - 1),
        ka_s=(1,), ka_r=(1,),
        kb_s=(X - 1,), kb_r=(X - 1,),
        zak_s=(1,), zak_r=(1,),
        zbk_s=(HP,), zbk_r=(HP,),
        kf_s=(3,), kf_r=(2,),
        sa_s=(1,), sa_r=(1,),
        sb_s=(X - 1,), sb_r=(X - 1,),
        zs_s=(DP - 1,), zs_r=(DP - 1,),
        sec_s=(2,), sec_r=(2,),
        ld=(len(ins) + 2,),
    )
    return ins, outs, bufs, sems


def make_kernel(dims):
    (NI, L, D, SEQ, T, NE, HD, HB, E, DP) = dims
    npd = NE // E
    QB = npd * HD
    NQ = NE * HD
    X = E // 2
    DB = D // DP
    HP = DP // 2
    scale = HD ** -0.5
    ins, outs, bufs, sems = make_plan(dims)
    names = [n if n in STAY else "in_" + n for n in ins]
    names += list(outs) + list(bufs) + list(sems) + fetched(ins)

    def kernel(*refs):
        r = SimpleNamespace(**dict(zip(names, refs)))
        sec = lax.axis_index("section")
        dpi = lax.axis_index("dp")
        me = lax.axis_index("expert")
        core = lax.rem(me, 2)
        xi = me // 2
        sib = xi * 2 + (1 - core)
        dec = sec == 1
        enc = sec == 0
        other = 1 - sec
        half = lax.rem(dpi, 2)
        mate = dpi + 1 - 2 * half
        row0 = pl.multiple_of(me * L, L)

        def to_expert(j):
            return (sec, dpi, j)

        def to_dp(j):
            return (sec, j, me)

        def to_section(j):
            return (other, dpi, j)

        def rcopy(src, dst, ssem, rsem, dev):
            return pltpu.make_async_remote_copy(
                src_ref=src, dst_ref=dst, send_sem=ssem, recv_sem=rsem, device_id=dev,
                device_id_type=MESH,
            )

        def chip(x):
            return x * 2 + core

        def q_copy(a, kind, block, to, slot):
            ref = r.wqr if kind == 0 else r.wo_all
            ref = ref.at[a, pl.ds(pl.multiple_of(block * QB, QB), QB)]
            return rcopy(ref, ref, r.q_s.at[a, kind, slot], r.q_r.at[a, kind, block], to_expert(to))

        def w_ref(kind, c):
            return (r.win_all if kind == 0 else r.wback_all).at[c]

        def w_piece(kind, c, p):
            rows = (D if kind == 0 else HB) // NP
            return w_ref(kind, c).at[pl.ds(pl.multiple_of(p * rows, rows), rows)]

        def sib_copy(kind, c):
            ref = w_ref(kind, c)
            return rcopy(ref, ref, r.sib_s.at[kind], r.sib_r.at[kind], to_expert(sib))

        def shared(q, parity):
            return NS * parity + q

        def over_x_at(q):
            return shared(q, half) if q < NS else NS + q

        def wx_copy(kind, c, q, to_x, frm_x):
            ref = w_piece(kind, c, over_x_at(q))
            return rcopy(
                ref, ref, r.wx_s.at[kind, to_x, q], r.wx_r.at[kind, frm_x, q],
                to_expert(chip(to_x)),
            )

        def wz_copy(kind, x, q, parity):
            ref = w_piece(kind, chip(x), shared(q, parity))
            return rcopy(ref, ref, r.wz_s.at[kind, x, q], r.wz_r.at[kind, x, q], to_dp(mate))

        def wf_copy(kind, c, x, p):
            ref = w_piece(kind, c, p)
            return rcopy(ref, ref, r.wf_s.at[kind, x, p], r.wf_r.at[kind, x, p], to_expert(sib))

        def rows_of(ref, i, j):
            return ref.at[i, pl.ds(pl.multiple_of(j * L, L), L)]

        def kv_copy(i, block, to, slot):
            ref = rows_of(r.kv_s, i, block)
            return rcopy(ref, ref, r.kv_ss.at[i, slot], r.kv_rs.at[i, block], to_expert(to))

        def ckv_copy(i, to):
            return rcopy(
                r.ckv_own.at[i], rows_of(r.kv_c, i, me), r.ckv_s.at[i, to], r.ckv_r.at[i, me],
                to_section(to),
            )

        def ckv_relay(i, block):
            ref = rows_of(r.kv_c, i, block)
            return rcopy(ref, ref, r.ckv_s.at[i, block], r.ckv_r.at[i, block], to_expert(sib))

        def ckv_gather(i):
            same = xpeers() + [xi]
            for x in same:
                ckv_relay(i, chip(x)).wait_recv()
                ckv_relay(i, chip(x)).start()
            for x in same:
                ckv_relay(i, x * 2 + 1 - core).wait_recv()

        def dsum_copy(i, x):
            at = x * 2 + 1 - core
            return rcopy(
                rows_of(r.dckv_send, i, at), r.dsum_r.at[i, x], r.dsum_ss.at[i, x],
                r.dsum_rs.at[i, x], to_expert(sib),
            )

        def dckv_copy(i, to_x, frm_x):
            return rcopy(
                rows_of(r.dckv_send, i, chip(to_x)), r.dckv_recv.at[i, frm_x],
                r.dckv_s.at[i, to_x], r.dckv_r.at[i, frm_x], to_section(chip(to_x)),
            )

        def dckv_out(i):
            order = xpeers() + [xi]
            for x in order:
                dsum_copy(i, x).start()
            for x in order:
                dsum_copy(i, x).wait_recv()
                at = pl.ds(pl.multiple_of(chip(x) * L, L), L)
                r.dckv_send[i, at] = (
                    r.dkv_acc[at] + r.dsum_r[i, x].astype(F32)
                ).astype(BF16)
                dckv_copy(i, x, xi).start()

        def dksum_copy(i, x):
            at = x * 2 + 1 - core
            return rcopy(
                rows_of(r.dkv_send, i, at), r.dksum_r.at[i, x], r.dksum_ss.at[i, x],
                r.dksum_rs.at[i, x], to_expert(sib),
            )

        def dkv_copy(i, to_x, frm_x):
            return rcopy(
                rows_of(r.dkv_send, i, chip(to_x)), r.dkv_recv.at[i, frm_x], r.dkv_s.at[i, to_x],
                r.dkv_r.at[i, frm_x], to_expert(chip(to_x)),
            )

        def dkv_out(i):
            for x in xpeers() + [xi]:
                dksum_copy(i, x).start()
            r.dkv_own[i] = r.dkv_acc[pl.ds(row0, L)]
            for x in xpeers():
                dksum_copy(i, x).wait_recv()
                at = pl.ds(pl.multiple_of(chip(x) * L, L), L)
                r.dkv_send[i, at] = (r.dkv_acc[at] + r.dksum_r[i, x].astype(F32)).astype(BF16)
                dkv_copy(i, x, xi).start()

        def dkv_in(i):
            dksum_copy(i, xi).wait_recv()
            total = r.dkv_own[i] + r.dksum_r[i, xi].astype(F32)
            for x in xpeers():
                dkv_copy(i, x, x).wait_recv()
                total = total + r.dkv_recv[i, x].astype(F32)
            return total

        def over_x(src, dst, ssem, rsem, o):
            return rcopy(src, dst, ssem, rsem, to_expert(chip(lax.rem(xi + o + 1, X))))

        def to_mate(src, dst, ssem, rsem):
            return rcopy(src, dst, ssem, rsem, to_dp(mate))

        def mates_at(k):
            return lax.rem(dpi // 2 + k, HP) * 2 + 1 - half

        def mine_at(k):
            return lax.rem(dpi // 2 + k, HP) * 2 + half

        def over_dp(src, dst, ssem, rsem, k):
            return rcopy(src, dst, ssem, rsem, to_dp(mine_at(k)))

        def over_sib(src, dst, ssem, rsem):
            return rcopy(src, dst, ssem, rsem, to_expert(sib))

        def a_copy(kind, x):
            return over_sib(
                r.a_big.at[kind, x], r.a_big_r.at[kind, x], r.a_s.at[kind, x], r.a_r.at[kind, x]
            )

        def block_rows(d):
            return pl.ds(pl.multiple_of(d * DB, DB), DB)

        def b_copy(kind, o, d):
            return over_x(
                r.b_big.at[o, kind, block_rows(d)], r.b_big_r.at[o, kind, block_rows(d)],
                r.b_s.at[o, kind, d], r.b_r.at[o, kind, d], o,
            )

        def zab_copy(kind, k):
            return to_mate(
                r.za_big.at[kind, k], r.za_big_r.at[kind, k], r.zab_s.at[kind, k],
                r.zab_r.at[kind, k],
            )

        def zbb_copy(kind, k):
            return over_dp(
                r.zb_big.at[kind, k - 1], r.zb_big_r.at[kind, k - 1], r.zbb_s.at[kind, k],
                r.zbb_r.at[kind, k], k,
            )

        def aq_copy(a):
            return over_sib(r.a_qo.at[a], r.a_qo_r.at[a], r.aq_s.at[a], r.aq_r.at[a])

        def zaq_copy(a):
            return to_mate(r.za_qo.at[a], r.za_qo_r.at[a], r.zaq_s.at[a], r.zaq_r.at[a])

        def zbq_copy(a, k):
            return over_dp(
                r.zb_qo.at[a, k - 1], r.zb_qo_r.at[a, k - 1], r.zbq_s.at[a, k], r.zbq_r.at[a, k], k
            )

        def bq_copy(a, o):
            return over_x(
                r.b_qo.at[a, o], r.b_qo_r.at[a, o], r.bq_s.at[a, o], r.bq_r.at[a, o], o
            )

        def ka_copy():
            return over_sib(r.g_kv.at[1 - core], r.kv_ar, r.ka_s.at[0], r.ka_r.at[0])

        def kb_copy(o):
            return over_x(r.kv_b, r.kv_br.at[o], r.kb_s.at[o], r.kb_r.at[o], o)

        def zak_copy():
            return to_mate(r.za_kv, r.za_kv_r, r.zak_s.at[0], r.zak_r.at[0])

        def zbk_copy(k):
            return over_dp(r.zb_kv.at[k - 1], r.zb_kv_r.at[k - 1], r.zbk_s.at[k], r.zbk_r.at[k], k)

        def kf_copy():
            return over_sib(r.kv_fin, r.kv_sib, r.kf_s.at[0], r.kf_r.at[0])

        def ks_copy(to_core):
            return rcopy(
                r.kv_fin, r.kv_sec, r.kf_s.at[1 + to_core], r.kf_r.at[1],
                to_section(xi * 2 + to_core),
            )

        def sa_copy():
            return over_sib(r.small, r.sm_ar, r.sa_s.at[0], r.sa_r.at[0])

        def sb_copy(o):
            return over_x(r.sm_b, r.sm_br.at[o], r.sb_s.at[o], r.sb_r.at[o], o)

        def zs_copy(o):
            return rcopy(
                r.za_sm, r.za_sm_r.at[o], r.zs_s.at[o], r.zs_r.at[o],
                to_dp(lax.rem(dpi + o + 1, DP)),
            )

        def sec_copy(kind):
            src, dst = ((r.qo_fin, r.qo_sec), (r.sm_fin, r.sm_sec))[kind]
            return rcopy(src, dst, r.sec_s.at[kind], r.sec_r.at[kind], to_section(me))

        def peers():
            return [lax.rem(me + o, E) for o in range(1, E)]

        def xpeers():
            return [lax.rem(xi + o, X) for o in range(1, X)]

        def dpeers():
            return [lax.rem(dpi + o, DP) for o in range(1, DP)]

        def load(name):
            src = getattr(r, "in_" + name)
            if name in PLACED:
                dst = w_ref(PLACED.index(name), me)
            else:
                dst = getattr(r, name)
            return pltpu.make_async_copy(src, dst, r.ld.at[ins.index(name)])

        def store(name):
            k = ("layer", "ig").index(name)
            src, dst = getattr(r, "o_" + name), getattr(r, "out_" + name)
            return pltpu.make_async_copy(src, dst, r.ld.at[len(ins) + k])

        soon = ["x", "ng", "nb", "wkv", "wq", "wo"]
        early = soon + ["win", "wback", "pairs", "routes_s"]
        late = [n for n in ins if n not in early and n not in STAY]
        for name in early + late:
            load(name).start()
        barrier = pltpu.get_barrier_semaphore()
        for j in peers():
            pl.semaphore_signal(barrier, inc=1, device_id=to_expert(j), device_id_type=MESH)
        for j in dpeers():
            pl.semaphore_signal(barrier, inc=1, device_id=to_dp(j), device_id_type=MESH)
        for j in range(E):
            pl.semaphore_signal(barrier, inc=1, device_id=to_section(j), device_id_type=MESH)

        def gather_send(copy):
            copy(me, sib, sib).start()
            for x in xpeers():
                copy(me, chip(x), chip(x)).start()

        def gather_relay(copy):
            for x in xpeers():
                copy(chip(x), sib, x * 2 + 1 - core).wait_recv()
                copy(chip(x), sib, x * 2 + 1 - core).start()

        def gather_take(copy):
            copy(sib, sib, sib).wait_recv()
            for x in xpeers():
                c = x * 2 + 1 - core
                copy(c, sib, c).wait_recv()

        def gather_sent(copy):
            copy(me, sib, sib).wait_send()
            for x in xpeers():
                copy(me, chip(x), chip(x)).wait_send()
                copy(chip(x), sib, x * 2 + 1 - core).wait_send()

        def q_of(a, kind):
            return lambda block, to, slot: q_copy(a, kind, block, to, slot)

        def kv_of(i):
            return lambda block, to, slot: kv_copy(i, block, to, slot)

        def norm_rows(x, gain, shift):
            return norm_stats(x)[0] * gain + shift

        def gain_of(which):
            if which == 1:
                return r.cg[...], r.cb[...]
            return r.ng[which // 2 : which // 2 + 1], r.nb[which // 2 : which // 2 + 1]

        def own_query_weights(a, q_ref, o_ref, wr_ref):
            for j in range(npd):
                at = pl.multiple_of(me * QB + j * HD, HD)
                r.wqr[a, pl.ds(at, HD)] = q_ref[j]
                r.wo_all[a, pl.ds(at, HD)] = o_ref[j]
            r.wr_pad[...] = jnp.zeros_like(r.wr_pad)
            r.wr_pad[:NE] = wr_ref[...].astype(F32)
            r.wqr[a, pl.ds(NQ, RT)] = r.wr_pad[...].astype(BF16)

        def first_norm(i):
            g, b = gain_of(0)
            n = norm_rows(r.x[i].astype(F32), g, b).astype(BF16)
            r.n[i, 0] = n
            r.kv_s[i, pl.ds(row0, L)] = nn(n, r.wkv[...]).astype(BF16)

        for name in soon:
            load(name).wait()
        own_query_weights(0, r.wq, r.wo, r.wr)
        first_norm(0)
        pl.semaphore_wait(barrier, (E - 1) + (DP - 1) + E)

        gather_send(q_of(0, 0))
        gather_send(kv_of(0))
        gather_send(q_of(0, 1))
        for name in PLACED:
            load(name).wait()
        for kind in (0, 1):
            sib_copy(kind, me).start()
        for part in (range(NS), range(NS, NX)):
            for kind in (0, 1):
                for q in part:
                    for x in xpeers():
                        wx_copy(kind, me, q, x, xi).start()

        def later_norms(i, _):
            first_norm(i)
            gather_send(kv_of(i))
            return 0

        lax.fori_loop(1, NI, later_norms, 0)
        for name in late + ["pairs", "routes_s"]:
            load(name).wait()
        own_query_weights(1, r.cq, r.co, r.cr)

        @pl.when(dec)
        def _():
            for kind in (0, 1):
                gather_send(q_of(1, kind))

        def weights_over_x(kind, q):
            for x in xpeers():
                wx_copy(kind, chip(x), q, x, x).wait_recv()
                if q < NS:
                    wz_copy(kind, x, q, half).start()
                wf_copy(kind, chip(x), x, over_x_at(q)).start()

        def weights_over_z(kind, q):
            for x in xpeers():
                wz_copy(kind, x, q, 1 - half).wait_recv()
                wf_copy(kind, chip(x), x, shared(q, 1 - half)).start()

        def weights_over_sib(kind):
            for x in xpeers():
                for p in range(NP):
                    wf_copy(kind, x * 2 + 1 - core, x, p).wait_recv()

        def weights_sent():
            for kind in (0, 1):
                sib_copy(kind, me).wait_send()
                for x in xpeers():
                    for q in range(NX):
                        wx_copy(kind, me, q, x, xi).wait_send()
                    for q in range(NS):
                        wz_copy(kind, x, q, half).wait_send()
                    for p in range(NP):
                        wf_copy(kind, chip(x), x, p).wait_send()

        zeros_h = jnp.zeros((HD, L), BF16)

        def set_bias(i, a):
            own = r.pairs[sec, i, :, pl.ds(row0, L)].astype(F32)
            if a == 0:
                keys = r.pairs[sec, i].astype(F32)
            else:
                keys = r.pairs[0, i].astype(F32)
            kc = jnp.broadcast_to(keys, (128, SEQ)).T
            if L > 128:
                kc = jnp.concatenate([kc] * (L // 128), 1)
            same = kc == own
            if a == 0:
                qpos = row0 + lax.broadcasted_iota(jnp.int32, (1, L), 1)
                limit = jnp.where(dec, qpos, SEQ)
                same = same & (lax.broadcasted_iota(jnp.int32, (SEQ, L), 0) <= limit)
            r.bias[...] = jnp.where(same, 0.0, -1e30)

        def route_rows(i, a):
            ref = r.routes_s if a == 0 else r.routes_c
            return [ref[i, k : k + 1, pl.ds(row0, L)] for k in range(T)]

        def pick(rows, route, size):
            total = jnp.zeros((size, L), F32)
            for e in range(NE):
                total = jnp.where(route == e, rows[e * size : (e + 1) * size], total)
            return total

        def project_queries(i, a):
            n = r.n[i, a]
            ql = nt(r.wqr[a], n)
            routes = route_rows(i, a)
            chosen = []
            for k in range(T):
                r.qt[a, i, k] = (pick(ql[:NQ], routes[k], HD).astype(BF16).astype(F32) * scale).astype(BF16)
                chosen.append(pick(ql[NQ : NQ + NE], routes[k], 1))
            top = chosen[0]
            for k in range(1, T):
                top = jnp.maximum(top, chosen[k])
            ex = [jnp.exp(c - top) for c in chosen]
            total = ex[0]
            for k in range(1, T):
                total = total + ex[k]
            for k in range(T):
                r.gate[a, i, k] = jnp.broadcast_to(ex[k] / total, (8, L))

        def attend(i, a, kv_ref, base):
            kv = kv_ref[i]
            r.kvt[a, i] = kv.astype(F32).T.astype(BF16)

            def one(k, _):
                q = jnp.concatenate([r.qt[a, i, k], zeros_h], 0)
                s = nn(kv, q) + r.bias[...]
                m = jnp.max(s, 0, keepdims=True)
                ex = jnp.exp(s - m)
                p = (ex * (1.0 / jnp.sum(ex, 0, keepdims=True))).astype(BF16)
                r.p[a, i, k] = p
                r.heads[a, i, k] = nn(r.kvt[a, i, HD:], p)
                return 0

            lax.fori_loop(0, T, one, 0, unroll=True)
            routes = route_rows(i, a)
            gated = [
                r.heads[a, i, k].astype(BF16).astype(F32) * r.gate[a, i, k, 0:1] for k in range(T)
            ]
            for e in range(NE):
                block = jnp.zeros((HD, L), F32)
                for k in range(T):
                    block = jnp.where(routes[k] == e, gated[k], block)
                r.ht[a, i, e * HD : (e + 1) * HD] = block.astype(BF16)
            return base + tn(r.ht[a, i], r.wo_all[a])

        def attend_back(i, a, kv_ref, dx, send_ref):
            dxb = dx.astype(BF16)
            routes = route_rows(i, a)
            r.g_o[a] += nn(r.ht[a, i], dxb)
            gt = nt(r.wo_all[a], dxb)
            dgates = []
            for k in range(T):
                g = pick(gt, routes[k], HD)
                dgates.append(
                    jnp.sum(r.heads[a, i, k].astype(BF16).astype(F32) * g, 0, keepdims=True)
                )
                r.dq[k] = (g * r.gate[a, i, k, 0:1]).astype(BF16)
            gates = [r.gate[a, i, k, 0:1] for k in range(T)]
            mid = gates[0] * dgates[0]
            for k in range(1, T):
                mid = mid + gates[k] * dgates[k]
            dchosen = [gates[k] * (dgates[k] - mid) for k in range(T)]
            kv = kv_ref[i]
            r.dkv_acc[...] = jnp.zeros_like(r.dkv_acc)

            def one(k, _):
                dheads = r.dq[k]
                p = r.p[a, i, k]
                dv = jnp.concatenate([zeros_h, dheads], 0)
                dp = nn(kv, dv)
                pf = p.astype(F32)
                delta = jnp.sum(dp * pf, 0, keepdims=True)
                ds = (pf * (dp - delta)).astype(BF16)
                qk = jnp.concatenate([r.qt[a, i, k], zeros_h], 0)
                r.dkv_acc[...] += nt(ds, qk) + nt(p, dv)
                r.dq[k] = (nn(r.kvt[a, i, :HD], ds) * scale).astype(BF16)
                return 0

            lax.fori_loop(0, T, one, 0, unroll=True)
            send_ref[i] = r.dkv_acc[...].astype(BF16)
            blocks = []
            for e in range(NE):
                block = jnp.zeros((HD, L), F32)
                for k in range(T):
                    block = jnp.where(routes[k] == e, r.dq[k].astype(F32), block)
                blocks.append(block)
            logit_rows = jnp.zeros((RT, L), F32)
            rows = lax.broadcasted_iota(jnp.int32, (RT, L), 0)
            for k in range(T):
                logit_rows = jnp.where(rows == routes[k], dchosen[k], logit_rows)
            dql = jnp.concatenate(blocks + [logit_rows], 0).astype(BF16)
            r.g_qr[a] += nn(dql, r.n[i, a])
            return tn(dql, r.wqr[a])

        def chunk_at(s):
            return lax.rem(xi + s // 2, X) * 2 + jnp.where(lax.rem(s, 2) == 0, core, 1 - core)

        def chunk_out(s):
            return lax.rem(xi + s // 2 + 1, X) * 2 + jnp.where(lax.rem(s, 2) == 0, 1 - core, core)

        def ffn_forward(i, low, high):
            n = r.n[i, 2]

            def one(s, _):
                c = chunk_at(s)
                act, slope = gelu_parts(nn(n, r.win_all[c]))
                act = act.astype(BF16)
                r.act[i, c] = act
                r.dh[i, c] = slope.astype(BF16)
                r.acc[...] += nn(act, r.wback_all[c])
                return 0

            lax.fori_loop(low, high, one, 0, unroll=True)

        def ffn_middle(i):
            n = r.n[i, 2]
            r.acc[...] = jnp.zeros_like(r.acc)

            def one(c, _):
                act, slope = gelu_parts(nn(n, r.win_all[c]))
                r.act[i, c] = act.astype(BF16)
                dh = (r.dh[i, c].astype(F32) * slope).astype(BF16)
                r.dh[i, c] = dh
                r.acc[...] += nt(dh, r.win_all[c])
                return 0

            lax.fori_loop(0, E, one, 0, unroll=True)
            return r.acc[...]

        def big_sib(kind):
            for o, x in enumerate(xpeers()):
                a_copy(kind, x).wait_recv()
                r.b_big[o, kind] = (
                    r.g_big[chip(x), kind] + r.a_big_r[kind, x].astype(F32)
                ).astype(BF16)

        def big_sib_own(kind):
            a_copy(kind, xi).wait_recv()
            r.g_big[me, kind] += r.a_big_r[kind, xi].astype(F32)

        def dp_at(s):
            return mates_at(s) if s < HP else mine_at((s - HP + 1) % HP)

        def big_send(kind, low, high):
            for s in range(low, high):
                for o in range(X - 1):
                    b_copy(kind, o, dp_at(s)).start()

        def big_over_x(kind, s):
            d = dp_at(s)
            total = r.g_big[me, kind, block_rows(d)]
            for o in range(X - 1):
                b_copy(kind, o, d).wait_recv()
                total = total + r.b_big_r[o, kind, block_rows(d)].astype(F32)
            if s < HP:
                r.za_big[kind, s] = total.astype(BF16)
                zab_copy(kind, s).start()
                return
            k = (s - HP + 1) % HP
            zab_copy(kind, k).wait_recv()
            total = total + r.za_big_r[kind, k].astype(F32)
            if k > 0:
                r.zb_big[kind, k - 1] = total.astype(BF16)
                zbb_copy(kind, k).start()
            else:
                r.g_big[me, kind, block_rows(d)] = total

        def big_end(kind, out):
            total = r.g_big[me, kind, block_rows(dpi)]
            for k in range(1, HP):
                zbb_copy(kind, k).wait_recv()
                total = total + r.zb_big_r[kind, k - 1].astype(F32)
            out[...] = total

        def hand_out(i, s, c, kind):
            @pl.when(jnp.logical_and(i == NI - 1, lax.rem(s, 2) == 0))
            def _():
                x = c // 2
                r.a_big[kind, x] = r.g_big[c, kind].astype(BF16)
                a_copy(kind, x).start()

        def ffn_back(i):
            dz = r.dz[i]
            dzt = dz.astype(F32).T.astype(BF16)
            nt_ = r.n[i, 2].astype(F32).T.astype(BF16)
            r.acc[...] = jnp.zeros_like(r.acc)

            def back(s, _):
                c = chunk_out(s)
                r.g_big[c, 1] += nn(dzt, r.act[i, c])
                hand_out(i, s, c, 1)
                return 0

            lax.fori_loop(0, E, back, 0, unroll=True)

            @pl.when(i == NI - 1)
            def _():
                big_sib(1)
                big_send(1, 0, HP)

            def inward(s, _):
                c = chunk_out(s)
                dh = (nt(dz, r.wback_all[c]) * r.dh[i, c].astype(F32)).astype(BF16)
                r.acc[...] += nt(dh, r.win_all[c])
                r.g_big[c, 0] += nn(nt_, dh)
                hand_out(i, s, c, 0)
                return 0

            lax.fori_loop(0, E, inward, 0, unroll=True)
            return r.acc[...]

        def ffn_weights(kind):
            for i in range(NI):
                r.turned[i] = (r.cot[i] if kind == 1 else r.n[i, 2]).astype(F32).T.astype(BF16)

            def one(s, _):
                c = chunk_out(s)
                total = jnp.zeros((D, HB), F32)
                for i in range(NI):
                    total += nn(r.turned[i], (r.act if kind == 1 else r.dh)[i, c])
                r.g_big[c, kind] = total
                hand_out(NI - 1, s, c, kind)
                return 0

            lax.fori_loop(0, E, one, 0)

        def ffn_output(i):
            r.acc[...] = r.x2[i]

            def one(c, _):
                r.acc[...] += nn(r.act[i, c], r.wback_all[c])
                return 0

            lax.fori_loop(0, E, one, 0, unroll=True)
            r.o_layer[i] = r.acc[...].astype(BF16)

        def add_small(which, dgain, dshift):
            r.small[2 * which : 2 * which + 1] += dgain
            r.small[2 * which + 1 : 2 * which + 2] += dshift

        def qo_rows(a, c):
            at = pl.ds(pl.multiple_of(c * QB, QB), QB)
            return jnp.concatenate([r.g_qr[a, at], r.g_o[a, at]], 0)

        def qo_send(a):
            for x in range(X):
                r.a_qo[a, x] = qo_rows(a, x * 2 + (1 - core)).astype(BF16)
            aq_copy(a).start()

        def qo_sib(a):
            aq_copy(a).wait_recv()
            for x in range(X):
                total = qo_rows(a, chip(x)) + r.a_qo_r[a, x].astype(F32)
                r.own_qo[a, x] = total.T
            for k in range(HP):
                r.za_qo[a, k] = r.own_qo[a, :, block_rows(mates_at(k))].astype(BF16)
            zaq_copy(a).start()

        def qo_mate(a):
            zaq_copy(a).wait_recv()
            for k in range(HP):
                total = r.own_qo[a, :, block_rows(mine_at(k))] + r.za_qo_r[a, k].astype(F32)
                if k > 0:
                    r.zb_qo[a, k - 1] = total.astype(BF16)
                    zbq_copy(a, k).start()
                else:
                    r.own_qo[a, :, block_rows(dpi)] = total

        def qo_over_dp(a):
            total = r.own_qo[a, :, block_rows(dpi)]
            for k in range(1, HP):
                zbq_copy(a, k).wait_recv()
                total = total + r.zb_qo_r[a, k - 1].astype(F32)
            r.own_qo[a, :, block_rows(dpi)] = total
            for o, x in enumerate(xpeers()):
                r.b_qo[a, o] = r.own_qo[a, x, block_rows(dpi)].astype(BF16)
                bq_copy(a, o).start()

        def qo_end(a):
            total = r.own_qo[a, xi, block_rows(dpi)]
            for o in range(X - 1):
                bq_copy(a, o).wait_recv()
                total = total + r.b_qo_r[a, o].astype(F32)
            return total

        kv_busy = enc | (core == 0)
        kv_sib_busy = enc | (core == 1)

        def kv_send():
            @pl.when(kv_sib_busy)
            def _():
                ka_copy().start()

        def kv_sib():
            @pl.when(kv_busy)
            def _():
                ka_copy().wait_recv()
                r.kv_sum[...] = r.g_kv[core] + r.kv_ar[...]
                for k in range(HP):
                    r.za_kv[k] = r.kv_sum[block_rows(mates_at(k))].astype(BF16)
                zak_copy().start()

        def kv_mate():
            @pl.when(kv_busy)
            def _():
                zak_copy().wait_recv()
                for k in range(HP):
                    total = r.kv_sum[block_rows(mine_at(k))] + r.za_kv_r[k].astype(F32)
                    if k > 0:
                        r.zb_kv[k - 1] = total.astype(BF16)
                        zbk_copy(k).start()
                    else:
                        r.kv_fin[...] = total

        def kv_over_dp():
            @pl.when(kv_busy)
            def _():
                total = r.kv_fin[...]
                for k in range(1, HP):
                    zbk_copy(k).wait_recv()
                    total = total + r.zb_kv_r[k - 1].astype(F32)
                r.kv_fin[...] = total
                r.kv_b[...] = total.astype(BF16)
                for o in range(X - 1):
                    kb_copy(o).start()

        def kv_over_x():
            @pl.when(kv_busy)
            def _():
                total = r.kv_fin[...]
                for o in range(X - 1):
                    kb_copy(o).wait_recv()
                    total = total + r.kv_br[o].astype(F32)
                r.kv_fin[...] = total
                kf_copy().start()

            @pl.when(enc & (core == 1))
            def _():
                ks_copy(0).start()
                ks_copy(1).start()

        def kv_end():
            @pl.when(kv_sib_busy)
            def _():
                kf_copy().wait_recv()

            @pl.when(dec)
            def _():
                ks_copy(core).wait_recv()
                r.o_kv[0] = jnp.where(core == 0, r.kv_fin[...], r.kv_sib[...])
                r.o_kv[1] = r.kv_sec[...]

            @pl.when(enc)
            def _():
                r.o_kv[0] = jnp.where(core == 0, r.kv_fin[...], r.kv_sib[...])
                r.o_kv[1] = jnp.where(core == 0, r.kv_sib[...], r.kv_fin[...])

        def small_sib():
            sa_copy().wait_recv()
            r.sm_fin[...] = r.small[...] + r.sm_ar[...]
            r.sm_b[...] = r.sm_fin[...].astype(BF16)
            for o in range(X - 1):
                sb_copy(o).start()

        def small_over_x():
            total = r.sm_fin[...]
            for o in range(X - 1):
                sb_copy(o).wait_recv()
                total = total + r.sm_br[o].astype(F32)
            r.sm_fin[...] = total
            r.za_sm[...] = total.astype(BF16)
            for o in range(DP - 1):
                zs_copy(o).start()

        def small_over_dp():
            total = r.sm_fin[...]
            for o in range(DP - 1):
                zs_copy(o).wait_recv()
                total = total + r.za_sm_r[o].astype(F32)
            r.sm_fin[...] = total

        def self_forward(i):
            x1 = attend(i, 0, r.kv_s, r.x[i].astype(F32))
            r.x1[i] = x1

            @pl.when(enc)
            def _():
                g, b = gain_of(2)
                r.n[i, 2] = norm_rows(r.x1[i], g, b).astype(BF16)

            @pl.when(dec)
            def _():
                g, b = gain_of(1)
                r.n[i, 1] = norm_rows(r.x1[i], g, b).astype(BF16)

        def encoded(i):
            mem = r.acc[...].astype(BF16)
            r.o_layer[i] = mem
            r.ckv_own[i] = nn(mem, r.ckv[...]).astype(BF16)
            for x in xpeers():
                ckv_copy(i, chip(x)).start()
            ckv_copy(i, me).start()

        gather_relay(q_of(0, 0))
        gather_take(q_of(0, 0))
        project_queries(0, 0)
        set_bias(0, 0)
        gather_relay(kv_of(0))
        gather_relay(q_of(0, 1))
        gather_take(kv_of(0))
        gather_take(q_of(0, 1))
        self_forward(0)
        for q in range(NS):
            weights_over_x(0, q)
        for kind in (0, 1):
            sib_copy(kind, sib).wait_recv()

        @pl.when(enc)
        def _():
            r.acc[...] = r.x1[0]
            ffn_forward(0, 0, 2)

        for q in range(NS):
            weights_over_x(1, q)
            weights_over_z(0, q)
        for q in range(NS, NX):
            weights_over_x(0, q)
        for q in range(NS):
            weights_over_z(1, q)
        for q in range(NS, NX):
            weights_over_x(1, q)
        @pl.when(enc)
        def _():
            ffn_forward(0, 2, 3)

        for kind in (0, 1):
            weights_over_sib(kind)

        @pl.when(enc)
        def _():
            ffn_forward(0, 3, E)
            encoded(0)

        def later_rows(i, _):
            project_queries(i, 0)
            set_bias(i, 0)
            gather_relay(kv_of(i))
            gather_take(kv_of(i))
            self_forward(i)

            @pl.when(enc)
            def _():
                r.acc[...] = r.x1[i]
                ffn_forward(i, 0, E)
                encoded(i)

            return 0

        lax.fori_loop(1, NI, later_rows, 0)

        @pl.when(enc)
        def _():
            store("layer").start()

        r.small[...] = jnp.zeros_like(r.small)
        r.g_qr[...] = jnp.zeros_like(r.g_qr)
        r.g_o[...] = jnp.zeros_like(r.g_o)
        r.g_kv[...] = jnp.zeros_like(r.g_kv)

        def zero_big(c, _):
            r.g_big[c] = jnp.zeros((2, D, HB), F32)
            return 0

        lax.fori_loop(0, E, zero_big, 0)

        @pl.when(dec)
        def _():
            for kind in (0, 1):
                gather_relay(q_of(1, kind))
            for kind in (0, 1):
                gather_take(q_of(1, kind))

            def ahead(i, _):
                project_queries(i, 1)
                dz = r.cot[i]

                def one(c, _):
                    r.dh[i, c] = nt(dz, r.wback_all[c]).astype(BF16)
                    return 0

                lax.fori_loop(0, E, one, 0)
                return 0

            lax.fori_loop(0, NI, ahead, 0)

            def middle(i, _):
                set_bias(i, 1)
                ckv_gather(i)
                x2 = attend(i, 1, r.kv_c, r.x1[i])
                r.x2[i] = x2
                g, b = gain_of(2)
                r.n[i, 2] = norm_rows(x2, g, b).astype(BF16)
                dn = ffn_middle(i)
                dx, dg, db = norm_back(r.x2[i], g, dn)
                add_small(2, dg, db)
                r.o_ig[i] = r.cot[i].astype(F32) + dx
                dn = attend_back(i, 1, r.kv_c, r.o_ig[i], r.dckv_send)
                dckv_out(i)
                g, b = gain_of(1)
                dx, dg, db = norm_back(r.x1[i], g, dn)
                add_small(1, dg, db)
                r.o_ig[i] += dx
                return 0

            lax.fori_loop(0, NI, middle, 0)

            qo_send(1)

        def backward(i, _):
            @pl.when(enc)
            def _():
                total = jnp.zeros((L, 2 * HD), F32)
                for x in range(X):
                    dckv_copy(i, x, x).wait_recv()
                    total = total + r.dckv_recv[i, x].astype(F32)
                dkv = total.astype(BF16)
                dmem = nt(dkv, r.ckv[...]).astype(BF16).astype(F32)
                dx = r.cot[i].astype(F32) + dmem
                r.o_ig[i] = dx
                r.dz[i] = dx.astype(BF16)
                dn = ffn_back(i)
                r.g_kv[1] += tn(r.o_layer[i], dkv)
                g, b = gain_of(2)
                dx, dg, db = norm_back(r.x1[i], g, dn)
                add_small(2, dg, db)
                r.o_ig[i] += dx

            first = i == 0
            last = i == NI - 1

            @pl.when(dec & first)
            def _():
                ffn_weights(1)

            r.dn[i] = attend_back(i, 0, r.kv_s, r.o_ig[i], r.dkv_send)

            @pl.when(dec & first)
            def _():
                big_sib(1)
                qo_sib(1)
                big_send(1, 0, HP)

            dkv_out(i)

            @pl.when(dec & first)
            def _():
                ffn_weights(0)
                big_send(1, HP, DP)
                big_sib(0)

            @pl.when(enc & last)
            def _():
                big_send(1, HP, DP)
                big_sib(0)

            @pl.when(dec & last)
            def _():
                big_send(0, 0, HP)

            @pl.when(last)
            def _():
                qo_send(0)

            return 0

        lax.fori_loop(0, NI, backward, 0)
        for kind in (1, 0):
            big_sib_own(kind)
        for s in range(HP):
            big_over_x(1, s)

        @pl.when(dec)
        def _():
            qo_mate(1)
            for s in range(HP, DP - 1):
                big_over_x(1, s)

        def first_layer(i, _):
            dkv = dkv_in(i).astype(BF16)
            r.g_kv[0] += tn(r.n[i, 0], dkv)
            dn = r.dn[i] + nt(dkv, r.wkv[...])
            g, b = gain_of(0)
            dx, dg, db = norm_back(r.x[i].astype(F32), g, dn)
            add_small(0, dg, db)
            r.o_ig[i] += dx
            return 0

        lax.fori_loop(0, NI, first_layer, 0)
        store("ig").start()

        for a in range(2):
            r.small[6 + a * NE : 6 + (a + 1) * NE] = r.g_qr[a, NQ : NQ + NE]
        sa_copy().start()
        kv_send()

        qo_sib(0)
        small_sib()
        kv_sib()

        @pl.when(enc)
        def _():
            big_send(0, 0, DP)
            for s in range(HP, DP - 1):
                big_over_x(1, s)

        @pl.when(dec)
        def _():
            big_send(0, HP, DP)

            def output(i, _):
                ffn_output(i)
                return 0

            lax.fori_loop(0, NI, output, 0)
            store("layer").start()

        small_over_x()
        big_over_x(1, DP - 1)
        for s in range(HP):
            big_over_x(0, s)
        kv_mate()
        qo_mate(0)

        @pl.when(dec)
        def _():
            qo_over_dp(1)

        for s in range(HP, DP - 1):
            big_over_x(0, s)
        small_over_dp()

        @pl.when(dec)
        def _():
            sec_copy(1).start()
            r.qo_fin[...] = qo_end(1)
            sec_copy(0).start()
            r.o_qo[1] = r.qo_fin[...]
            r.o_small[...] = r.sm_fin[...]

        kv_over_dp()
        qo_over_dp(0)
        big_over_x(0, DP - 1)
        kv_over_x()
        r.o_qo[0] = qo_end(0)
        big_end(1, r.o_back)
        big_end(0, r.o_in)
        kv_end()

        @pl.when(enc)
        def _():
            sec_copy(1).wait_recv()
            sec_copy(0).wait_recv()
            r.o_qo[1] = r.qo_sec[...]
            rows = lax.broadcasted_iota(jnp.int32, (SR, D), 0)
            theirs = ((rows >= 2) & (rows < 4)) | ((rows >= 6 + NE) & (rows < 6 + 2 * NE))
            r.o_small[...] = jnp.where(theirs, r.sm_sec[...], r.sm_fin[...])

        store("layer").wait()
        store("ig").wait()
        for kind in (0, 1):
            gather_sent(q_of(0, kind))
            for x in range(X):
                a_copy(kind, x).wait_send()
            for o in range(X - 1):
                for d in range(DP):
                    b_copy(kind, o, d).wait_send()
            for k in range(HP):
                zab_copy(kind, k).wait_send()
            for k in range(1, HP):
                zbb_copy(kind, k).wait_send()
        weights_sent()
        sa_copy().wait_send()
        for o in range(X - 1):
            sb_copy(o).wait_send()
        for o in range(DP - 1):
            zs_copy(o).wait_send()

        def qo_sent(a):
            aq_copy(a).wait_send()
            for o in range(X - 1):
                bq_copy(a, o).wait_send()
            zaq_copy(a).wait_send()
            for k in range(1, HP):
                zbq_copy(a, k).wait_send()

        qo_sent(0)

        @pl.when(dec)
        def _():
            for kind in (0, 1):
                gather_sent(q_of(1, kind))
                sec_copy(kind).wait_send()
            qo_sent(1)

        @pl.when(kv_sib_busy)
        def _():
            ka_copy().wait_send()

        @pl.when(kv_busy)
        def _():
            for o in range(X - 1):
                kb_copy(o).wait_send()
            zak_copy().wait_send()
            for k in range(1, HP):
                zbk_copy(k).wait_send()
            kf_copy().wait_send()

        @pl.when(enc & (core == 1))
        def _():
            ks_copy(0).wait_send()
            ks_copy(1).wait_send()

        def sent(i, _):
            gather_sent(kv_of(i))
            for x in xpeers():
                dkv_copy(i, x, xi).wait_send()
            for x in range(X):
                dksum_copy(i, x).wait_send()

            @pl.when(enc)
            def _():
                for x in range(X):
                    ckv_copy(i, chip(x)).wait_send()

            @pl.when(dec)
            def _():
                for x in range(X):
                    ckv_relay(i, chip(x)).wait_send()
                    dsum_copy(i, x).wait_send()
                    dckv_copy(i, x, xi).wait_send()

            return 0

        lax.fori_loop(0, NI, sent, 0)

    return kernel


def make_finish(E, NE, EB, QB):
    def kernel(
        layer, grads, w_in, w_back, qo, kv, small, o_layer, o_grads, o_gain, o_bias, o_kv, o_router,
        o_query, o_out, o_w_in, o_w_back, o_cgain, o_cbias, o_ckv, o_crouter, o_cquery, o_cout,
    ):
        me = lax.axis_index("expert")
        o_layer[...] = layer[...]
        o_grads[...] = grads[...]
        o_w_in[...] = w_in[...]
        o_w_back[...] = w_back[...].T
        for a, (q, o) in enumerate(((o_query, o_out), (o_cquery, o_cout))):
            both = qo[a].T
            q[...] = both[:QB]
            o[...] = both[QB:]
        for a, out in enumerate((o_kv, o_ckv)):
            total = kv[a, :EB]
            for j in range(1, E):
                total = jnp.where(me == j, kv[a, j * EB : (j + 1) * EB], total)
            out[...] = total
        off = (lax.axis_index("dp") * E + me) * EB
        part = small[:, pl.ds(pl.multiple_of(off // 128 * 128, 128), 128)]
        part = pltpu.roll(part, lax.rem(128 - lax.rem(off, 128), 128), 1)[:, :EB]
        o_gain[0] = jnp.concatenate([part[0:1], part[4:5]], 0)
        o_bias[0] = jnp.concatenate([part[1:2], part[5:6]], 0)
        o_cgain[...] = part[2:3]
        o_cbias[...] = part[3:4]
        o_router[...] = part[6 : 6 + NE]
        o_crouter[...] = part[6 + NE : 6 + 2 * NE]

    return kernel


def body(
    inputs, cotangents, pair_ids, self_routes, cross_routes, norm_gain, norm_bias, w_kv, w_router,
    w_query, w_out, w_in, w_back, cross_gain, cross_bias, cross_kv, cross_router, cross_query,
    cross_out,
):
    E = lax.axis_size("expert")
    DP = lax.axis_size("dp")
    _, MB, R, L, D = inputs.shape
    NI = MB * R
    SEQ = pair_ids.shape[-1]
    T = self_routes.shape[-1]
    NE = w_router.shape[-1]
    HD = w_query.shape[-1]
    HB = w_in.shape[-1]
    npd = NE // E
    QB = npd * HD
    dims = (NI, L, D, SEQ, T, NE, HD, HB, E, DP)
    ins, outs, bufs, sems = make_plan(dims)

    operands = [
        inputs.reshape(NI, L, D),
        cotangents.reshape(NI, L, D),
        pair_ids.reshape(2, NI, 1, SEQ),
        jnp.swapaxes(self_routes.reshape(NI, SEQ, T), 1, 2),
        jnp.swapaxes(cross_routes.reshape(NI, SEQ, T), 1, 2),
        norm_gain[0],
        norm_bias[0],
        w_kv[0],
        w_router[0].T,
        jnp.swapaxes(w_query[0], 1, 2),
        w_out[0],
        w_in[0],
        w_back[0],
        cross_gain[None],
        cross_bias[None],
        cross_kv,
        cross_router.T,
        jnp.swapaxes(cross_query, 1, 2),
        cross_out,
    ]
    vmem = pl.BlockSpec(memory_space=pltpu.VMEM)
    anywhere = pl.BlockSpec(memory_space=pl.ANY)
    res = pl.pallas_call(
        make_kernel(dims),
        out_shape=[jax.ShapeDtypeStruct(s, t) for s, t in outs.values()],
        in_specs=[vmem if n in STAY else anywhere for n in ins],
        out_specs=[anywhere if n[:4] == "out_" else vmem for n in outs],
        scratch_shapes=[pltpu.VMEM(s, t) for s, t in bufs.values()]
        + [pltpu.SemaphoreType.DMA(s) for s in sems.values()]
        + [pltpu.VMEM(o.shape, o.dtype) for n, o in zip(ins, operands) if n in fetched(ins)],
        compiler_params=pltpu.CompilerParams(
            collective_id=0, has_side_effects=True, vmem_limit_bytes=62 * 1024 * 1024
        ),
        name="layers",
    )(*operands)
    DB = D // DP
    EB = DB // E
    shapes = [
        ((NI, L, D), BF16),
        ((NI, L, D), F32),
        ((1, 2, EB), F32),
        ((1, 2, EB), F32),
        ((EB, 2 * HD), F32),
        ((NE, EB), F32),
        ((QB, DB), F32),
        ((QB, DB), F32),
        ((DB, HB), F32),
        ((HB, DB), F32),
        ((1, EB), F32),
        ((1, EB), F32),
        ((EB, 2 * HD), F32),
        ((NE, EB), F32),
        ((QB, DB), F32),
        ((QB, DB), F32),
    ]
    (
        layer, grads, gain, bias, kv, router, query, out, w_in_g, w_back_g, c_gain, c_bias, c_kv,
        c_router, c_query, c_out,
    ) = pl.pallas_call(
        make_finish(E, NE, EB, QB),
        out_shape=[jax.ShapeDtypeStruct(s, t) for s, t in shapes],
        in_specs=[vmem] * len(outs),
        out_specs=[vmem] * len(shapes),
        name="results",
    )(*res)

    def of_query(g):
        return jnp.swapaxes(g.reshape(npd, HD, DB), 1, 2)

    def of_out(g):
        return g.reshape(npd, HD, DB)

    return (
        layer.reshape(inputs.shape),
        grads.reshape(inputs.shape),
        gain,
        bias,
        kv[None],
        router.T[None],
        of_query(query)[None],
        of_out(out)[None],
        w_in_g[None],
        w_back_g[None],
        c_gain[0],
        c_bias[0],
        c_kv,
        c_router.T,
        of_query(c_query),
        of_out(c_out),
    )


def solution(mesh):
    placed = (
        P("section", None, "dp", "expert", None),
        P("section", None, "dp", "expert", None),
        P(None, None, "dp", None),
        P("section", None, "dp", None, None),
        P(None, "dp", None, None),
        P("section", None, None),
        P("section", None, None),
        P("section", None, None),
        P("section", None, None),
        P("section", "expert", None, None),
        P("section", "expert", None, None),
        P("section", None, "expert"),
        P("section", "expert", None),
        P(),
        P(),
        P(),
        P(),
        P("expert", None, None),
        P("expert", None, None),
    )
    return jax.shard_map(
        body,
        mesh=mesh,
        in_specs=placed,
        out_specs=(
            P("section", None, "dp", "expert", None),
            P("section", None, "dp", "expert", None),
            P("section", None, ("dp", "expert")),
            P("section", None, ("dp", "expert")),
            P("section", ("dp", "expert"), None),
            P("section", ("dp", "expert"), None),
            P("section", "expert", "dp", None),
            P("section", "expert", None, "dp"),
            P("section", "dp", "expert"),
            P("section", "expert", "dp"),
            P(("dp", "expert")),
            P(("dp", "expert")),
            P(("dp", "expert"), None),
            P(("dp", "expert"), None),
            P("expert", "dp", None),
            P("expert", None, "dp"),
        ),
        check_vma=False,
    )
```

time: 136 us -> 109 us (0.80)
  Pallas kernels: 135 us -> 108 us
    pallas_call x1, Pallas kernels: 132 us -> 105 us  [body(): pl.pallas_call(make_kernel(dims), out_shape=[jax.ShapeDtypeStruct(s, t) f...]
where the time goes in v3:
time: 109 us
  Pallas kernels  108 us (99%)
    pallas_call x1, Pallas kernels, body(): pl.pallas_call(make_kernel(dims), out_shape=[jax.ShapeDtypeStruct(s, t) f...  105 us
    pallas_call x1, Pallas kernels, body(): pl.pallas_call(make_finish(E, NE, EB, QB), out_shape=[jax.ShapeDtypeStruc...  3.12 us

profile of v3, /device:TPU:0, one launch (start us, length us, event | category | flops | bytes accessed | tf_op | source)
XLA Modules:
  0.0 109.2 jit_solution(8208798445801146231)
XLA Ops:
  0.7 105.3 %layers.1 = (bf16[2,256,512]{2,1,0:T(8,128)(2,1)}, f32[2,256,512]{2,1,0:T(8,128)}, f32[128,512]{1,0:T(8,128)}, f32[128,512]{1,0:T(8,128)}, f32[2,128,128]{2,1,0:...) custom-call(bf16[2,256,512]{2,1,0:T(8,128)(2,1)} %bitcast.49, bf16[2,256,512]{2,1,0:T(8,128)(2,1)} %bitcast.50, ...), custom_call_target="tpu_custom_call" | custom-call | tf_op jit(solution)/shard_map/layers/pallas_call | solution.py:1461
  105.9 3.1 %results.1 = (bf16[2,256,512]{2,1,0:T(8,128)(2,1)}, f32[2,256,512]{2,1,0:T(8,128)}, f32[1,2,32]{2,1,0:T(2,128)}, f32[1,2,32]{2,1,0:T(2,128)}, f32[32,128]{1,0:T(...) custom-call(bf16[2,256,512]{2,1,0:T(8,128)(2,1)} %get-tuple-element., ...), custom_call_target="tpu_custom_call" | custom-call | tf_op jit(solution)/shard_map/results/pallas_call | solution.py:1497

commit v4 on v3

--- a/solution.py
+++ b/solution.py
@@ -15,6 +15,7 @@
 NP = 8
 NS = 3
 NX = NP - NS
+NH = 2
 
 
 def nn(a, b):
@@ -31,11 +32,11 @@
 
 def gelu_parts(h):
     c = 0.7978845608028654
-    h2 = h * h
-    t = jnp.tanh(c * h * (1.0 + 0.044715 * h2))
-    half = 0.5 * (1.0 + t)
-    slope = half + 0.5 * h * (1.0 - t * t) * (c * (1.0 + 3 * 0.044715 * h2))
-    return h * half, slope
+    a = c + (c * 0.044715) * (h * h)
+    t = jnp.tanh(h * a)
+    half = 0.5 + 0.5 * t
+    act = h * half
+    return act, half + act * ((1.0 - t) * (3.0 * a - 2.0 * c))
 
 
 def norm_stats(x):
@@ -84,7 +85,7 @@
         o_back=((DB, HB), F32),
         o_qo=((2, DB, 2 * QB), F32),
         o_kv=((2, DB, 2 * HD), F32),
-        o_small=((SR, D), F32),
+        o_small=((SR, 128), F32),
     )
     bufs = dict(
         o_layer=((NI, L, D), BF16),
@@ -109,6 +110,7 @@
         bias=((SEQ, L), F32),
         qt=((2, NI, T, HD, L), BF16),
         gate=((2, NI, T, 8, L), F32),
+        inv=((2, NI, T, 8, L), F32),
         p=((2, NI, T, SEQ, L), BF16),
         heads=((2, NI, T, HD, L), F32),
         ht=((2, NI, NQ, L), BF16),
@@ -137,20 +139,16 @@
         za_big_r=((2, HP, DB, HB), BF16),
         zb_big=((2, HP - 1, DB, HB), BF16),
         zb_big_r=((2, HP - 1, DB, HB), BF16),
-        own_qo=((2, X, D, 2 * QB), F32),
-        za_qo=((2, HP, X, DB, 2 * QB), BF16),
-        za_qo_r=((2, HP, X, DB, 2 * QB), BF16),
-        zb_qo=((2, HP - 1, X, DB, 2 * QB), BF16),
-        zb_qo_r=((2, HP - 1, X, DB, 2 * QB), BF16),
-        b_qo=((2, X - 1, DB, 2 * QB), BF16),
-        b_qo_r=((2, X - 1, DB, 2 * QB), BF16),
+        b_qo=((2, X - 1, 2 * QB, D), BF16),
+        b_qo_r=((2, X - 1, 2 * QB, D), BF16),
+        own_qo=((D, 2 * QB), F32),
+        c_qo=((2, DP - 1, DB, 2 * QB), BF16),
+        c_qo_r=((2, DP - 1, DB, 2 * QB), BF16),
         qo_own=((2, DB, 2 * QB), F32),
         kv_ar=((D, 2 * HD), F32),
         kv_sum=((D, 2 * HD), F32),
-        za_kv=((HP, DB, 2 * HD), BF16),
-        za_kv_r=((HP, DB, 2 * HD), BF16),
-        zb_kv=((HP - 1, DB, 2 * HD), BF16),
-        zb_kv_r=((HP - 1, DB, 2 * HD), BF16),
+        c_kv=((DP - 1, DB, 2 * HD), BF16),
+        c_kv_r=((DP - 1, DB, 2 * HD), BF16),
         kv_b=((DB, 2 * HD), BF16),
         kv_br=((X - 1, DB, 2 * HD), BF16),
         kv_fin=((DB, 2 * HD), F32),
@@ -160,9 +158,10 @@
         sm_b=((SR, D), BF16),
         sm_br=((X - 1, SR, D), BF16),
         za_sm=((SR, D), BF16),
-        za_sm_r=((DP - 1, SR, D), BF16),
+        za_sm_r=((DP - 1, SR, 128), BF16),
+        sm_own=((SR, 128), F32),
         sm_fin=((SR, D), F32),
-        sm_sec=((SR, D), F32),
+        sm_sec=((SR, 128), F32),
         qo_fin=((DB, 2 * QB), F32),
         qo_sec=((DB, 2 * QB), F32),
     )
@@ -179,17 +178,15 @@
         dkv_s=(NI, X), dkv_r=(NI, X),
         dksum_ss=(NI, X), dksum_rs=(NI, X),
         a_s=(2, X), a_r=(2, X),
-        b_s=(X - 1, 2, DP), b_r=(X - 1, 2, DP),
-        zab_s=(2, HP), zab_r=(2, HP),
-        zbb_s=(2, HP), zbb_r=(2, HP),
+        b_s=(X - 1, 2, DP, NH), b_r=(X - 1, 2, DP, NH),
+        zab_s=(2, HP, NH), zab_r=(2, HP, NH),
+        zbb_s=(2, HP, NH), zbb_r=(2, HP, NH),
         aq_s=(2,), aq_r=(2,),
-        zaq_s=(2,), zaq_r=(2,),
-        zbq_s=(2, HP), zbq_r=(2, HP),
+        cq_s=(2, DP - 1), cq_r=(2, DP - 1),
         bq_s=(2, X - 1), bq_r=(2, X - 1),
         ka_s=(1,), ka_r=(1,),
         kb_s=(X - 1,), kb_r=(X - 1,),
-        zak_s=(1,), zak_r=(1,),
-        zbk_s=(HP,), zbk_r=(HP,),
+        ck_s=(DP - 1,), ck_r=(DP - 1,),
         kf_s=(3,), kf_r=(2,),
         sa_s=(1,), sa_r=(1,),
         sb_s=(X - 1,), sb_r=(X - 1,),
@@ -390,33 +387,41 @@
         def block_rows(d):
             return pl.ds(pl.multiple_of(d * DB, DB), DB)
 
-        def b_copy(kind, o, d):
+        HB_ROWS = DB // NH
+
+        def part_rows(d, h):
+            return pl.ds(pl.multiple_of(d * DB + h * HB_ROWS, HB_ROWS), HB_ROWS)
+
+        def sub_rows(h):
+            return pl.ds(h * HB_ROWS, HB_ROWS)
+
+        def b_copy(kind, o, d, h):
             return over_x(
-                r.b_big.at[o, kind, block_rows(d)], r.b_big_r.at[o, kind, block_rows(d)],
-                r.b_s.at[o, kind, d], r.b_r.at[o, kind, d], o,
+                r.b_big.at[o, kind, part_rows(d, h)], r.b_big_r.at[o, kind, part_rows(d, h)],
+                r.b_s.at[o, kind, d, h], r.b_r.at[o, kind, d, h], o,
             )
 
-        def zab_copy(kind, k):
+        def zab_copy(kind, k, h):
             return to_mate(
-                r.za_big.at[kind, k], r.za_big_r.at[kind, k], r.zab_s.at[kind, k],
-                r.zab_r.at[kind, k],
+                r.za_big.at[kind, k, sub_rows(h)], r.za_big_r.at[kind, k, sub_rows(h)],
+                r.zab_s.at[kind, k, h], r.zab_r.at[kind, k, h],
             )
 
-        def zbb_copy(kind, k):
+        def zbb_copy(kind, k, h):
             return over_dp(
-                r.zb_big.at[kind, k - 1], r.zb_big_r.at[kind, k - 1], r.zbb_s.at[kind, k],
-                r.zbb_r.at[kind, k], k,
+                r.zb_big.at[kind, k - 1, sub_rows(h)], r.zb_big_r.at[kind, k - 1, sub_rows(h)],
+                r.zbb_s.at[kind, k, h], r.zbb_r.at[kind, k, h], k,
             )
 
         def aq_copy(a):
             return over_sib(r.a_qo.at[a], r.a_qo_r.at[a], r.aq_s.at[a], r.aq_r.at[a])
 
-        def zaq_copy(a):
-            return to_mate(r.za_qo.at[a], r.za_qo_r.at[a], r.zaq_s.at[a], r.zaq_r.at[a])
-
-        def zbq_copy(a, k):
-            return over_dp(
-                r.zb_qo.at[a, k - 1], r.zb_qo_r.at[a, k - 1], r.zbq_s.at[a, k], r.zbq_r.at[a, k], k
+        def around(src, dst, ssem, rsem, o):
+            return rcopy(src, dst, ssem, rsem, to_dp(lax.rem(dpi + o + 1, DP)))
+
+        def cq_copy(a, o):
+            return around(
+                r.c_qo.at[a, o], r.c_qo_r.at[a, o], r.cq_s.at[a, o], r.cq_r.at[a, o], o
             )
 
         def bq_copy(a, o):
@@ -430,11 +435,8 @@
         def kb_copy(o):
             return over_x(r.kv_b, r.kv_br.at[o], r.kb_s.at[o], r.kb_r.at[o], o)
 
-        def zak_copy():
-            return to_mate(r.za_kv, r.za_kv_r, r.zak_s.at[0], r.zak_r.at[0])
-
-        def zbk_copy(k):
-            return over_dp(r.zb_kv.at[k - 1], r.zb_kv_r.at[k - 1], r.zbk_s.at[k], r.zbk_r.at[k], k)
+        def ck_copy(o):
+            return around(r.c_kv.at[o], r.c_kv_r.at[o], r.ck_s.at[o], r.ck_r.at[o], o)
 
         def kf_copy():
             return over_sib(r.kv_fin, r.kv_sib, r.kf_s.at[0], r.kf_r.at[0])
@@ -451,14 +453,15 @@
         def sb_copy(o):
             return over_x(r.sm_b, r.sm_br.at[o], r.sb_s.at[o], r.sb_r.at[o], o)
 
+        def lanes(d):
+            return pl.ds(pl.multiple_of(d * DB // 128 * 128, 128), 128)
+
         def zs_copy(o):
-            return rcopy(
-                r.za_sm, r.za_sm_r.at[o], r.zs_s.at[o], r.zs_r.at[o],
-                to_dp(lax.rem(dpi + o + 1, DP)),
-            )
+            src = r.za_sm.at[:, lanes(lax.rem(dpi + o + 1, DP))]
+            return around(src, r.za_sm_r.at[o], r.zs_s.at[o], r.zs_r.at[o], o)
 
         def sec_copy(kind):
-            src, dst = ((r.qo_fin, r.qo_sec), (r.sm_fin, r.sm_sec))[kind]
+            src, dst = ((r.qo_fin, r.qo_sec), (r.sm_own, r.sm_sec))[kind]
             return rcopy(src, dst, r.sec_s.at[kind], r.sec_r.at[kind], to_section(me))
 
         def peers():
@@ -556,6 +559,15 @@
         gather_send(q_of(0, 0))
         gather_send(kv_of(0))
         gather_send(q_of(0, 1))
+        def later_norms(i, _):
+            first_norm(i)
+            gather_send(kv_of(i))
+            return 0
+
+        @pl.when(dec)
+        def _():
+            lax.fori_loop(1, NI, later_norms, 0)
+
         for name in PLACED:
             load(name).wait()
         for kind in (0, 1):
@@ -566,12 +578,10 @@
                     for x in xpeers():
                         wx_copy(kind, me, q, x, xi).start()
 
-        def later_norms(i, _):
-            first_norm(i)
-            gather_send(kv_of(i))
-            return 0
-
-        lax.fori_loop(1, NI, later_norms, 0)
+        @pl.when(enc)
+        def _():
+            lax.fori_loop(1, NI, later_norms, 0)
+
         for name in late + ["pairs", "routes_s"]:
             load(name).wait()
         own_query_weights(1, r.cq, r.co, r.cr)
@@ -664,9 +674,11 @@
                 s = nn(kv, q) + r.bias[...]
                 m = jnp.max(s, 0, keepdims=True)
                 ex = jnp.exp(s - m)
-                p = (ex * (1.0 / jnp.sum(ex, 0, keepdims=True))).astype(BF16)
+                inv = 1.0 / jnp.sum(ex, 0, keepdims=True)
+                p = ex.astype(BF16)
                 r.p[a, i, k] = p
-                r.heads[a, i, k] = nn(r.kvt[a, i, HD:], p)
+                r.inv[a, i, k] = jnp.broadcast_to(inv, (8, L))
+                r.heads[a, i, k] = nn(r.kvt[a, i, HD:], p) * inv
                 return 0
 
             lax.fori_loop(0, T, one, 0, unroll=True)
@@ -702,13 +714,11 @@
             r.dkv_acc[...] = jnp.zeros_like(r.dkv_acc)
 
             def one(k, _):
-                dheads = r.dq[k]
+                dheads = (r.dq[k].astype(F32) * r.inv[a, i, k, 0:1]).astype(BF16)
                 p = r.p[a, i, k]
                 dv = jnp.concatenate([zeros_h, dheads], 0)
-                dp = nn(kv, dv)
-                pf = p.astype(F32)
-                delta = jnp.sum(dp * pf, 0, keepdims=True)
-                ds = (pf * (dp - delta)).astype(BF16)
+                delta = jnp.sum(dheads.astype(F32) * r.heads[a, i, k], 0, keepdims=True)
+                ds = (p.astype(F32) * (nn(kv, dv) - delta)).astype(BF16)
                 qk = jnp.concatenate([r.qt[a, i, k], zeros_h], 0)
                 r.dkv_acc[...] += nt(ds, qk) + nt(p, dv)
                 r.dq[k] = (nn(r.kvt[a, i, :HD], ds) * scale).astype(BF16)
@@ -781,34 +791,40 @@
 
         def big_send(kind, low, high):
             for s in range(low, high):
-                for o in range(X - 1):
-                    b_copy(kind, o, dp_at(s)).start()
+                for h in range(NH):
+                    for o in range(X - 1):
+                        b_copy(kind, o, dp_at(s), h).start()
 
         def big_over_x(kind, s):
+            for h in range(NH):
+                big_part_over_x(kind, s, h)
+
+        def big_part_over_x(kind, s, h):
             d = dp_at(s)
-            total = r.g_big[me, kind, block_rows(d)]
+            total = r.g_big[me, kind, part_rows(d, h)]
             for o in range(X - 1):
-                b_copy(kind, o, d).wait_recv()
-                total = total + r.b_big_r[o, kind, block_rows(d)].astype(F32)
+                b_copy(kind, o, d, h).wait_recv()
+                total = total + r.b_big_r[o, kind, part_rows(d, h)].astype(F32)
             if s < HP:
-                r.za_big[kind, s] = total.astype(BF16)
-                zab_copy(kind, s).start()
+                r.za_big[kind, s, sub_rows(h)] = total.astype(BF16)
+                zab_copy(kind, s, h).start()
                 return
             k = (s - HP + 1) % HP
-            zab_copy(kind, k).wait_recv()
-            total = total + r.za_big_r[kind, k].astype(F32)
+            zab_copy(kind, k, h).wait_recv()
+            total = total + r.za_big_r[kind, k, sub_rows(h)].astype(F32)
             if k > 0:
-                r.zb_big[kind, k - 1] = total.astype(BF16)
-                zbb_copy(kind, k).start()
+                r.zb_big[kind, k - 1, sub_rows(h)] = total.astype(BF16)
+                zbb_copy(kind, k, h).start()
             else:
-                r.g_big[me, kind, block_rows(d)] = total
+                r.g_big[me, kind, part_rows(d, h)] = total
 
         def big_end(kind, out):
-            total = r.g_big[me, kind, block_rows(dpi)]
-            for k in range(1, HP):
-                zbb_copy(kind, k).wait_recv()
-                total = total + r.zb_big_r[kind, k - 1].astype(F32)
-            out[...] = total
+            for h in range(NH):
+                total = r.g_big[me, kind, part_rows(dpi, h)]
+                for k in range(1, HP):
+                    zbb_copy(kind, k, h).wait_recv()
+                    total = total + r.zb_big_r[kind, k - 1, sub_rows(h)].astype(F32)
+                out[sub_rows(h)] = total
 
         def hand_out(i, s, c, kind):
             @pl.when(jnp.logical_and(i == NI - 1, lax.rem(s, 2) == 0))
@@ -885,40 +901,31 @@
                 r.a_qo[a, x] = qo_rows(a, x * 2 + (1 - core)).astype(BF16)
             aq_copy(a).start()
 
+        def rows_around(o):
+            return block_rows(lax.rem(dpi + o + 1, DP))
+
         def qo_sib(a):
             aq_copy(a).wait_recv()
-            for x in range(X):
-                total = qo_rows(a, chip(x)) + r.a_qo_r[a, x].astype(F32)
-                r.own_qo[a, x] = total.T
-            for k in range(HP):
-                r.za_qo[a, k] = r.own_qo[a, :, block_rows(mates_at(k))].astype(BF16)
-            zaq_copy(a).start()
-
-        def qo_mate(a):
-            zaq_copy(a).wait_recv()
-            for k in range(HP):
-                total = r.own_qo[a, :, block_rows(mine_at(k))] + r.za_qo_r[a, k].astype(F32)
-                if k > 0:
-                    r.zb_qo[a, k - 1] = total.astype(BF16)
-                    zbq_copy(a, k).start()
-                else:
-                    r.own_qo[a, :, block_rows(dpi)] = total
-
-        def qo_over_dp(a):
-            total = r.own_qo[a, :, block_rows(dpi)]
-            for k in range(1, HP):
-                zbq_copy(a, k).wait_recv()
-                total = total + r.zb_qo_r[a, k - 1].astype(F32)
-            r.own_qo[a, :, block_rows(dpi)] = total
             for o, x in enumerate(xpeers()):
-                r.b_qo[a, o] = r.own_qo[a, x, block_rows(dpi)].astype(BF16)
+                r.b_qo[a, o] = (qo_rows(a, chip(x)) + r.a_qo_r[a, x].astype(F32)).astype(BF16)
                 bq_copy(a, o).start()
 
-        def qo_end(a):
-            total = r.own_qo[a, xi, block_rows(dpi)]
+        def qo_over_x(a):
+            total = qo_rows(a, me) + r.a_qo_r[a, xi].astype(F32)
             for o in range(X - 1):
                 bq_copy(a, o).wait_recv()
                 total = total + r.b_qo_r[a, o].astype(F32)
+            r.own_qo[...] = total.T
+            for o in range(DP - 1):
+                r.c_qo[a, o] = r.own_qo[rows_around(o)].astype(BF16)
+                cq_copy(a, o).start()
+            r.qo_own[a] = r.own_qo[block_rows(dpi)]
+
+        def qo_end(a):
+            total = r.qo_own[a]
+            for o in range(DP - 1):
+                cq_copy(a, o).wait_recv()
+                total = total + r.c_qo_r[a, o].astype(F32)
             return total
 
         kv_busy = enc | (core == 0)
@@ -934,29 +941,17 @@
             def _():
                 ka_copy().wait_recv()
                 r.kv_sum[...] = r.g_kv[core] + r.kv_ar[...]
-                for k in range(HP):
-                    r.za_kv[k] = r.kv_sum[block_rows(mates_at(k))].astype(BF16)
-                zak_copy().start()
-
-        def kv_mate():
-            @pl.when(kv_busy)
-            def _():
-                zak_copy().wait_recv()
-                for k in range(HP):
-                    total = r.kv_sum[block_rows(mine_at(k))] + r.za_kv_r[k].astype(F32)
-                    if k > 0:
-                        r.zb_kv[k - 1] = total.astype(BF16)
-                        zbk_copy(k).start()
-                    else:
-                        r.kv_fin[...] = total
+                for o in range(DP - 1):
+                    r.c_kv[o] = r.kv_sum[rows_around(o)].astype(BF16)
+                    ck_copy(o).start()
 
         def kv_over_dp():
             @pl.when(kv_busy)
             def _():
-                total = r.kv_fin[...]
-                for k in range(1, HP):
-                    zbk_copy(k).wait_recv()
-                    total = total + r.zb_kv_r[k - 1].astype(F32)
+                total = r.kv_sum[block_rows(dpi)]
+                for o in range(DP - 1):
+                    ck_copy(o).wait_recv()
+                    total = total + r.c_kv_r[o].astype(F32)
                 r.kv_fin[...] = total
                 r.kv_b[...] = total.astype(BF16)
                 for o in range(X - 1):
@@ -1011,11 +1006,11 @@
                 zs_copy(o).start()
 
         def small_over_dp():
-            total = r.sm_fin[...]
+            total = r.sm_fin[:, lanes(dpi)]
             for o in range(DP - 1):
                 zs_copy(o).wait_recv()
                 total = total + r.za_sm_r[o].astype(F32)
-            r.sm_fin[...] = total
+            r.sm_own[...] = total
 
         def self_forward(i):
             x1 = attend(i, 0, r.kv_s, r.x[i].astype(F32))
@@ -1048,6 +1043,18 @@
         gather_take(kv_of(0))
         gather_take(q_of(0, 1))
         self_forward(0)
+        def later_rows(i, _):
+            project_queries(i, 0)
+            set_bias(i, 0)
+            gather_relay(kv_of(i))
+            gather_take(kv_of(i))
+            self_forward(i)
+            return 0
+
+        @pl.when(dec)
+        def _():
+            lax.fori_loop(1, NI, later_rows, 0)
+
         for q in range(NS):
             weights_over_x(0, q)
         for kind in (0, 1):
@@ -1079,25 +1086,16 @@
             ffn_forward(0, 3, E)
             encoded(0)
 
-        def later_rows(i, _):
-            project_queries(i, 0)
-            set_bias(i, 0)
-            gather_relay(kv_of(i))
-            gather_take(kv_of(i))
-            self_forward(i)
-
-            @pl.when(enc)
-            def _():
+        @pl.when(enc)
+        def _():
+            def later_outputs(i, _):
+                later_rows(i, 0)
                 r.acc[...] = r.x1[i]
                 ffn_forward(i, 0, E)
                 encoded(i)
-
-            return 0
-
-        lax.fori_loop(1, NI, later_rows, 0)
-
-        @pl.when(enc)
-        def _():
+                return 0
+
+            lax.fori_loop(1, NI, later_outputs, 0)
             store("layer").start()
 
         r.small[...] = jnp.zeros_like(r.small)
@@ -1193,20 +1191,11 @@
             @pl.when(dec & first)
             def _():
                 ffn_weights(0)
-                big_send(1, HP, DP)
+
+            @pl.when(last)
+            def _():
                 big_sib(0)
-
-            @pl.when(enc & last)
-            def _():
-                big_send(1, HP, DP)
-                big_sib(0)
-
-            @pl.when(dec & last)
-            def _():
                 big_send(0, 0, HP)
-
-            @pl.when(last)
-            def _():
                 qo_send(0)
 
             return 0
@@ -1219,9 +1208,7 @@
 
         @pl.when(dec)
         def _():
-            qo_mate(1)
-            for s in range(HP, DP - 1):
-                big_over_x(1, s)
+            qo_over_x(1)
 
         def first_layer(i, _):
             dkv = dkv_in(i).astype(BF16)
@@ -1245,16 +1232,14 @@
         small_sib()
         kv_sib()
 
-        @pl.when(enc)
-        def _():
-            big_send(0, 0, DP)
-            for s in range(HP, DP - 1):
-                big_over_x(1, s)
+        for s in range(HP, DP):
+            for kind in (1, 0):
+                big_send(kind, s, s + 1)
+        for s in range(HP):
+            big_over_x(0, s)
 
         @pl.when(dec)
         def _():
-            big_send(0, HP, DP)
-
             def output(i, _):
                 ffn_output(i)
                 return 0
@@ -1263,18 +1248,12 @@
             store("layer").start()
 
         small_over_x()
-        big_over_x(1, DP - 1)
-        for s in range(HP):
-            big_over_x(0, s)
-        kv_mate()
-        qo_mate(0)
-
-        @pl.when(dec)
-        def _():
-            qo_over_dp(1)
-
+
+        qo_over_x(0)
         for s in range(HP, DP - 1):
-            big_over_x(0, s)
+            for kind in (1, 0):
+                big_over_x(kind, s)
+        kv_over_dp()
         small_over_dp()
 
         @pl.when(dec)
@@ -1283,11 +1262,10 @@
             r.qo_fin[...] = qo_end(1)
             sec_copy(0).start()
             r.o_qo[1] = r.qo_fin[...]
-            r.o_small[...] = r.sm_fin[...]
-
-        kv_over_dp()
-        qo_over_dp(0)
-        big_over_x(0, DP - 1)
+            r.o_small[...] = r.sm_own[...]
+
+        for kind in (1, 0):
+            big_over_x(kind, DP - 1)
         kv_over_x()
         r.o_qo[0] = qo_end(0)
         big_end(1, r.o_back)
@@ -1299,9 +1277,9 @@
             sec_copy(1).wait_recv()
             sec_copy(0).wait_recv()
             r.o_qo[1] = r.qo_sec[...]
-            rows = lax.broadcasted_iota(jnp.int32, (SR, D), 0)
+            rows = lax.broadcasted_iota(jnp.int32, (SR, 128), 0)
             theirs = ((rows >= 2) & (rows < 4)) | ((rows >= 6 + NE) & (rows < 6 + 2 * NE))
-            r.o_small[...] = jnp.where(theirs, r.sm_sec[...], r.sm_fin[...])
+            r.o_small[...] = jnp.where(theirs, r.sm_sec[...], r.sm_own[...])
 
         store("layer").wait()
         store("ig").wait()
@@ -1309,13 +1287,14 @@
             gather_sent(q_of(0, kind))
             for x in range(X):
                 a_copy(kind, x).wait_send()
-            for o in range(X - 1):
-                for d in range(DP):
-                    b_copy(kind, o, d).wait_send()
-            for k in range(HP):
-                zab_copy(kind, k).wait_send()
-            for k in range(1, HP):
-                zbb_copy(kind, k).wait_send()
+            for h in range(NH):
+                for o in range(X - 1):
+                    for d in range(DP):
+                        b_copy(kind, o, d, h).wait_send()
+                for k in range(HP):
+                    zab_copy(kind, k, h).wait_send()
+                for k in range(1, HP):
+                    zbb_copy(kind, k, h).wait_send()
         weights_sent()
         sa_copy().wait_send()
         for o in range(X - 1):
@@ -1327,9 +1306,8 @@
             aq_copy(a).wait_send()
             for o in range(X - 1):
                 bq_copy(a, o).wait_send()
-            zaq_copy(a).wait_send()
-            for k in range(1, HP):
-                zbq_copy(a, k).wait_send()
+            for o in range(DP - 1):
+                cq_copy(a, o).wait_send()
 
         qo_sent(0)
 
@@ -1348,9 +1326,8 @@
         def _():
             for o in range(X - 1):
                 kb_copy(o).wait_send()
-            zak_copy().wait_send()
-            for k in range(1, HP):
-                zbk_copy(k).wait_send()
+            for o in range(DP - 1):
+                ck_copy(o).wait_send()
             kf_copy().wait_send()
 
         @pl.when(enc & (core == 1))
@@ -1404,8 +1381,7 @@
                 total = jnp.where(me == j, kv[a, j * EB : (j + 1) * EB], total)
             out[...] = total
         off = (lax.axis_index("dp") * E + me) * EB
-        part = small[:, pl.ds(pl.multiple_of(off // 128 * 128, 128), 128)]
-        part = pltpu.roll(part, lax.rem(128 - lax.rem(off, 128), 128), 1)[:, :EB]
+        part = pltpu.roll(small[...], lax.rem(128 - lax.rem(off, 128), 128), 1)[:, :EB]
         o_gain[0] = jnp.concatenate([part[0:1], part[4:5]], 0)
         o_bias[0] = jnp.concatenate([part[1:2], part[5:6]], 0)
         o_cgain[...] = part[2:3]

time: 109 us -> 103 us (0.945)
  Pallas kernels: 108 us -> 102 us
    pallas_call x1, Pallas kernels: 105 us -> 98.6 us  [body(): pl.pallas_call(make_kernel(dims), out_shape=[jax.ShapeDtypeStruct(s, t) f...]
where the time goes in v4:
time: 103 us
  Pallas kernels  102 us (99%)
    pallas_call x1, Pallas kernels, body(): pl.pallas_call(make_kernel(dims), out_shape=[jax.ShapeDtypeStruct(s, t) f...  98.6 us
    pallas_call x1, Pallas kernels, body(): pl.pallas_call(make_finish(E, NE, EB, QB), out_shape=[jax.ShapeDtypeStruc...  3.12 us

profile of v4, /device:TPU:0, one launch (start us, length us, event | category | flops | bytes accessed | tf_op | source)
XLA Modules:
  0.0 102.6 jit_solution(994083157202407909)
XLA Ops:
  0.7 98.6 %layers.1 = (bf16[2,256,512]{2,1,0:T(8,128)(2,1)}, f32[2,256,512]{2,1,0:T(8,128)}, f32[128,512]{1,0:T(8,128)}, f32[128,512]{1,0:T(8,128)}, f32[2,128,128]{2,1,0:...) custom-call(bf16[2,256,512]{2,1,0:T(8,128)(2,1)} %bitcast.49, bf16[2,256,512]{2,1,0:T(8,128)(2,1)} %bitcast.50, ...), custom_call_target="tpu_custom_call" | custom-call | tf_op jit(solution)/shard_map/layers/pallas_call | solution.py:1437
  99.3 3.1 %results.1 = (bf16[2,256,512]{2,1,0:T(8,128)(2,1)}, f32[2,256,512]{2,1,0:T(8,128)}, f32[1,2,32]{2,1,0:T(2,128)}, f32[1,2,32]{2,1,0:T(2,128)}, f32[32,128]{1,0:T(...) custom-call(bf16[2,256,512]{2,1,0:T(8,128)(2,1)} %get-tuple-element., ...), custom_call_target="tpu_custom_call" | custom-call | tf_op jit(solution)/shard_map/results/pallas_call | solution.py:1473

commit v5 on v4

--- a/solution.py
+++ b/solution.py
@@ -836,8 +836,6 @@
         def ffn_back(i):
             dz = r.dz[i]
             dzt = dz.astype(F32).T.astype(BF16)
-            nt_ = r.n[i, 2].astype(F32).T.astype(BF16)
-            r.acc[...] = jnp.zeros_like(r.acc)
 
             def back(s, _):
                 c = chunk_out(s)
@@ -851,6 +849,9 @@
             def _():
                 big_sib(1)
                 big_send(1, 0, HP)
+
+            nt_ = r.n[i, 2].astype(F32).T.astype(BF16)
+            r.acc[...] = jnp.zeros_like(r.acc)
 
             def inward(s, _):
                 c = chunk_out(s)
@@ -1194,6 +1195,7 @@
 
             @pl.when(last)
             def _():
+                big_send(1, HP, DP - 1)
                 big_sib(0)
                 big_send(0, 0, HP)
                 qo_send(0)
@@ -1232,9 +1234,9 @@
         small_sib()
         kv_sib()
 
-        for s in range(HP, DP):
-            for kind in (1, 0):
-                big_send(kind, s, s + 1)
+        big_send(0, HP, DP - 1)
+        for s in range(HP, DP - 1):
+            big_over_x(1, s)
         for s in range(HP):
             big_over_x(0, s)
 
@@ -1250,10 +1252,11 @@
         small_over_x()
 
         qo_over_x(0)
+        kv_over_dp()
+        for kind in (1, 0):
+            big_send(kind, DP - 1, DP)
         for s in range(HP, DP - 1):
-            for kind in (1, 0):
-                big_over_x(kind, s)
-        kv_over_dp()
+            big_over_x(0, s)
         small_over_dp()
 
         @pl.when(dec)

time: 103 us -> 101 us (0.981)
  Pallas kernels: 102 us -> 99.8 us
    pallas_call x1, Pallas kernels: 98.6 us -> 96.7 us  [body(): pl.pallas_call(make_kernel(dims), out_shape=[jax.ShapeDtypeStruct(s, t) f...]
where the time goes in v5:
time: 101 us
  Pallas kernels  99.8 us (99%)
    pallas_call x1, Pallas kernels, body(): pl.pallas_call(make_kernel(dims), out_shape=[jax.ShapeDtypeStruct(s, t) f...  96.7 us
    pallas_call x1, Pallas kernels, body(): pl.pallas_call(make_finish(E, NE, EB, QB), out_shape=[jax.ShapeDtypeStruc...  3.12 us

profile of v5, /device:TPU:0, one launch (start us, length us, event | category | flops | bytes accessed | tf_op | source)
XLA Modules:
  0.0 100.7 jit_solution(3232870129449029902)
XLA Ops:
  0.7 96.7 %layers.1 = (bf16[2,256,512]{2,1,0:T(8,128)(2,1)}, f32[2,256,512]{2,1,0:T(8,128)}, f32[128,512]{1,0:T(8,128)}, f32[128,512]{1,0:T(8,128)}, f32[2,128,128]{2,1,0:...) custom-call(bf16[2,256,512]{2,1,0:T(8,128)(2,1)} %bitcast.49, bf16[2,256,512]{2,1,0:T(8,128)(2,1)} %bitcast.50, ...), custom_call_target="tpu_custom_call" | custom-call | tf_op jit(solution)/shard_map/layers/pallas_call | solution.py:1440
  97.4 3.1 %results.1 = (bf16[2,256,512]{2,1,0:T(8,128)(2,1)}, f32[2,256,512]{2,1,0:T(8,128)}, f32[1,2,32]{2,1,0:T(2,128)}, f32[1,2,32]{2,1,0:T(2,128)}, f32[32,128]{1,0:T(...) custom-call(bf16[2,256,512]{2,1,0:T(8,128)(2,1)} %get-tuple-element., ...), custom_call_target="tpu_custom_call" | custom-call | tf_op jit(solution)/shard_map/results/pallas_call | solution.py:1476

commit v6 on v5

--- a/solution.py
+++ b/solution.py
@@ -1069,6 +1069,13 @@
         for q in range(NS):
             weights_over_x(1, q)
             weights_over_z(0, q)
+        @pl.when(dec)
+        def _():
+            for i in range(NI):
+                for s in range(2):
+                    c = chunk_at(jnp.int32(s))
+                    r.dh[i, c] = nt(r.cot[i], r.wback_all[c]).astype(BF16)
+
         for q in range(NS, NX):
             weights_over_x(0, q)
         for q in range(NS):
@@ -1121,11 +1128,12 @@
                 project_queries(i, 1)
                 dz = r.cot[i]
 
-                def one(c, _):
+                def one(s, _):
+                    c = chunk_at(s)
                     r.dh[i, c] = nt(dz, r.wback_all[c]).astype(BF16)
                     return 0
 
-                lax.fori_loop(0, E, one, 0)
+                lax.fori_loop(2, E, one, 0)
                 return 0
 
             lax.fori_loop(0, NI, ahead, 0)

time: 101 us -> 99.6 us (0.986)
  Pallas kernels: 99.8 us -> 98.5 us
    pallas_call x1, Pallas kernels: 96.7 us -> 95.4 us  [body(): pl.pallas_call(make_kernel(dims), out_shape=[jax.ShapeDtypeStruct(s, t) f...]
where the time goes in v6:
time: 99.6 us; the launch traced here: 99.3 us
  Pallas kernels  98.5 us (99%)
    pallas_call x1, Pallas kernels, body(): pl.pallas_call(make_kernel(dims), out_shape=[jax.ShapeDtypeStruct(s, t) f...  95.4 us
    pallas_call x1, Pallas kernels, body(): pl.pallas_call(make_finish(E, NE, EB, QB), out_shape=[jax.ShapeDtypeStruc...  3.12 us

profile of v6, /device:TPU:0, one launch (start us, length us, event | category | flops | bytes accessed | tf_op | source)
XLA Modules:
  0.0 99.3 jit_solution(917778695328453198)
XLA Ops:
  0.7 95.4 %layers.1 = (bf16[2,256,512]{2,1,0:T(8,128)(2,1)}, f32[2,256,512]{2,1,0:T(8,128)}, f32[128,512]{1,0:T(8,128)}, f32[128,512]{1,0:T(8,128)}, f32[2,128,128]{2,1,0:...) custom-call(bf16[2,256,512]{2,1,0:T(8,128)(2,1)} %bitcast.49, bf16[2,256,512]{2,1,0:T(8,128)(2,1)} %bitcast.50, ...), custom_call_target="tpu_custom_call" | custom-call | tf_op jit(solution)/shard_map/layers/pallas_call | solution.py:1448
  96.0 3.1 %results.1 = (bf16[2,256,512]{2,1,0:T(8,128)(2,1)}, f32[2,256,512]{2,1,0:T(8,128)}, f32[1,2,32]{2,1,0:T(2,128)}, f32[1,2,32]{2,1,0:T(2,128)}, f32[32,128]{1,0:T(...) custom-call(bf16[2,256,512]{2,1,0:T(8,128)(2,1)} %get-tuple-element., ...), custom_call_target="tpu_custom_call" | custom-call | tf_op jit(solution)/shard_map/results/pallas_call | solution.py:1484
